TPU v7x, 32 devices: a whole 2x2x4 slice. The times are simulated.
32 devices in a mesh: lat: 4 (over y, x), lon: 8 (over z, core).
Axes of the slice: x: 2, y: 2, z: 4, core: 2. Of those that a mesh axis runs over, the one named last changes fastest.
Arguments:
- field: bfloat16 [96, 192, 384], P('lat', 'lon'), may hold values from -6 to 6
- cotangent: bfloat16 [96, 192, 384], P('lat', 'lon'), may hold values from -6 to 6
- mix_weight: bfloat16 [3, 384, 384], replicated, may hold values from -0.1875 to 0.1875
- taps: float32 [96, 3, 3, 8], replicated, may hold values from -1.8 to 1.8
- offsets: int32 [96, 3, 8], replicated, may hold values from -8 to 8, as said below
- counts: int32 [96], replicated, may hold values from 1 to 8, as said below
Outputs:
- grad_field: bfloat16 [96, 192, 384], P('lat', 'lon')
- grad_spectra: float32 [2, 384, 384, 384], P(None, 'lat', 'lon')
- grad_mix: float32 [3, 384, 384], replicated
Inputs may be any that keep to these rules, and one draw needn't show every extreme that they name: For every row and latitude offset the 8 longitude offsets are distinct. Tap slots of a row at or beyond counts are inactive; the polar rows use all 8.
All inputs are finite; a program needn't handle non-finite values.
Results may differ from a plain program's by a relative error of at most 0.0061.
Values may be sent and summed in bfloat16 or wider, within the bound.
A program may use at most 128 MiB of HBM per device.

v0:
```python
import math

import jax
import jax.numpy as jnp
from jax import lax
from jax.sharding import PartitionSpec as P

M = 384
L = 384
K = 3
R = 8
S = 8
LB = 32
SUBS = 1


def extended(shard, sides, width, wrap):
    for axis, dim in sides:
        devices, length = (lax.axis_size(axis), shard.shape[dim])
        up = [(i, (i + 1) % devices) for i in range(devices if wrap else devices - 1)]
        down = [(j, i) for i, j in up]
        last = lax.slice_in_dim(shard, length - width, length, axis=dim)
        leading = lax.slice_in_dim(shard, 0, width, axis=dim)
        before = lax.ppermute(last, axis, up)
        after = lax.ppermute(leading, axis, down)
        shard = jnp.concatenate([before, shard, after], axis=dim)
    return shard


def live_taps(taps, counts):
    slot_ids = lax.broadcasted_iota(jnp.int32, taps.shape, 3)
    keep_mask = slot_ids < counts[:, None, None, None]
    return jnp.where(keep_mask, taps, jnp.float32(0.0)).astype(jnp.bfloat16)


def band_matrix(weights, shifts, orient, lon_width):
    row_total = weights.shape[0]
    ext_width = lon_width + 2 * R
    out_col = lax.broadcasted_iota(jnp.int32, (lon_width, ext_width), 0)
    in_col = lax.broadcasted_iota(jnp.int32, (lon_width, ext_width), 1)
    summed = jnp.zeros((row_total, 3, weights.shape[1], lon_width, ext_width), jnp.float32)
    for tap_slot in range(S):
        target = out_col[None, None] + R + orient * shifts[:, :, tap_slot, None, None]
        tap_hit = (in_col[None, None] == target).astype(jnp.float32)
        tap_value = jnp.transpose(weights[:, :, :, tap_slot], (0, 2, 1)).astype(jnp.float32)
        summed = summed + tap_value[:, :, :, None, None] * tap_hit[:, :, None]
    return summed.astype(jnp.bfloat16)


def dft_table(lon_total, orders):
    columns = lax.broadcasted_iota(jnp.int32, (lon_total,), 0)
    phases = orders[:, None] * columns[None, :] % lon_total
    angles = 2.0 * math.pi / lon_total * phases.astype(jnp.float32)
    return jnp.stack([jnp.cos(angles), -jnp.sin(angles)]).astype(jnp.bfloat16)


def colatitudes(lat_total):
    angles = (lax.broadcasted_iota(jnp.int32, (lat_total,), 0).astype(jnp.float32) + 0.5) * (
        math.pi / lat_total
    )
    return (jnp.cos(angles), jnp.log(jnp.sin(angles)))


def seed_logs(order_total):
    degrees = lax.broadcasted_iota(jnp.int32, (order_total,), 0).astype(jnp.float32)
    step_logs = jnp.log((2.0 * degrees + 1.0) / (2.0 * degrees + 2.0))
    prefix = jnp.concatenate([jnp.zeros((1,), jnp.float32), jnp.cumsum(step_logs)[:-1]])
    return 0.5 * jnp.log((2.0 * degrees + 1.0) / (4.0 * math.pi)) + 0.5 * prefix


def advance(degree, previous, earlier, orders, cosines):
    deg_f = jnp.asarray(degree).astype(jnp.float32)
    ord_f = orders.astype(jnp.float32)[:, None]
    higher = (degree > orders)[:, None]
    lower_a = jnp.where(higher, deg_f * deg_f - ord_f * ord_f, 1.0)
    factor_a = jnp.sqrt((4.0 * deg_f * deg_f - 1.0) / lower_a)
    upper_b = jnp.maximum((deg_f - 1.0) * (deg_f - 1.0) - ord_f * ord_f, 0.0)
    lower_b = jnp.maximum(4.0 * (deg_f - 1.0) * (deg_f - 1.0) - 1.0, 1.0)
    factor_b = jnp.sqrt(upper_b / lower_b)
    grown = factor_a * (cosines[None, :] * previous - factor_b * earlier)
    seeded = jnp.where((degree == orders)[:, None], jnp.float32(1.0), jnp.float32(0.0))
    return jnp.where(higher, grown, seeded)


def rescale(previous, earlier, scales):
    biggest = jnp.maximum(jnp.abs(previous), jnp.abs(earlier))
    divisor = jnp.where(biggest > 0.0, biggest, jnp.float32(1.0))
    return (previous / divisor, earlier / divisor, scales + jnp.log(divisor))


def legendre_range(
    start_block, orders, cosines, logscale, spec_part, result, row_offset, leg_scale
):
    state_zero = jnp.zeros(logscale.shape, jnp.float32)

    def block_step(block_idx, loop_state):
        previous, earlier, scales, summed = loop_state
        factor = jnp.exp(scales)
        levels = []
        for inner_step in range(LB):
            degree = block_idx * LB + inner_step
            fresh = advance(degree, previous, earlier, orders, cosines)
            levels.append(fresh * factor)
            earlier, previous = (previous, fresh)
        contrib = (
            jnp.einsum(
                "lmt,pmct->pmcl", jnp.stack(levels), spec_part, precision=lax.Precision.HIGHEST
            )
            * leg_scale
        )
        level_start = (block_idx * LB).astype(jnp.int32)
        zero_index = jnp.zeros((), jnp.int32)
        summed = lax.dynamic_update_slice(
            summed,
            contrib,
            (zero_index, jnp.asarray(row_offset).astype(jnp.int32), zero_index, level_start),
        )
        previous, earlier, scales = rescale(previous, earlier, scales)
        return (previous, earlier, scales, summed)

    return lax.fori_loop(
        start_block, L // LB, block_step, (state_zero, state_zero, logscale, result)
    )[3]


def on_device(field, cotangent, mix_weight, taps, offsets, counts):
    lat_dev, lon_dev, channels = field.shape
    lat_count = lax.axis_size("lat")
    lon_count = lax.axis_size("lon")
    total_lat = lat_dev * lat_count
    total_lon = lon_dev * lon_count
    lat_pos = lax.axis_index("lat")
    first_row = lat_pos * lat_dev
    live_table = live_taps(taps, counts)
    taps_padded = jnp.pad(live_table, ((1, 1), (0, 0), (0, 0), (0, 0)))
    shifts_padded = jnp.pad(offsets, ((1, 1), (0, 0), (0, 0)))
    taps_ext = lax.dynamic_slice_in_dim(taps_padded, first_row, lat_dev + 2, 0)
    shifts_ext = lax.dynamic_slice_in_dim(shifts_padded, first_row, lat_dev + 2, 0)
    band_own = band_matrix(taps_ext[1:-1], shifts_ext[1:-1], 1, lon_dev)
    band_back = band_matrix(taps_ext, shifts_ext, -1, lon_dev)
    basis_own = jnp.einsum(
        "tfd,kcd->tfkc", cotangent, mix_weight, preferred_element_type=jnp.float32
    ).astype(jnp.bfloat16)
    stacked = jnp.concatenate([field, basis_own.reshape(lat_dev, lon_dev, K * channels)], axis=2)
    wide_rims = extended(stacked, (("lon", 1),), R, True)
    full_ext = extended(wide_rims, (("lat", 0),), 1, False)
    field_ext = full_ext[:, :, :channels]
    basis_ext = full_ext[:, :, channels:].reshape(lat_dev + 2, lon_dev + 2 * R, K, channels)
    response = jnp.zeros((lat_dev, lon_dev, K, channels), jnp.float32)
    for lat_step in range(3):
        response = response + jnp.einsum(
            "tkfx,txc->tfkc",
            band_own[:, lat_step],
            field_ext[lat_step : lat_step + lat_dev],
            preferred_element_type=jnp.float32,
        )
    response = response.astype(jnp.bfloat16)
    mix_local = jnp.einsum(
        "tfkc,tfd->kcd", response, cotangent, preferred_element_type=jnp.float32
    ) * (1.0 / math.sqrt(total_lat * total_lon))
    grad_mix = lax.psum(mix_local, ("lat", "lon"))
    adjoint = cotangent.astype(jnp.float32)
    for lat_step in range(3):
        row_base = 2 - lat_step
        adjoint = adjoint + jnp.einsum(
            "tkfx,txkc->tfc",
            band_back[row_base : row_base + lat_dev, lat_step],
            basis_ext[row_base : row_base + lat_dev],
            preferred_element_type=jnp.float32,
        )
    grad_field = adjoint.astype(jnp.bfloat16)
    column_set = lax.all_to_all(grad_field, "lon", split_axis=2, concat_axis=1, tiled=True)
    all_orders = lax.broadcasted_iota(jnp.int32, (M,), 0)
    block_rows = M // lat_count
    dft_rows = dft_table(total_lon, all_orders)
    spectra = (
        jnp.einsum("tfc,pmf->pmct", column_set, dft_rows, preferred_element_type=jnp.float32)
        * (1.0 / math.sqrt(total_lon))
    ).astype(jnp.bfloat16)
    mode_block = lax.all_to_all(spectra, "lat", split_axis=1, concat_axis=3, tiled=True)
    spec_full = mode_block.astype(jnp.float32)
    cosines, log_sines = colatitudes(total_lat)
    order_logs = seed_logs(M)
    group_rows = block_rows // SUBS
    chan_block = spec_full.shape[2]
    result = jnp.zeros((2, block_rows, chan_block, L), jnp.float32)
    leg_scale = math.sqrt(4.0 * math.pi / total_lat)
    local_rows = 0 + lax.broadcasted_iota(jnp.int32, (group_rows,), 0)
    orders = lat_pos * block_rows + local_rows
    order_hit = all_orders[None, :] == orders[:, None]
    seed_part = jnp.sum(jnp.where(order_hit, order_logs[None, :], jnp.float32(0.0)), axis=1)
    logscale = seed_part[:, None] + orders.astype(jnp.float32)[:, None] * log_sines[None, :]
    start_block = jnp.min(orders) // LB
    result = legendre_range(start_block, orders, cosines, logscale, spec_full, result, 0, leg_scale)
    return (grad_field, result, grad_mix)


def solution(mesh):
    placed = (P("lat", "lon", None), P("lat", "lon", None), P(), P(), P(), P())
    return jax.shard_map(
        on_device,
        mesh=mesh,
        in_specs=placed,
        out_specs=(P("lat", "lon", None), P(None, "lat", "lon", None), P()),
        check_vma=False,
    )
```

profile of v0, /device:TPU:0, one launch (start us, length us, event | category | flops | bytes accessed | tf_op | source)
XLA Modules:
  0.0 550.0 jit_solution(17398720262903318899)
XLA Ops:
  12.3 4.0 collective-permute-start.1
  44.2 3.3 fusion.150
  48.4 3.1 add_convert_fusion
  52.9 4.6 collective-permute-start.3
  63.5 3.6 copy.353
  67.1 5.2 reshape.1990
  72.3 4.4 all-to-all-start
  76.9 7.1 %add_convert_fusion.2 = bf16[24,3,3,24,40]{4,3,2,0,1:T(8,128)(2,1)} fusion(f32[24,3,24,40]{3,2,0,1:T(8,128)} %get-tuple-element.852, f32[24,3,3]{2,0,1:T(8,128)S(1)} %copy-done.8, f32[24,3,24,40]{3,2,0,1:T(8,128)} %get-tuple-element.851, f32[24,3,3]{2,0,1:T(8,128)} %copy.366, f32[24,3,24,40]{3,2,0,1:T(8,128)} %get-tuple-element.850, ...), kind=kLoop, calls=%fused_computation.274 | loop fusion | flops 3317760 | bytes 2633472 | tf_op jit(solution)/shard_map/convert_element_type | solution.py:47
  83.9 6.4 %all-to-all-done = bf16[8,2,13824]{2,1,0:T(2,128)(2,1)} async-done(((bf16[8,2,13824]{2,1,0:T(2,128)(2,1)}), bf16[8,2,13824]{2,1,0:T(2,128)(2,1)}, u32[]{:S(2)}, u32[]{:S(2)}) %all-to-all-start) | async-done | bytes 442400 | tf_op jit(solution)/shard_map/all_to_all | solution.py:172
  90.3 5.7 %reshape.1991 = bf16[384,24,24]{2,1,0:T(8,128)(2,1)} reshape(bf16[8,2,13824]{2,1,0:T(2,128)(2,1)} %all-to-all-done) | data formatting | bytes 884736
  96.0 4.1 copy.354
  100.1 3.3 fusion.114
  103.5 6.0 %copy.356 = bf16[2,384,48,24]{2,3,0,1:T(8,128)(2,1)} copy(bf16[2,384,48,24]{1,2,3,0:T(8,128)(2,1)} %fusion.114) | data formatting | bytes 3538944 | tf_op jit(solution)/shard_map/convert_element_type | solution.py:179
  109.5 8.9 %reshape.1992 = bf16[4,2,110592]{2,1,0:T(2,128)(2,1)} reshape(bf16[384,2,24,48]{3,2,1,0:T(8,128)(2,1)} %bitcast.711) | data formatting | bytes 3538944
  118.4 6.0 %all-to-all-start.1 = ((bf16[4,2,110592]{2,1,0:T(2,128)(2,1)}), bf16[4,2,110592]{2,1,0:T(2,128)(2,1)}, u32[]{:S(2)}, u32[]{:S(2)}) async-start(bf16[4,2,110592]{2,1,0:T(2,128)(2,1)} %reshape.1992), calls=%async_computation.1 | async-start | bytes 3538944 | tf_op jit(solution)/shard_map/all_to_all | solution.py:180
  124.5 13.9 %all-reduce.4.cloned.1.call-start = ((), (), s32[]{:S(2)}) async-start(), calls=%async_computation.2 | async-start | bytes 3538944 | tf_op jit(solution)/shard_map/psum | solution.py:161
  138.4 3.1 fusion.170
  141.5 3.1 fusion.175
  144.6 5.4 bitcast_multiply_fusion
  150.1 6.6 %reshape.1993 = bf16[384,2,24,48]{3,2,1,0:T(8,128)(2,1)} reshape(bf16[4,2,110592]{2,1,0:T(2,128)(2,1)} %all-to-all-done.1) | data formatting | bytes 3538944
  156.7 5.9 %copy.357 = bf16[2,384,48,24]{1,3,2,0:T(8,128)(2,1)S(1)} copy(bf16[2,384,48,24]{2,3,0,1:T(8,128)(2,1)} %bitcast.712) | data formatting | bytes 3538944 | tf_op jit(solution)/shard_map/all_to_all | solution.py:180
  162.7 4.8 reshape.1976
  167.5 4.9 copy.358
  172.4 6.9 %copy.359 = f32[2,96,48,96]{3,2,0,1:T(8,128)} copy(f32[2,96,48,96]{1,3,2,0:T(8,128)} %bitcast.714) | data formatting | bytes 7077888
  179.3 12.6 %broadcast_in_dim.978 = f32[2,96,48,384]{2,3,0,1:T(8,128)} broadcast(f32[]{:T(128)} %constant.387.clone.1), dimensions={} | broadcast | bytes 14155780 | tf_op jit(solution)/shard_map/broadcast_in_dim | solution.py:186
  191.8 322.3 %while.22 = (s32[]{:T(128)}, f32[96,96]{1,0:T(8,128)S(1)}, f32[96,96]{1,0:T(8,128)S(1)}, f32[96,96]{1,0:T(8,128)S(1)}, f32[2,96,48,384]{2,3,0,1:T(8,128)}, /*ind...) while((s32[]{:T(128)}, f32[96,96]{1,0:T(8,128)S(1)}, ...), condition=%wide.region_5.6_spmd.clone.clone.clone, body=%wide.region_4.5_spmd.clone.clone.clone.sunk | while | flops 342472032 | bytes 14677411 | solution.py:121
  193.1 2.5 exponential_multiply_fusion.39
  196.6 2.5 stack.338
  199.1 19.5 %bitcast_dynamic-update-slice_fusion.2 = f32[2,96,48,384]{2,3,0,1:T(8,128)} fusion(f32[2,96,48,384]{2,3,0,1:T(8,128)} %get-tuple-element.1368, s32[]{:T(128)S(6)} %select_n.1786, f32[2,96,48,96]{3,2,0,1:T(8,128)} %get-tuple-element.1413, f32[32,96,96]{2,0,1:T(8,128)S(1)} %stack.338), kind=kOutput, calls=%fused_computation.3.clone.1 | convolution fusion | flops 340033536 | bytes 9043972 | tf_op jit(solution)/shard_map/while/body/lmt,pmct->pmcl/dot_general | solution.py:106
  219.9 2.5 exponential_multiply_fusion.39
  223.4 2.5 stack.338
  226.0 19.5 %bitcast_dynamic-update-slice_fusion.2 = f32[2,96,48,384]{2,3,0,1:T(8,128)} fusion(f32[2,96,48,384]{2,3,0,1:T(8,128)} %get-tuple-element.1368, s32[]{:T(128)S(6)} %select_n.1786, f32[2,96,48,96]{3,2,0,1:T(8,128)} %get-tuple-element.1413, f32[32,96,96]{2,0,1:T(8,128)S(1)} %stack.338), kind=kOutput, calls=%fused_computation.3.clone.1 | convolution fusion | flops 340033536 | bytes 9043972 | tf_op jit(solution)/shard_map/while/body/lmt,pmct->pmcl/dot_general | solution.py:106
  246.8 2.5 exponential_multiply_fusion.39
  250.2 2.5 stack.338
  252.8 19.6 %bitcast_dynamic-update-slice_fusion.2 = f32[2,96,48,384]{2,3,0,1:T(8,128)} fusion(f32[2,96,48,384]{2,3,0,1:T(8,128)} %get-tuple-element.1368, s32[]{:T(128)S(6)} %select_n.1786, f32[2,96,48,96]{3,2,0,1:T(8,128)} %get-tuple-element.1413, f32[32,96,96]{2,0,1:T(8,128)S(1)} %stack.338), kind=kOutput, calls=%fused_computation.3.clone.1 | convolution fusion | flops 340033536 | bytes 9043972 | tf_op jit(solution)/shard_map/while/body/lmt,pmct->pmcl/dot_general | solution.py:106
  273.6 2.5 exponential_multiply_fusion.39
  277.1 2.5 stack.338
  279.6 19.6 %bitcast_dynamic-update-slice_fusion.2 = f32[2,96,48,384]{2,3,0,1:T(8,128)} fusion(f32[2,96,48,384]{2,3,0,1:T(8,128)} %get-tuple-element.1368, s32[]{:T(128)S(6)} %select_n.1786, f32[2,96,48,96]{3,2,0,1:T(8,128)} %get-tuple-element.1413, f32[32,96,96]{2,0,1:T(8,128)S(1)} %stack.338), kind=kOutput, calls=%fused_computation.3.clone.1 | convolution fusion | flops 340033536 | bytes 9043972 | tf_op jit(solution)/shard_map/while/body/lmt,pmct->pmcl/dot_general | solution.py:106
  300.5 2.5 exponential_multiply_fusion.39
  304.0 2.5 stack.338
  306.5 19.5 %bitcast_dynamic-update-slice_fusion.2 = f32[2,96,48,384]{2,3,0,1:T(8,128)} fusion(f32[2,96,48,384]{2,3,0,1:T(8,128)} %get-tuple-element.1368, s32[]{:T(128)S(6)} %select_n.1786, f32[2,96,48,96]{3,2,0,1:T(8,128)} %get-tuple-element.1413, f32[32,96,96]{2,0,1:T(8,128)S(1)} %stack.338), kind=kOutput, calls=%fused_computation.3.clone.1 | convolution fusion | flops 340033536 | bytes 9043972 | tf_op jit(solution)/shard_map/while/body/lmt,pmct->pmcl/dot_general | solution.py:106
  327.3 2.5 exponential_multiply_fusion.39
  330.8 2.5 stack.338
  333.4 19.5 %bitcast_dynamic-update-slice_fusion.2 = f32[2,96,48,384]{2,3,0,1:T(8,128)} fusion(f32[2,96,48,384]{2,3,0,1:T(8,128)} %get-tuple-element.1368, s32[]{:T(128)S(6)} %select_n.1786, f32[2,96,48,96]{3,2,0,1:T(8,128)} %get-tuple-element.1413, f32[32,96,96]{2,0,1:T(8,128)S(1)} %stack.338), kind=kOutput, calls=%fused_computation.3.clone.1 | convolution fusion | flops 340033536 | bytes 9043972 | tf_op jit(solution)/shard_map/while/body/lmt,pmct->pmcl/dot_general | solution.py:106
  354.2 2.5 exponential_multiply_fusion.39
  357.7 2.5 stack.338
  360.2 19.6 %bitcast_dynamic-update-slice_fusion.2 = f32[2,96,48,384]{2,3,0,1:T(8,128)} fusion(f32[2,96,48,384]{2,3,0,1:T(8,128)} %get-tuple-element.1368, s32[]{:T(128)S(6)} %select_n.1786, f32[2,96,48,96]{3,2,0,1:T(8,128)} %get-tuple-element.1413, f32[32,96,96]{2,0,1:T(8,128)S(1)} %stack.338), kind=kOutput, calls=%fused_computation.3.clone.1 | convolution fusion | flops 340033536 | bytes 9043972 | tf_op jit(solution)/shard_map/while/body/lmt,pmct->pmcl/dot_general | solution.py:106
  381.1 2.5 exponential_multiply_fusion.39
  384.5 2.5 stack.338
  387.1 19.6 %bitcast_dynamic-update-slice_fusion.2 = f32[2,96,48,384]{2,3,0,1:T(8,128)} fusion(f32[2,96,48,384]{2,3,0,1:T(8,128)} %get-tuple-element.1368, s32[]{:T(128)S(6)} %select_n.1786, f32[2,96,48,96]{3,2,0,1:T(8,128)} %get-tuple-element.1413, f32[32,96,96]{2,0,1:T(8,128)S(1)} %stack.338), kind=kOutput, calls=%fused_computation.3.clone.1 | convolution fusion | flops 340033536 | bytes 9043972 | tf_op jit(solution)/shard_map/while/body/lmt,pmct->pmcl/dot_general | solution.py:106
  408.0 2.5 exponential_multiply_fusion.39
  411.5 2.5 stack.338
  414.0 19.5 %bitcast_dynamic-update-slice_fusion.2 = f32[2,96,48,384]{2,3,0,1:T(8,128)} fusion(f32[2,96,48,384]{2,3,0,1:T(8,128)} %get-tuple-element.1368, s32[]{:T(128)S(6)} %select_n.1786, f32[2,96,48,96]{3,2,0,1:T(8,128)} %get-tuple-element.1413, f32[32,96,96]{2,0,1:T(8,128)S(1)} %stack.338), kind=kOutput, calls=%fused_computation.3.clone.1 | convolution fusion | flops 340033536 | bytes 9043972 | tf_op jit(solution)/shard_map/while/body/lmt,pmct->pmcl/dot_general | solution.py:106
  434.8 2.5 exponential_multiply_fusion.39
  438.3 2.5 stack.338
  440.8 19.6 %bitcast_dynamic-update-slice_fusion.2 = f32[2,96,48,384]{2,3,0,1:T(8,128)} fusion(f32[2,96,48,384]{2,3,0,1:T(8,128)} %get-tuple-element.1368, s32[]{:T(128)S(6)} %select_n.1786, f32[2,96,48,96]{3,2,0,1:T(8,128)} %get-tuple-element.1413, f32[32,96,96]{2,0,1:T(8,128)S(1)} %stack.338), kind=kOutput, calls=%fused_computation.3.clone.1 | convolution fusion | flops 340033536 | bytes 9043972 | tf_op jit(solution)/shard_map/while/body/lmt,pmct->pmcl/dot_general | solution.py:106
  461.7 2.5 exponential_multiply_fusion.39
  465.2 2.5 stack.338
  467.7 19.6 %bitcast_dynamic-update-slice_fusion.2 = f32[2,96,48,384]{2,3,0,1:T(8,128)} fusion(f32[2,96,48,384]{2,3,0,1:T(8,128)} %get-tuple-element.1368, s32[]{:T(128)S(6)} %select_n.1786, f32[2,96,48,96]{3,2,0,1:T(8,128)} %get-tuple-element.1413, f32[32,96,96]{2,0,1:T(8,128)S(1)} %stack.338), kind=kOutput, calls=%fused_computation.3.clone.1 | convolution fusion | flops 340033536 | bytes 9043972 | tf_op jit(solution)/shard_map/while/body/lmt,pmct->pmcl/dot_general | solution.py:106
  488.6 2.5 exponential_multiply_fusion.39
  492.0 2.5 stack.338
  494.6 19.6 %bitcast_dynamic-update-slice_fusion.2 = f32[2,96,48,384]{2,3,0,1:T(8,128)} fusion(f32[2,96,48,384]{2,3,0,1:T(8,128)} %get-tuple-element.1368, s32[]{:T(128)S(6)} %select_n.1786, f32[2,96,48,96]{3,2,0,1:T(8,128)} %get-tuple-element.1413, f32[32,96,96]{2,0,1:T(8,128)S(1)} %stack.338), kind=kOutput, calls=%fused_computation.3.clone.1 | convolution fusion | flops 340033536 | bytes 9043972 | tf_op jit(solution)/shard_map/while/body/lmt,pmct->pmcl/dot_general | solution.py:106
  514.2 26.0 %copy.368 = f32[2,96,48,384]{3,2,1,0:T(8,128)} copy(f32[2,96,48,384]{2,3,0,1:T(8,128)} %get-tuple-element.600) | data formatting | bytes 28311552
  540.2 2.8 copy.494
  (845 shorter events, 60.7 us)
Async XLA Ops:
  7.2 1.2 copy-start
  7.2 3.3 copy-start.3
  10.5 9.7 %copy-start.6 = (s32[96,3,8]{0,2,1:T(8,128)S(1)}, s32[96,3,8]{0,2,1:T(8,128)}, u32[]{:S(2)}) copy-start(s32[96,3,8]{0,2,1:T(8,128)} %param.12) | copy-start | bytes 27652
  10.6 12.4 %copy-start.12 = (f32[96,3,3,8]{0,3,2,1:T(8,128)S(1)}, f32[96,3,3,8]{0,3,2,1:T(8,128)}, u32[]{:S(2)}) copy-start(f32[96,3,3,8]{0,3,2,1:T(8,128)} %param.11) | copy-start | bytes 82948
  10.6 12.4 %copy-start.13 = (s32[96]{0:T(128)S(1)}, s32[96]{0:T(128)}, u32[]{:S(2)}) copy-start(s32[96]{0:T(128)} %param.13) | copy-start | bytes 1156
  11.9 39.7 %collective-permute-start = (bf16[24,8,1536]{2,1,0:T(8,128)(2,1)}, bf16[24,8,1536]{2,1,0:T(8,128)(2,1)S(1)}, u32[]{:S(2)}, u32[]{:S(2)}) collective-permute-start(bf16[24,8,1536]{2,1,0:T(8,128)(2,1)} %get-tuple-element.827), channel_id=1, source_target_pairs={{0,1},{1,2},{2,3},{3,4},{4,5},{5,6},{6,7},{7,0},{8,9},{9,10},{10,1... | collective-permute-start | bytes 1769480 | tf_op jit(solution)/shard_map/ppermute | solution.py:24
  12.3 39.2 %collective-permute-start.1 = (bf16[24,8,1536]{2,1,0:T(8,128)(2,1)}, bf16[24,8,1536]{2,1,0:T(8,128)(2,1)S(1)}, u32[]{:S(2)}, u32[]{:S(2)}) collective-permute-start(bf16[24,8,1536]{2,1,0:T(8,128)(2,1)} %get-tuple-element.828), channel_id=1, source_target_pairs={{1,0},{2,1},{3,2},{4,3},{5,4},{6,5},{7,6},{0,7},{9,8},{10,9},{11,1... | collective-permute-start | bytes 1769480 | tf_op jit(solution)/shard_map/ppermute | solution.py:25
  47.4 1.0 copy-start.4
  47.4 1.0 copy-start.5
  51.6 6.9 %collective-permute-start.2 = (bf16[1,40,1536]{2,1,0:T(8,128)(2,1)S(1)}, bf16[1,40,1536]{2,1,0:T(8,128)(2,1)S(1)}, u32[]{:S(2)}, u32[]{:S(2)}) collective-permute-start(bf16[1,40,1536]{2,1,0:T(8,128)(2,1)S(1)} %get-tuple-element.825), channel_id=1, source_target_pairs={{8,0},{16,8},{24,16},{9,1},{17,9},{25,17},{10,2},{18,10},{26,18},{... | collective-permute-start | bytes 368648 | tf_op jit(solution)/shard_map/ppermute | solution.py:25
  52.9 7.0 %collective-permute-start.3 = (bf16[1,40,1536]{2,1,0:T(8,128)(2,1)S(1)}, bf16[1,40,1536]{2,1,0:T(8,128)(2,1)S(1)}, u32[]{:S(2)}, u32[]{:S(2)}) collective-permute-start(bf16[1,40,1536]{2,1,0:T(8,128)(2,1)S(1)} %get-tuple-element.826), channel_id=1, source_target_pairs={{0,8},{8,16},{16,24},{1,9},{9,17},{17,25},{2,10},{10,18},{18,26},{... | collective-permute-start | bytes 368648 | tf_op jit(solution)/shard_map/ppermute | solution.py:24
  58.5 2.1 copy-start.10
  61.0 1.0 copy-start.2
  63.4 13.3 %copy-start.14 = (f32[96]{0:T(128)S(1)}, f32[96]{0:T(128)}, u32[]{:S(2)}) copy-start(f32[96]{0:T(128)} %sine_log_fusion) | copy-start | bytes 1156
  63.4 13.3 %copy-start.15 = (f32[96]{0:T(128)S(1)}, f32[96]{0:T(128)}, u32[]{:S(2)}) copy-start(f32[96]{0:T(128)} %get-tuple-element.894) | copy-start | bytes 1156
  63.5 13.4 %copy-start.7 = (f32[24,3,3]{2,0,1:T(8,128)S(1)}, f32[24,3,3]{2,0,1:T(8,128)}, u32[]{:S(2)}) copy-start(f32[24,3,3]{2,0,1:T(8,128)} %copy.365) | copy-start | bytes 2596
  63.5 13.4 %copy-start.8 = (f32[24,3,3]{2,0,1:T(8,128)S(1)}, f32[24,3,3]{2,0,1:T(8,128)}, u32[]{:S(2)}) copy-start(f32[24,3,3]{2,0,1:T(8,128)} %copy.367) | copy-start | bytes 2596
  63.5 13.4 %copy-start.9 = (f32[24,3,3]{2,0,1:T(8,128)S(1)}, f32[24,3,3]{2,0,1:T(8,128)}, u32[]{:S(2)}) copy-start(f32[24,3,3]{2,0,1:T(8,128)} %copy.363) | copy-start | bytes 2596
  72.3 18.0 %all-to-all-start = ((bf16[8,2,13824]{2,1,0:T(2,128)(2,1)}), bf16[8,2,13824]{2,1,0:T(2,128)(2,1)}, u32[]{:S(2)}, u32[]{:S(2)}) async-start(bf16[8,2,13824]{2,1,0:T(2,128)(2,1)} %reshape.1990), calls=%async_computation | async-start | bytes 884736 | tf_op jit(solution)/shard_map/all_to_all | solution.py:172
  118.4 31.7 %all-to-all-start.1 = ((bf16[4,2,110592]{2,1,0:T(2,128)(2,1)}), bf16[4,2,110592]{2,1,0:T(2,128)(2,1)}, u32[]{:S(2)}, u32[]{:S(2)}) async-start(bf16[4,2,110592]{2,1,0:T(2,128)(2,1)} %reshape.1992), calls=%async_computation.1 | async-start | bytes 3538944 | tf_op jit(solution)/shard_map/all_to_all | solution.py:180
  124.5 415.7 %all-reduce.4.cloned.1.call-start = ((), (), s32[]{:S(2)}) async-start(), calls=%async_computation.2 | async-start | bytes 3538944 | tf_op jit(solution)/shard_map/psum | solution.py:161
  141.5 3.1 copy-start.11
  514.2 28.9 %copy-start.1 = (bf16[3,384,384]{2,1,0:T(8,128)(2,1)S(1)}, bf16[3,384,384]{2,1,0:T(8,128)(2,1)}, u32[]{:S(2)}) copy-start(bf16[3,384,384]{2,1,0:T(8,128)(2,1)} %param.10) | copy-start | bytes 2654212
Sparse Core Ops, SparseCore 0:
  150.2 132.1 all-reduce.3
where the time goes:
time: 559 us; the launch traced here: 550 us
  matrix products  254 us (45%)
  local copies, waits for them, and re-layouts  157 us (28%)
  other arithmetic  74.2 us (13%)
  starting transfers between devices  34.7 us (6%)
  between operations  17.2 us (3%)
  waiting for transfers between devices  7.81 us (1%)
    dot_general x12, matrix products, block_step(): jnp.einsum('lmt,pmct->pmcl', jnp.stack(levels), spec_part, precision=lax....  235 us
    unnamed x48, local copies, waits for them, and re-layouts  69.2 us
    mul x84, other arithmetic, block_step(): levels.append(fresh * factor)  42.6 us
    another operation x12, local copies, waits for them, and re-layouts, block_step(): jnp.stack(levels)  30.5 us
    psum x1, starting transfers between devices, on_device(): grad_mix = lax.psum(mix_local, ('lat', 'lon'))  13.9 us
    broadcast_in_dim x1, local copies, waits for them, and re-layouts, on_device(): result = jnp.zeros((2, block_rows, chan_block, L), jnp.float32)  12.6 us
    convert_element_type x24, local copies, waits for them, and re-layouts, band_matrix(): jnp.transpose(weights[:, :, :, tap_slot], (0, 2, 1)).astype(jnp.float32)  11.7 us
  transfers between devices with their start and end apart: 7, of which 2 were waited for; matrix products, arithmetic and copies ran while one was open for 80% of the time, Pallas kernels for 0%

commit v1 on v0

v1 whole, which is shorter than its diff:
```python
import functools
import math

import jax
import jax.numpy as jnp
from jax import lax
from jax.experimental import pallas as pl
from jax.experimental.pallas import tpu as pltpu
from jax.sharding import PartitionSpec as P

M = 384
L = 384
K = 3
R = 8
S = 8
LB = 32
MSTEP = 8
VMEM_BYTES = 56 * 1024 * 1024


def round_up(value, unit):
    return -(-value // unit) * unit


def live_taps(taps, counts):
    slot_ids = lax.broadcasted_iota(jnp.int32, taps.shape, 3)
    keep_mask = slot_ids < counts[:, None, None, None]
    return jnp.where(keep_mask, taps, jnp.float32(0.0)).astype(jnp.bfloat16)


def dft_table(lon_total, orders):
    columns = lax.broadcasted_iota(jnp.int32, (lon_total,), 0)
    phases = orders[:, None] * columns[None, :] % lon_total
    angles = 2.0 * math.pi / lon_total * phases.astype(jnp.float32)
    return jnp.stack([jnp.cos(angles), -jnp.sin(angles)]).astype(jnp.bfloat16)


def colatitudes(lat_total):
    angles = (lax.broadcasted_iota(jnp.int32, (lat_total,), 0).astype(jnp.float32) + 0.5) * (
        math.pi / lat_total
    )
    return (jnp.cos(angles), jnp.log(jnp.sin(angles)))


def seed_logs(order_total):
    degrees = lax.broadcasted_iota(jnp.int32, (order_total,), 0).astype(jnp.float32)
    step_logs = jnp.log((2.0 * degrees + 1.0) / (2.0 * degrees + 2.0))
    prefix = jnp.concatenate([jnp.zeros((1,), jnp.float32), jnp.cumsum(step_logs)[:-1]])
    return 0.5 * jnp.log((2.0 * degrees + 1.0) / (4.0 * math.pi)) + 0.5 * prefix


def legendre_kernel(first_ref, cos_ref, seed_ref, table_ref, prev_ref, early_ref, scale_ref, *stage_refs):
    step = pl.program_id(0)
    rows, width = seed_ref.shape
    first = first_ref[0]

    @pl.when(step == 0)
    def _():
        prev_ref[...] = jnp.zeros_like(prev_ref)
        early_ref[...] = jnp.zeros_like(early_ref)
        scale_ref[...] = seed_ref[...]

    chunk = 48 if rows % 48 == 0 else 8
    cosines = cos_ref[...]
    for begin in range(0, rows, chunk):
        span = slice(begin, begin + chunk)
        order_i = lax.broadcasted_iota(jnp.int32, (chunk, LB), 0) + (first + begin)
        degree_i = lax.broadcasted_iota(jnp.int32, (chunk, LB), 1) + step * LB
        order = order_i.astype(jnp.float32)
        degree = degree_i.astype(jnp.float32)
        higher = degree_i > order_i
        lower_a = jnp.where(higher, degree * degree - order * order, 1.0)
        factor_a = jnp.sqrt((4.0 * degree * degree - 1.0) / lower_a)
        upper_b = jnp.maximum((degree - 1.0) * (degree - 1.0) - order * order, 0.0)
        lower_b = jnp.maximum(4.0 * (degree - 1.0) * (degree - 1.0) - 1.0, 1.0)
        factor_b = jnp.sqrt(upper_b / lower_b)
        gain = jnp.where(higher, factor_a, 0.0)
        back = jnp.where(higher, factor_a * factor_b, 0.0)
        wide_order = lax.broadcasted_iota(jnp.int32, (chunk, width), 0) + (first + begin)
        previous = prev_ref[span, :]
        earlier = early_ref[span, :]
        scales = scale_ref[span, :]
        factor = jnp.exp(scales)
        for inner in range(LB):
            seeded = jnp.where(wide_order == step * LB + inner, 1.0, 0.0)
            fresh = (
                gain[:, inner : inner + 1] * (cosines * previous)
                - back[:, inner : inner + 1] * earlier
                + seeded
            )
            level = fresh * factor
            for tile, stage_ref in enumerate(stage_refs):
                stage_ref[pl.ds(begin * LB + inner, chunk, stride=LB), :] = level[:, tile * 128 : tile * 128 + 128]
            earlier, previous = previous, fresh
        biggest = jnp.maximum(jnp.abs(previous), jnp.abs(earlier))
        divisor = jnp.where(biggest > 0.0, biggest, 1.0)
        prev_ref[span, :] = previous / divisor
        early_ref[span, :] = earlier / divisor
        scale_ref[span, :] = scales + jnp.log(divisor)
    for tile, stage_ref in enumerate(stage_refs):
        staged = stage_ref[...].reshape(rows, LB, 128).astype(jnp.bfloat16)
        table_ref[:, :, tile * 128 : tile * 128 + 128] = staged


def legendre_table(first_order, cosines, logscale):
    rows, lat_total = logscale.shape
    width = round_up(lat_total, 128)
    spare = width - lat_total
    cos_pad = jnp.pad(cosines, (0, spare))[None, :]
    seed_pad = jnp.pad(logscale, ((0, 0), (0, spare)), constant_values=-1.0e4)
    stage_rows = rows * LB
    return pl.pallas_call(
        legendre_kernel,
        grid=(L // LB,),
        in_specs=[
            pl.BlockSpec(memory_space=pltpu.SMEM),
            pl.BlockSpec((1, width), lambda i: (0, 0)),
            pl.BlockSpec((rows, width), lambda i: (0, 0)),
        ],
        out_specs=pl.BlockSpec((rows, LB, width), lambda i: (0, i, 0)),
        out_shape=jax.ShapeDtypeStruct((rows, L, width), jnp.bfloat16),
        scratch_shapes=[pltpu.VMEM((rows, width), jnp.float32)] * 3
        + [pltpu.VMEM((stage_rows, 128), jnp.float32)] * (width // 128),
        compiler_params=pltpu.CompilerParams(vmem_limit_bytes=VMEM_BYTES),
        cost_estimate=pl.CostEstimate(
            flops=rows * L * width * 10, bytes_accessed=rows * L * width * 2, transcendentals=0
        ),
        name="legendre_table",
    )(first_order.reshape(1), cos_pad, seed_pad)


def synthesis_kernel(lon_total, lat_total, dft_ref, grid_ref, table_ref, out_ref, modes_ref):
    step = pl.program_id(0)
    bands, _, packed = grid_ref.shape
    rows = dft_ref.shape[0] // 2
    chans = out_ref.shape[2]
    lat_dev = packed // chans
    width = table_ref.shape[2]

    @pl.when(step == 0)
    def _():
        @pl.loop(0, bands)
        def _(band):
            modes = jnp.dot(dft_ref[...], grid_ref[band], preferred_element_type=jnp.float32)
            modes = (modes * (1.0 / math.sqrt(lon_total))).astype(jnp.bfloat16).astype(jnp.float32)
            for lat in range(lat_dev):
                dest = pl.ds(pl.multiple_of((band * lat_dev + lat) * rows, 8), rows)
                lanes = slice(lat * chans, (lat + 1) * chans)
                modes_ref[dest, 0:chans] = modes[0:rows, lanes]
                modes_ref[dest, chans : 2 * chans] = modes[rows : 2 * rows, lanes]

    leg_scale = math.sqrt(4.0 * math.pi / lat_total)
    for inner in range(MSTEP):
        picked = modes_ref[pl.ds(step * MSTEP + inner, lat_total, stride=rows), :]
        if width > lat_total:
            spare = jnp.zeros((width - lat_total, picked.shape[1]), jnp.float32)
            picked = jnp.concatenate([picked, spare], axis=0)
        turned = picked.T[0 : 2 * chans].astype(jnp.bfloat16)
        product = lax.dot_general(
            turned, table_ref[inner], (((1,), (1,)), ((), ())), preferred_element_type=jnp.float32
        )
        product = product * leg_scale
        out_ref[0, inner] = product[0:chans]
        out_ref[1, inner] = product[chans : 2 * chans]


def synthesis(dft_rows, gathered, table, chans, lat_total, lon_total):
    rows = table.shape[0]
    width = table.shape[2]
    whole = lambda i: (0, 0)
    return pl.pallas_call(
        functools.partial(synthesis_kernel, lon_total, lat_total),
        grid=(rows // MSTEP,),
        in_specs=[
            pl.BlockSpec(dft_rows.shape, whole),
            pl.BlockSpec(gathered.shape, lambda i: (0, 0, 0), pipeline_mode=pl.Buffered(1)),
            pl.BlockSpec((MSTEP, L, width), lambda i: (i, 0, 0)),
        ],
        out_specs=pl.BlockSpec((2, MSTEP, chans, L), lambda i: (0, i, 0, 0)),
        out_shape=jax.ShapeDtypeStruct((2, rows, chans, L), jnp.float32),
        scratch_shapes=[pltpu.VMEM((lat_total * rows, 128), jnp.float32)],
        compiler_params=pltpu.CompilerParams(vmem_limit_bytes=VMEM_BYTES),
        name="dft_synthesis",
    )(dft_rows, gathered, table)


def grid_kernel(
    lon_count, ext_ref, cot_ref, weight_ref, tap_own_ref, shift_own_ref, tap_back_ref, shift_back_ref,
    response_ref, field_ref, send_ref, moved_ref, total_ref, packed_ref,
):
    lat_dev = tap_own_ref.shape[0]
    cells, channels = cot_ref.shape
    lon_dev = cells // lat_dev
    lanes = tap_own_ref.shape[2]
    ext_width = lanes // 3
    lane = lax.broadcasted_iota(jnp.int32, (lon_dev, lanes), 1)
    lane = jnp.where(lane >= 2 * ext_width, lane - 2 * ext_width, jnp.where(lane >= ext_width, lane - ext_width, lane))
    relative = lane - lax.broadcasted_iota(jnp.int32, (lon_dev, lanes), 0) - R

    def bands(row, tap_ref, shift_ref):
        summed = [jnp.zeros((lon_dev, lanes), jnp.float32)] * K
        for slot in range(S):
            hit = relative == shift_ref[row, slot : slot + 1, :]
            for k in range(K):
                tap = tap_ref[row, k * S + slot : k * S + slot + 1, :]
                summed[k] = summed[k] + jnp.where(hit, tap, 0.0)
        return jnp.concatenate(summed, axis=0).astype(jnp.bfloat16)

    @pl.loop(0, lat_dev // 2)
    def _(pair):
        own, back = [], []
        for half in range(2):
            row = pair * 2 + half
            rows = pl.ds(pl.multiple_of(row * ext_width, 16), lanes)
            own.append(
                jnp.dot(
                    bands(row, tap_own_ref, shift_own_ref), ext_ref[rows, 0:channels],
                    preferred_element_type=jnp.float32,
                )
            )
            back.append(
                jnp.dot(
                    bands(row, tap_back_ref, shift_back_ref), ext_ref[rows, channels : 2 * channels],
                    preferred_element_type=jnp.float32,
                )
            )
        dest = pl.ds(pl.multiple_of(pair * 2 * lon_dev, 16), 2 * lon_dev)
        for k in range(K):
            part = slice(k * lon_dev, (k + 1) * lon_dev)
            cols = slice(k * channels, (k + 1) * channels)
            response_ref[dest, cols] = jnp.concatenate([own[0][part], own[1][part]], axis=0).astype(jnp.bfloat16)
            moved_ref[dest, cols] = jnp.concatenate([back[0][part], back[1][part]], axis=0).astype(jnp.bfloat16)

    total = cot_ref[...].astype(jnp.float32)
    for k in range(K):
        total = total + lax.dot_general(
            moved_ref[:, k * channels : (k + 1) * channels], weight_ref[k],
            (((1,), (1,)), ((), ())), preferred_element_type=jnp.float32,
        )
    rounded = total.astype(jnp.bfloat16)
    field_ref[...] = rounded
    total_ref[...] = rounded.astype(jnp.float32)
    chans = channels // lon_count
    for lat in range(lat_dev):
        for dest in range(lon_count):
            packed_ref[dest, :, lat * chans : (lat + 1) * chans] = total_ref[
                lat * lon_dev : (lat + 1) * lon_dev, dest * chans : (dest + 1) * chans
            ]
    send_ref[...] = packed_ref[...].astype(jnp.bfloat16)


def grid_part(ext, cot, mix_weight, tap_own, shift_own, tap_back, shift_back, lon_count):
    cells, channels = cot.shape
    lat_dev = tap_own.shape[0]
    lon_dev = cells // lat_dev
    packed = (lon_count, lon_dev, lat_dev * (channels // lon_count))
    return pl.pallas_call(
        functools.partial(grid_kernel, lon_count),
        in_specs=[pl.BlockSpec(memory_space=pltpu.VMEM)] * 7,
        out_specs=[pl.BlockSpec(memory_space=pltpu.VMEM)] * 3,
        out_shape=[
            jax.ShapeDtypeStruct((cells, K * channels), jnp.bfloat16),
            jax.ShapeDtypeStruct((cells, channels), jnp.bfloat16),
            jax.ShapeDtypeStruct(packed, jnp.bfloat16),
        ],
        scratch_shapes=[
            pltpu.VMEM((cells, K * channels), jnp.bfloat16),
            pltpu.VMEM((cells, channels), jnp.float32),
            pltpu.VMEM(packed, jnp.float32),
        ],
        compiler_params=pltpu.CompilerParams(vmem_limit_bytes=VMEM_BYTES),
        name="grid_part",
    )(ext, cot, mix_weight, tap_own, shift_own, tap_back, shift_back)


def swap_edges(shard, axis, dim, width, wrap):
    devices, length = lax.axis_size(axis), shard.shape[dim]
    up = [(i, (i + 1) % devices) for i in range(devices if wrap else devices - 1)]
    down = [(j, i) for i, j in up]
    before = lax.ppermute(lax.slice_in_dim(shard, length - width, length, axis=dim), axis, up)
    after = lax.ppermute(lax.slice_in_dim(shard, 0, width, axis=dim), axis, down)
    return before, after


def spread(values, ext_width):
    return jnp.repeat(values, ext_width, axis=-1)


def on_device(field, cotangent, mix_weight, taps, offsets, counts):
    lat_dev, lon_dev, channels = field.shape
    lat_count = lax.axis_size("lat")
    lon_count = lax.axis_size("lon")
    total_lat = lat_dev * lat_count
    total_lon = lon_dev * lon_count
    lat_pos = lax.axis_index("lat")
    block_rows = M // lat_count
    chans = channels // lon_count
    first_row = lat_pos * lat_dev
    ext_width = round_up(lon_dev + 2 * R, 16)

    both = jnp.concatenate([field, cotangent], axis=2)
    before, after = swap_edges(both, "lon", 1, R, True)
    spare = jnp.zeros((lat_dev, ext_width - lon_dev - 2 * R, 2 * channels), jnp.bfloat16)
    wide = jnp.concatenate([before, both, after, spare], axis=1)
    above, below = swap_edges(wide, "lat", 0, 1, False)
    ext = jnp.concatenate([above, wide, below], axis=0).reshape((lat_dev + 2) * ext_width, 2 * channels)

    live = live_taps(taps, counts).astype(jnp.float32)
    live_ext = lax.dynamic_slice_in_dim(jnp.pad(live, ((1, 1), (0, 0), (0, 0), (0, 0))), first_row, lat_dev + 2, 0)
    shift_ext = lax.dynamic_slice_in_dim(jnp.pad(offsets, ((1, 1), (0, 0), (0, 0))), first_row, lat_dev + 2, 0)
    tap_own = spread(jnp.transpose(live_ext[1:-1], (0, 1, 3, 2)), ext_width).reshape(lat_dev, K * S, 3 * ext_width)
    shift_own = spread(jnp.transpose(shift_ext[1:-1], (0, 2, 1)), ext_width)
    live_back = jnp.stack([live_ext[a : a + lat_dev, :, 2 - a, :] for a in range(3)], axis=-1)
    shift_back = jnp.stack([-shift_ext[a : a + lat_dev, 2 - a, :] for a in range(3)], axis=-1)
    tap_back = spread(live_back, ext_width).reshape(lat_dev, K * S, 3 * ext_width)
    shift_back = spread(shift_back, ext_width)

    cot_flat = cotangent.reshape(lat_dev * lon_dev, channels)
    response, grad_field, packed = grid_part(
        ext, cot_flat, mix_weight, tap_own, shift_own, tap_back, shift_back, lon_count
    )

    cosines, log_sines = colatitudes(total_lat)
    orders = lat_pos * block_rows + lax.broadcasted_iota(jnp.int32, (block_rows,), 0)
    own_logs = lax.dynamic_slice_in_dim(seed_logs(M), lat_pos * block_rows, block_rows, 0)
    logscale = own_logs[:, None] + orders.astype(jnp.float32)[:, None] * log_sines[None, :]
    table = legendre_table((lat_pos * block_rows).astype(jnp.int32), cosines, logscale)
    dft_rows = dft_table(total_lon, orders).reshape(2 * block_rows, total_lon)

    columns = lax.all_to_all(packed, "lon", split_axis=0, concat_axis=0, tiled=True)
    columns = columns.reshape(total_lon, lat_dev * chans)
    gathered = lax.all_gather(columns, "lat", axis=0, tiled=False)
    grad_spectra = synthesis(dft_rows, gathered, table, chans, total_lat, total_lon)

    mix_local = lax.dot_general(
        response, cot_flat, (((0,), (0,)), ((), ())), preferred_element_type=jnp.float32
    ) * (1.0 / math.sqrt(total_lat * total_lon))
    grad_mix = lax.psum(mix_local, ("lat", "lon")).reshape(K, channels, channels)
    return (grad_field.reshape(lat_dev, lon_dev, channels), grad_spectra, grad_mix)


def solution(mesh):
    placed = (P("lat", "lon", None), P("lat", "lon", None), P(), P(), P(), P())
    return jax.shard_map(
        on_device,
        mesh=mesh,
        in_specs=placed,
        out_specs=(P("lat", "lon", None), P(None, "lat", "lon", None), P()),
        check_vma=False,
    )
```

time: 559 us -> 215 us (0.38); the launches traced: 550 us -> 214 us
  matrix products: 254 us -> 3.6 us
  local copies, waits for them, and re-layouts: 157 us -> 14.5 us
  waiting for transfers between devices: 7.81 us -> 98.6 us
  other arithmetic: 74.2 us -> 3.42 us
  Pallas kernels: 0 us -> 50.7 us
  starting transfers between devices: 34.7 us -> 9.76 us
  blocking collectives: 0 us -> 17.7 us
    dot_general x20 -> x1, matrix products: 254 us -> 3.6 us  [on_device(): lax.dot_general(response, cot_flat, (((0,), (0,)), ((), ())), preferred_e...]
    psum x1, waiting for transfers between devices: 0.01 us -> 92.7 us  [on_device(): lax.psum(mix_local, ('lat', 'lon')).reshape(K, channels, channels)]
    unnamed x48 -> x10, local copies, waits for them, and re-layouts: 69.2 us -> 3.87 us
    pallas_call x0 -> x3, Pallas kernels: none -> 50.7 us  [the longest x1 23.5 us: legendre_table(): pl.pallas_call(legendre_kernel, grid=(L // LB,), in_specs=[pl.BlockSpec(m...]
    mul x86 -> x0, other arithmetic: 44 us -> none  [the longest x84 42.6 us: block_step(): levels.append(fresh * factor)]
    convert_element_type x28 -> x0, local copies, waits for them, and re-layouts: 31.1 us -> none  [the longest x24 11.7 us: band_matrix(): jnp.transpose(weights[:, :, :, tap_slot], (0, 2, 1)).astype(jnp.float32)]
    another operation x15 -> x6, local copies, waits for them, and re-layouts: 30.7 us -> 3.14 us  [the longest x1 1.3 us: on_device(): spread(live_back, ext_width).reshape(lat_dev, K * S, 3 * ext_width)]
    all_to_all x0 -> x1, blocking collectives: none -> 17.7 us  [on_device(): lax.all_to_all(packed, 'lon', split_axis=0, concat_axis=0, tiled=True)]
  transfers between devices with their start and end apart: 7 -> 6, of which waited for: 2 -> 3; matrix products, arithmetic and copies ran while one was open for 80% -> 7% of each run, Pallas kernels for 0% -> 19%
where the time goes in v1:
time: 215 us; the launch traced here: 214 us
  waiting for transfers between devices  98.6 us (46%)
  Pallas kernels  50.7 us (24%)
  blocking collectives  17.7 us (8%)
  between operations  15.6 us (7%)
  local copies, waits for them, and re-layouts  14.5 us (7%)
  starting transfers between devices  9.76 us (5%)
  matrix products  3.6 us (2%)
  other arithmetic  3.42 us (2%)
    psum x1, waiting for transfers between devices, on_device(): lax.psum(mix_local, ('lat', 'lon')).reshape(K, channels, channels)  92.7 us
    pallas_call x1, Pallas kernels, legendre_table(): pl.pallas_call(legendre_kernel, grid=(L // LB,), in_specs=[pl.BlockSpec(m...  23.5 us
    pallas_call x1, Pallas kernels, synthesis(): pl.pallas_call(functools.partial(synthesis_kernel, lon_total, lat_total),...  17.8 us
    all_to_all x1, blocking collectives, on_device(): lax.all_to_all(packed, 'lon', split_axis=0, concat_axis=0, tiled=True)  17.7 us
    pallas_call x1, Pallas kernels, grid_part(): pl.pallas_call(functools.partial(grid_kernel, lon_count), in_specs=[pl.Bl...  9.41 us
    ppermute x2, starting transfers between devices, swap_edges(): lax.ppermute(lax.slice_in_dim(shard, 0, width, axis=dim), axis, down)  5.33 us
    ppermute x2, starting transfers between devices, swap_edges(): lax.ppermute(lax.slice_in_dim(shard, length - width, length, axis=dim), a...  4.35 us
    ppermute x2, waiting for transfers between devices, swap_edges(): lax.ppermute(lax.slice_in_dim(shard, 0, width, axis=dim), axis, down)  4.32 us
  transfers between devices with their start and end apart: 6, of which 3 were waited for; matrix products, arithmetic and copies ran while one was open for 7% of the time, Pallas kernels for 19%

profile of v1, /device:TPU:0, one launch (start us, length us, event | category | flops | bytes accessed | tf_op | source)
XLA Modules:
  0.0 213.9 jit_solution(5306996565947074794)
XLA Ops:
  8.0 0.0 copy-start.1
  8.0 0.0 copy-start.3
  8.0 0.0 copy-start.2
  8.0 0.0 all-gather.2.cloned.1.call-start
  8.1 1.1 constant_dynamic-update-slice_fusion.1
  9.1 1.1 constant_dynamic-update-slice_fusion
  10.2 0.8 fusion.15
  11.0 0.5 collective-permute-start
  11.4 4.0 %collective-permute-start.1 = (bf16[24,8,768]{2,1,0:T(8,128)(2,1)S(1)}, bf16[24,8,768]{2,1,0:T(8,128)(2,1)S(1)}, u32[]{:S(2)}, u32[]{:S(2)}) collective-permute-start(bf16[24,8,768]{2,1,0:T(8,128)(2,1)S(1)} %get-tuple-element.12), channel_id=1, source_target_pairs={{1,0},{2,1},{3,2},{4,3},{5,4},{6,5},{7,6},{0,7},{9,8},{10,9},{11,1... | collective-permute-start | bytes 884744 | tf_op jit(solution)/shard_map/ppermute | solution.py:281
  15.5 0.0 copy-done.1
  15.5 0.1 fusion.8
  15.6 0.1 copy.26
  15.7 0.3 broadcast_in_dim.33
  16.0 0.9 reshape.184.shift_back_ref
  16.9 0.0 copy-done.3
  16.9 0.0 copy-done.2
  16.9 0.1 dynamic-slice_convert_fusion
  17.0 0.1 slice_bitcast_fusion.3
  17.1 0.2 copy.25
  17.3 0.8 broadcast_in_dim.32
  18.1 1.3 reshape_reshape.7.tap_back_ref
  19.4 0.1 slice_bitcast_fusion
  19.4 0.2 copy.21
  19.7 0.8 broadcast_in_dim.30
  20.5 1.3 reshape_reshape.6.tap_own_ref
  21.7 0.0 collective-permute-done
  21.7 0.0 collective-permute-done.1
  21.8 3.9 %collective-permute-start.2 = (bf16[1,48,768]{2,1,0:T(8,128)(2,1)S(1)}, bf16[1,48,768]{2,1,0:T(8,128)(2,1)S(1)}, u32[]{:S(2)}, u32[]{:S(2)}) collective-permute-start(bf16[1,48,768]{2,1,0:T(8,128)(2,1)S(1)} %get-tuple-element.9), channel_id=1, source_target_pairs={{0,8},{8,16},{16,24},{1,9},{9,17},{17,25},{2,10},{10,18},{18,26},{... | collective-permute-start | bytes 221192 | tf_op jit(solution)/shard_map/ppermute | solution.py:280
  25.7 1.3 collective-permute-start.3
  27.0 0.1 dynamic-slice_bitcast_fusion
  27.1 0.1 copy.22
  27.2 0.3 broadcast_in_dim.31
  27.5 0.9 reshape.183.shift_own_ref
  28.3 0.0 collective-permute-done.2
  28.3 4.3 %collective-permute-done.3 = bf16[1,48,768]{2,1,0:T(8,128)(2,1)S(1)} collective-permute-done((bf16[1,48,768]{2,1,0:T(8,128)(2,1)S(1)}, bf16[1,48,768]{2,1,0:T(8,128)(2,1)S(1)}, u32[]{:S(2)}, u32[]{:S(2)}) %collective-permute-start.3) | collective-permute-done | bytes 73760 | tf_op jit(solution)/shard_map/ppermute | solution.py:281
  32.7 1.4 pad_maximum_fusion
  34.0 0.0 copy-start
  34.0 9.4 %grid_part.1 = (bf16[576,1152]{1,0:T(8,128)(2,1)}, bf16[576,384]{1,0:T(8,128)(2,1)}, bf16[8,24,1152]{2,1,0:T(8,128)(2,1)}) custom-call(bf16[1248,768]{1,0:T(8,128)(2,1)} %bitcast.34, bf16[576,384]{1,0:T(8,128)(2,1)} %bitcast.35, bf16[3,384,384]{2,1,0:T(8,128)(2,1)} %weight_ref.1, f32[24,24,144]{2,1,0:T(8,128)} %reshape_reshape.6.tap_own_ref, ...), custom_call_target="tpu_custom_call" | custom-call | tf_op jit(solution)/shard_map/grid_part/pallas_call | solution.py:257
  43.4 17.7 %all_to_all.5 = bf16[8,24,1152]{2,1,0:T(8,128)(2,1)} all-to-all(bf16[8,24,1152]{2,1,0:T(8,128)(2,1)} %get-tuple-element.7), channel_id=1, replica_groups=mesh['lat'=4,'lon'=8] {'lon'}, dimensions={0} | all-to-all | bytes 884736 | tf_op jit(solution)/shard_map/all_to_all | solution.py:330
  61.1 0.0 all-gather.2.cloned.1.call-update
  61.2 0.0 all-reduce.6.cloned.1.call-start
  61.2 0.3 reduce-window.9
  61.5 0.1 slice.58
  61.7 0.1 slice_reduce_fusion
  61.8 0.1 add_bitcast_fusion
  61.8 0.1 fusion.11
  61.9 0.1 dynamic_slice.11
  62.0 0.0 copy-done
  62.0 3.6 %convolution_multiply_fusion = f32[1152,384]{1,0:T(8,128)} fusion(bf16[576,1152]{1,0:T(8,128)(2,1)} %get-tuple-element.8, bf16[576,384]{1,0:T(8,128)(2,1)S(1)} %bitcast.36), kind=kOutput, calls=%fused_computation | convolution fusion | flops 510050304 | bytes 3538944 | tf_op jit(solution)/shard_map/dot_general | solution.py:335
  65.6 0.0 all-reduce.6.cloned.1.call-update
  65.7 0.1 multiply_add_fusion
  65.8 0.6 pad.23.seed_ref
  66.5 0.5 pad_bitcast_fusion.cos_ref
  67.0 23.5 %legendre_table.1.table_ref = bf16[96,384,128]{2,1,0:T(8,128)(2,1)} custom-call(s32[1]{0:T(128)} %bitcast.13.first_ref, f32[1,128]{1,0:T(1,128)} %pad_bitcast_fusion.cos_ref, f32[96,128]{1,0:T(8,128)} %pad.23.seed_ref), custom_call_target="tpu_custom_call" | custom-call | flops 47185920 | bytes 9437184 | tf_op jit(solution)/shard_map/legendre_table/pallas_call | solution.py:112
  90.5 0.5 cosine_convert_fusion
  91.0 0.7 pad_maximum_fusion.1
  91.6 1.6 all-gather.2.cloned.1.call-done.grid_ref
  93.2 17.8 %dft_synthesis.1 = f32[2,96,48,384]{3,2,1,0:T(8,128)} custom-call(bf16[192,192]{1,0:T(8,128)(2,1)} %bitcast.39, bf16[4,192,1152]{2,1,0:T(8,128)(2,1)} %all-gather.2.cloned.1.call-done.grid_ref, bf16[96,384,128]{2,1,0:T(8,128)(2,1)} %legendre_table.1.table_ref), custom_call_target="tpu_custom_call" | custom-call | tf_op jit(solution)/shard_map/dft_synthesis/pallas_call | solution.py:171
  111.0 92.7 %all-reduce.6.cloned.1.call-done = f32[3,384,384]{2,1,0:T(8,128)} async-done(((f32[3,384,384]{2,1,0:T(8,128)}), f32[3,384,384]{2,1,0:T(8,128)}) %all-reduce.6.cloned.1.call-update) | async-done | bytes 1769488 | tf_op jit(solution)/shard_map/psum | solution.py:338
  203.7 2.8 %copy.31 = f32[3,384,384]{2,1,0:T(8,128)} copy(f32[3,384,384]{2,1,0:T(8,128)} %all-reduce.6.cloned.1.call-done) | data formatting | bytes 3538944
  (10 shorter events, 0.2 us)
Async XLA Ops:
  8.0 7.5 %copy-start.1 = (s32[96,3,8]{0,2,1:T(8,128)S(1)}, s32[96,3,8]{0,2,1:T(8,128)}, u32[]{:S(2)}) copy-start(s32[96,3,8]{0,2,1:T(8,128)} %param.10) | copy-start | bytes 27652
  8.0 8.9 %copy-start.3 = (s32[96]{0:T(128)S(1)}, s32[96]{0:T(128)}, u32[]{:S(2)}) copy-start(s32[96]{0:T(128)} %param.11) | copy-start | bytes 1156
  8.0 8.8 %copy-start.2 = (f32[96,3,3,8]{0,3,2,1:T(8,128)S(1)}, f32[96,3,3,8]{0,3,2,1:T(8,128)}, u32[]{:S(2)}) copy-start(f32[96,3,3,8]{0,3,2,1:T(8,128)} %param.9) | copy-start | bytes 82948
  8.0 85.2 %all-gather.2.cloned.1.call-start = ((), (), s32[]{:S(2)}) async-start(), calls=%async_computation.1 | async-start | bytes 2211840 | tf_op jit(solution)/shard_map/all_gather | solution.py:332
  11.0 10.7 %collective-permute-start = (bf16[24,8,768]{2,1,0:T(8,128)(2,1)}, bf16[24,8,768]{2,1,0:T(8,128)(2,1)S(1)}, u32[]{:S(2)}, u32[]{:S(2)}) collective-permute-start(bf16[24,8,768]{2,1,0:T(8,128)(2,1)} %get-tuple-element.11), channel_id=1, source_target_pairs={{0,1},{1,2},{2,3},{3,4},{4,5},{5,6},{6,7},{7,0},{8,9},{9,10},{10,1... | collective-permute-start | bytes 884744 | tf_op jit(solution)/shard_map/ppermute | solution.py:280
  11.4 10.3 %collective-permute-start.1 = (bf16[24,8,768]{2,1,0:T(8,128)(2,1)S(1)}, bf16[24,8,768]{2,1,0:T(8,128)(2,1)S(1)}, u32[]{:S(2)}, u32[]{:S(2)}) collective-permute-start(bf16[24,8,768]{2,1,0:T(8,128)(2,1)S(1)} %get-tuple-element.12), channel_id=1, source_target_pairs={{1,0},{2,1},{3,2},{4,3},{5,4},{6,5},{7,6},{0,7},{9,8},{10,9},{11,1... | collective-permute-start | bytes 884744 | tf_op jit(solution)/shard_map/ppermute | solution.py:281
  21.8 6.6 %collective-permute-start.2 = (bf16[1,48,768]{2,1,0:T(8,128)(2,1)S(1)}, bf16[1,48,768]{2,1,0:T(8,128)(2,1)S(1)}, u32[]{:S(2)}, u32[]{:S(2)}) collective-permute-start(bf16[1,48,768]{2,1,0:T(8,128)(2,1)S(1)} %get-tuple-element.9), channel_id=1, source_target_pairs={{0,8},{8,16},{16,24},{1,9},{9,17},{17,25},{2,10},{10,18},{18,26},{... | collective-permute-start | bytes 221192 | tf_op jit(solution)/shard_map/ppermute | solution.py:280
  25.7 7.0 %collective-permute-start.3 = (bf16[1,48,768]{2,1,0:T(8,128)(2,1)S(1)}, bf16[1,48,768]{2,1,0:T(8,128)(2,1)S(1)}, u32[]{:S(2)}, u32[]{:S(2)}) collective-permute-start(bf16[1,48,768]{2,1,0:T(8,128)(2,1)S(1)} %get-tuple-element.10), channel_id=1, source_target_pairs={{8,0},{16,8},{24,16},{9,1},{17,9},{25,17},{10,2},{18,10},{26,18},{... | collective-permute-start | bytes 221192 | tf_op jit(solution)/shard_map/ppermute | solution.py:281
  34.0 28.0 %copy-start = (bf16[24,24,384]{2,1,0:T(8,128)(2,1)S(1)}, bf16[24,24,384]{2,1,0:T(8,128)(2,1)}, u32[]{:S(2)}) copy-start(bf16[24,24,384]{2,1,0:T(8,128)(2,1)} %param.7) | copy-start | bytes 1327108
  61.2 142.5 %all-reduce.6.cloned.1.call-start = ((), (), s32[]{:S(2)}) async-start(), calls=%async_computation.2 | async-start | bytes 3538944 | tf_op jit(solution)/shard_map/psum | solution.py:338
Sparse Core Ops, SparseCore 0:
  61.3 31.8 all-gather.1
Sparse Core Ops, SparseCore 1:
  67.6 136.1 all-reduce.5

commit v2 on v1

--- a/solution.py
+++ b/solution.py
@@ -15,6 +15,8 @@
 S = 8
 LB = 32
 MSTEP = 8
+DEGREES = 128
+PITCH = LB + 1
 VMEM_BYTES = 56 * 1024 * 1024
 
 
@@ -49,16 +51,16 @@
     return 0.5 * jnp.log((2.0 * degrees + 1.0) / (4.0 * math.pi)) + 0.5 * prefix
 
 
-def legendre_kernel(first_ref, cos_ref, seed_ref, table_ref, prev_ref, early_ref, scale_ref, *stage_refs):
-    step = pl.program_id(0)
-    rows, width = seed_ref.shape
+def legendre_kernel(start_block, first_ref, cos_ref, prev_in, early_in, scale_in, table_ref, prev_ref, early_ref, scale_ref, *stage_refs):
+    step = start_block + pl.program_id(0)
+    rows, width = scale_in.shape
     first = first_ref[0]
 
-    @pl.when(step == 0)
+    @pl.when(pl.program_id(0) == 0)
     def _():
-        prev_ref[...] = jnp.zeros_like(prev_ref)
-        early_ref[...] = jnp.zeros_like(early_ref)
-        scale_ref[...] = seed_ref[...]
+        prev_ref[...] = prev_in[...]
+        early_ref[...] = early_in[...]
+        scale_ref[...] = scale_in[...]
 
     chunk = 48 if rows % 48 == 0 else 8
     cosines = cos_ref[...]
@@ -90,7 +92,7 @@
             )
             level = fresh * factor
             for tile, stage_ref in enumerate(stage_refs):
-                stage_ref[pl.ds(begin * LB + inner, chunk, stride=LB), :] = level[:, tile * 128 : tile * 128 + 128]
+                stage_ref[pl.ds(begin * PITCH + inner, chunk, stride=PITCH), :] = level[:, tile * 128 : tile * 128 + 128]
             earlier, previous = previous, fresh
         biggest = jnp.maximum(jnp.abs(previous), jnp.abs(earlier))
         divisor = jnp.where(biggest > 0.0, biggest, 1.0)
@@ -98,50 +100,63 @@
         early_ref[span, :] = earlier / divisor
         scale_ref[span, :] = scales + jnp.log(divisor)
     for tile, stage_ref in enumerate(stage_refs):
-        staged = stage_ref[...].reshape(rows, LB, 128).astype(jnp.bfloat16)
-        table_ref[:, :, tile * 128 : tile * 128 + 128] = staged
-
-
-def legendre_table(first_order, cosines, logscale):
+        for row in range(rows):
+            staged = stage_ref[row * PITCH : row * PITCH + LB, :]
+            table_ref[row, :, tile * 128 : tile * 128 + 128] = staged.astype(jnp.bfloat16)
+
+
+def legendre_state(cosines, logscale):
     rows, lat_total = logscale.shape
-    width = round_up(lat_total, 128)
-    spare = width - lat_total
+    spare = round_up(lat_total, 128) - lat_total
     cos_pad = jnp.pad(cosines, (0, spare))[None, :]
     seed_pad = jnp.pad(logscale, ((0, 0), (0, spare)), constant_values=-1.0e4)
-    stage_rows = rows * LB
-    return pl.pallas_call(
-        legendre_kernel,
-        grid=(L // LB,),
+    nothing = jnp.zeros_like(seed_pad)
+    return cos_pad, (nothing, nothing, seed_pad)
+
+
+def legendre_table(first_order, cos_pad, state, start_block):
+    rows, width = state[0].shape
+    plain = pl.BlockSpec((rows, width), lambda i: (0, 0))
+    held = jax.ShapeDtypeStruct((rows, width), jnp.float32)
+    outs = pl.pallas_call(
+        functools.partial(legendre_kernel, start_block),
+        grid=(DEGREES // LB,),
         in_specs=[
             pl.BlockSpec(memory_space=pltpu.SMEM),
             pl.BlockSpec((1, width), lambda i: (0, 0)),
-            pl.BlockSpec((rows, width), lambda i: (0, 0)),
+            plain,
+            plain,
+            plain,
         ],
-        out_specs=pl.BlockSpec((rows, LB, width), lambda i: (0, i, 0)),
-        out_shape=jax.ShapeDtypeStruct((rows, L, width), jnp.bfloat16),
-        scratch_shapes=[pltpu.VMEM((rows, width), jnp.float32)] * 3
-        + [pltpu.VMEM((stage_rows, 128), jnp.float32)] * (width // 128),
+        out_specs=[pl.BlockSpec((rows, LB, width), lambda i: (0, i, 0)), plain, plain, plain],
+        out_shape=[jax.ShapeDtypeStruct((rows, DEGREES, width), jnp.bfloat16), held, held, held],
+        scratch_shapes=[pltpu.VMEM((rows * PITCH, 128), jnp.float32)] * (width // 128),
         compiler_params=pltpu.CompilerParams(vmem_limit_bytes=VMEM_BYTES),
         cost_estimate=pl.CostEstimate(
-            flops=rows * L * width * 10, bytes_accessed=rows * L * width * 2, transcendentals=0
+            flops=rows * DEGREES * width * 5000, bytes_accessed=rows * DEGREES * width * 2, transcendentals=0
         ),
         name="legendre_table",
-    )(first_order.reshape(1), cos_pad, seed_pad)
-
-
-def synthesis_kernel(lon_total, lat_total, dft_ref, grid_ref, table_ref, out_ref, modes_ref):
+    )(first_order.reshape(1), cos_pad, *state)
+    return outs[0], tuple(outs[1:])
+
+
+def synthesis_kernel(lon_total, lat_total, band_count, *refs):
     step = pl.program_id(0)
-    bands, _, packed = grid_ref.shape
+    band_ref, dft_ref = refs[:2]
+    grid_refs = refs[2 : 2 + band_count]
+    table_refs = refs[2 + band_count : -2]
+    out_ref, modes_ref = refs[-2:]
+    packed = grid_refs[0].shape[1]
     rows = dft_ref.shape[0] // 2
     chans = out_ref.shape[2]
     lat_dev = packed // chans
-    width = table_ref.shape[2]
+    width = table_refs[0].shape[2]
 
     @pl.when(step == 0)
     def _():
-        @pl.loop(0, bands)
-        def _(band):
-            modes = jnp.dot(dft_ref[...], grid_ref[band], preferred_element_type=jnp.float32)
+        for source, grid_ref in enumerate(grid_refs):
+            band = band_ref[source]
+            modes = jnp.dot(dft_ref[...], grid_ref[...], preferred_element_type=jnp.float32)
             modes = (modes * (1.0 / math.sqrt(lon_total))).astype(jnp.bfloat16).astype(jnp.float32)
             for lat in range(lat_dev):
                 dest = pl.ds(pl.multiple_of((band * lat_dev + lat) * rows, 8), rows)
@@ -157,31 +172,36 @@
             picked = jnp.concatenate([picked, spare], axis=0)
         turned = picked.T[0 : 2 * chans].astype(jnp.bfloat16)
         product = lax.dot_general(
-            turned, table_ref[inner], (((1,), (1,)), ((), ())), preferred_element_type=jnp.float32
+            turned,
+            jnp.concatenate([table_ref[inner] for table_ref in table_refs], axis=0),
+            (((1,), (1,)), ((), ())),
+            preferred_element_type=jnp.float32,
         )
         product = product * leg_scale
         out_ref[0, inner] = product[0:chans]
         out_ref[1, inner] = product[chans : 2 * chans]
 
 
-def synthesis(dft_rows, gathered, table, chans, lat_total, lon_total):
-    rows = table.shape[0]
-    width = table.shape[2]
+def synthesis(bands, dft_rows, columns, tables, chans, lat_total, lon_total):
+    rows, _, width = tables[0].shape
     whole = lambda i: (0, 0)
+    table_spec = pl.BlockSpec((MSTEP, DEGREES, width), lambda i: (i, 0, 0))
+    grid_spec = pl.BlockSpec(columns[0].shape, whole, pipeline_mode=pl.Buffered(1))
     return pl.pallas_call(
-        functools.partial(synthesis_kernel, lon_total, lat_total),
+        functools.partial(synthesis_kernel, lon_total, lat_total, len(columns)),
         grid=(rows // MSTEP,),
-        in_specs=[
-            pl.BlockSpec(dft_rows.shape, whole),
-            pl.BlockSpec(gathered.shape, lambda i: (0, 0, 0), pipeline_mode=pl.Buffered(1)),
-            pl.BlockSpec((MSTEP, L, width), lambda i: (i, 0, 0)),
-        ],
+        in_specs=[pl.BlockSpec(memory_space=pltpu.SMEM), pl.BlockSpec(dft_rows.shape, whole)]
+        + [grid_spec] * len(columns)
+        + [table_spec] * len(tables),
         out_specs=pl.BlockSpec((2, MSTEP, chans, L), lambda i: (0, i, 0, 0)),
         out_shape=jax.ShapeDtypeStruct((2, rows, chans, L), jnp.float32),
         scratch_shapes=[pltpu.VMEM((lat_total * rows, 128), jnp.float32)],
         compiler_params=pltpu.CompilerParams(vmem_limit_bytes=VMEM_BYTES),
+        cost_estimate=pl.CostEstimate(
+            flops=20_000_000_000, bytes_accessed=8 * rows * chans * L, transcendentals=0
+        ),
         name="dft_synthesis",
-    )(dft_rows, gathered, table)
+    )(bands, dft_rows, *columns, *tables)
 
 
 def grid_kernel(
@@ -282,6 +302,22 @@
     return before, after
 
 
+def partner(position, turn, count):
+    if count & (count - 1) == 0:
+        return position ^ turn
+    return (position + turn) % count
+
+
+def source_of(position, turn, count):
+    if count & (count - 1) == 0:
+        return position ^ turn
+    return (position + count - turn) % count
+
+
+def swap_with(value, turn, count):
+    return lax.ppermute(value, "lat", [(i, partner(i, turn, count)) for i in range(count)])
+
+
 def spread(values, ext_width):
     return jnp.repeat(values, ext_width, axis=-1)
 
@@ -299,10 +335,26 @@
     ext_width = round_up(lon_dev + 2 * R, 16)
 
     both = jnp.concatenate([field, cotangent], axis=2)
+    cosines, log_sines = colatitudes(total_lat)
+    orders = lat_pos * block_rows + lax.broadcasted_iota(jnp.int32, (block_rows,), 0)
+    own_logs = lax.dynamic_slice_in_dim(seed_logs(M), lat_pos * block_rows, block_rows, 0)
+    logscale = own_logs[:, None] + orders.astype(jnp.float32)[:, None] * log_sines[None, :]
+    cos_pad, state = legendre_state(cosines, logscale)
+    first_order = (lat_pos * block_rows).astype(jnp.int32)
+    tables = []
+
+    def next_table(current):
+        table, later = legendre_table(first_order, cos_pad, current, len(tables) * DEGREES // LB)
+        tables.append(table)
+        return later
+
     before, after = swap_edges(both, "lon", 1, R, True)
+    state = next_table(state)
+    before, after, state = lax.optimization_barrier((before, after, state))
     spare = jnp.zeros((lat_dev, ext_width - lon_dev - 2 * R, 2 * channels), jnp.bfloat16)
     wide = jnp.concatenate([before, both, after, spare], axis=1)
     above, below = swap_edges(wide, "lat", 0, 1, False)
+    state = next_table(state)
     ext = jnp.concatenate([above, wide, below], axis=0).reshape((lat_dev + 2) * ext_width, 2 * channels)
 
     live = live_taps(taps, counts).astype(jnp.float32)
@@ -320,22 +372,48 @@
         ext, cot_flat, mix_weight, tap_own, shift_own, tap_back, shift_back, lon_count
     )
 
-    cosines, log_sines = colatitudes(total_lat)
-    orders = lat_pos * block_rows + lax.broadcasted_iota(jnp.int32, (block_rows,), 0)
-    own_logs = lax.dynamic_slice_in_dim(seed_logs(M), lat_pos * block_rows, block_rows, 0)
-    logscale = own_logs[:, None] + orders.astype(jnp.float32)[:, None] * log_sines[None, :]
-    table = legendre_table((lat_pos * block_rows).astype(jnp.int32), cosines, logscale)
     dft_rows = dft_table(total_lon, orders).reshape(2 * block_rows, total_lon)
-
-    columns = lax.all_to_all(packed, "lon", split_axis=0, concat_axis=0, tiled=True)
-    columns = columns.reshape(total_lon, lat_dev * chans)
-    gathered = lax.all_gather(columns, "lat", axis=0, tiled=False)
-    grad_spectra = synthesis(dft_rows, gathered, table, chans, total_lat, total_lon)
 
     mix_local = lax.dot_general(
         response, cot_flat, (((0,), (0,)), ((), ())), preferred_element_type=jnp.float32
     ) * (1.0 / math.sqrt(total_lat * total_lon))
-    grad_mix = lax.psum(mix_local, ("lat", "lon")).reshape(K, channels, channels)
+    mix_rows = K * channels
+    split_sum = mix_rows % (lat_count * lon_count) == 0
+    if split_sum:
+        mix_sent = mix_local.astype(jnp.bfloat16).reshape(lat_count, mix_rows // lat_count, channels)
+        packed, mix_sent, mix_local = lax.optimization_barrier((packed, mix_sent, mix_local))
+        lat_share = lax.dynamic_index_in_dim(
+            mix_local.reshape(lat_count, mix_rows // lat_count, channels), lat_pos, 0, keepdims=False
+        )
+        arrived = []
+        for turn in range(1, lat_count):
+            piece = lax.dynamic_index_in_dim(mix_sent, partner(lat_pos, turn, lat_count), 0, keepdims=False)
+            arrived.append(swap_with(piece, turn, lat_count))
+
+    columns = lax.all_to_all(packed, "lon", split_axis=0, concat_axis=0, tiled=True)
+    columns, state = lax.optimization_barrier((columns, state))
+    while len(tables) * DEGREES < L:
+        state = next_table(state)
+    columns = columns.reshape(total_lon, lat_dev * chans)
+    gathered, bands = [columns], [lat_pos]
+    for turn in range(1, lat_count):
+        gathered.append(swap_with(columns, turn, lat_count))
+        bands.append(source_of(lat_pos, turn, lat_count))
+    grad_spectra = synthesis(
+        jnp.stack(bands).astype(jnp.int32), dft_rows, gathered, tables, chans, total_lat, total_lon
+    )
+
+    if split_sum:
+        for piece in arrived:
+            lat_share = lat_share + piece.astype(jnp.float32)
+        lon_rows = mix_rows // (lat_count * lon_count)
+        lon_sent = lat_share.astype(jnp.bfloat16).reshape(lon_count, lon_rows, channels)
+        lon_got = lax.all_to_all(lon_sent, "lon", split_axis=0, concat_axis=0, tiled=True)
+        mix_share = jnp.sum(lon_got.astype(jnp.float32), axis=0).astype(jnp.bfloat16)
+        grad_mix = lax.all_gather(mix_share, ("lat", "lon"), axis=0, tiled=False).astype(jnp.float32)
+    else:
+        grad_mix = lax.psum(mix_local, ("lat", "lon"))
+    grad_mix = grad_mix.reshape(K, channels, channels)
     return (grad_field.reshape(lat_dev, lon_dev, channels), grad_spectra, grad_mix)
 
 

time: 215 us -> 172 us (0.80)
  waiting for transfers between devices: 98.6 us -> 30.4 us
  blocking collectives: 17.7 us -> 45.5 us
  starting transfers between devices: 9.76 us -> 26.4 us
  between operations: 15.6 us -> 0.82 us
  Pallas kernels: 50.7 us -> 45.1 us
  other arithmetic: 3.42 us -> 5.65 us
    psum x1 -> x0, waiting for transfers between devices: 92.7 us -> none  [on_device(): lax.psum(mix_local, ('lat', 'lon')).reshape(K, channels, channels)]
    all_gather x0 -> x1, blocking collectives: none -> 45.5 us  [on_device(): lax.all_gather(mix_share, ('lat', 'lon'), axis=0, tiled=False)]
    ppermute x0 -> x6, waiting for transfers between devices: none -> 22.7 us  [swap_with(): lax.ppermute(value, 'lat', [(i, partner(i, turn, count)) for i in range(c...]
    all_to_all x1 -> x0, blocking collectives: 17.7 us -> none  [on_device(): lax.all_to_all(packed, 'lon', split_axis=0, concat_axis=0, tiled=True)]
    all_to_all x0 -> x2, starting transfers between devices: none -> 8.62 us  [the longest x1 5.15 us: on_device(): lax.all_to_all(lon_sent, 'lon', split_axis=0, concat_axis=0, tiled=True)]
    ppermute x0 -> x6, starting transfers between devices: none -> 7.97 us  [swap_with(): lax.ppermute(value, 'lat', [(i, partner(i, turn, count)) for i in range(c...]
    all_to_all x0 -> x2, waiting for transfers between devices: none -> 7.6 us  [the longest x1 7.6 us: on_device(): lax.all_to_all(lon_sent, 'lon', split_axis=0, concat_axis=0, tiled=True)]
    pallas_call x2 -> x4, Pallas kernels: 41.3 us -> 35.7 us  [the longest x3 18.6 us: legendre_table(): pl.pallas_call(functools.partial(legendre_kernel, start_block), grid=(DEG...]
  transfers between devices with their start and end apart: 6 -> 12, of which waited for: 3 -> 7; matrix products, arithmetic and copies ran while one was open for 7% -> 8% of each run, Pallas kernels for 19% -> 11%
where the time goes in v2:
time: 172 us; the launch traced here: 171 us
  blocking collectives  45.5 us (26%)
  Pallas kernels  45.1 us (26%)
  waiting for transfers between devices  30.4 us (18%)
  starting transfers between devices  26.4 us (15%)
  local copies, waits for them, and re-layouts  14.5 us (8%)
  other arithmetic  5.65 us (3%)
  matrix products  2.38 us (1%)
    all_gather x1, blocking collectives, on_device(): lax.all_gather(mix_share, ('lat', 'lon'), axis=0, tiled=False)  45.5 us
    ppermute x6, waiting for transfers between devices, swap_with(): lax.ppermute(value, 'lat', [(i, partner(i, turn, count)) for i in range(c...  22.7 us
    pallas_call x3, Pallas kernels, legendre_table(): pl.pallas_call(functools.partial(legendre_kernel, start_block), grid=(DEG...  18.6 us
    pallas_call x1, Pallas kernels, synthesis(): pl.pallas_call(functools.partial(synthesis_kernel, lon_total, lat_total,...  17.1 us
    pallas_call x1, Pallas kernels, grid_part(): pl.pallas_call(functools.partial(grid_kernel, lon_count), in_specs=[pl.Bl...  9.4 us
    ppermute x6, starting transfers between devices, swap_with(): lax.ppermute(value, 'lat', [(i, partner(i, turn, count)) for i in range(c...  7.97 us
    all_to_all x1, waiting for transfers between devices, on_device(): lax.all_to_all(lon_sent, 'lon', split_axis=0, concat_axis=0, tiled=True)  7.6 us
    ppermute x2, starting transfers between devices, swap_edges(): lax.ppermute(lax.slice_in_dim(shard, 0, width, axis=dim), axis, down)  5.82 us
  transfers between devices with their start and end apart: 12, of which 7 were waited for; matrix products, arithmetic and copies ran while one was open for 8% of the time, Pallas kernels for 11%

profile of v2, /device:TPU:0, one launch (start us, length us, event | category | flops | bytes accessed | tf_op | source)
XLA Modules:
  0.0 170.7 jit_solution(12091455406286285059)
XLA Ops:
  0.7 1.1 constant_dynamic-update-slice_fusion.1
  1.7 1.1 constant_dynamic-update-slice_fusion
  2.9 4.5 %collective-permute-start.1 = (bf16[24,8,768]{2,1,0:T(8,128)(2,1)S(1)}, bf16[24,8,768]{2,1,0:T(8,128)(2,1)S(1)}, u32[]{:S(2)}, u32[]{:S(2)}) collective-permute-start(bf16[24,8,768]{2,1,0:T(8,128)(2,1)S(1)} %get-tuple-element.56), channel_id=1, source_target_pairs={{1,0},{2,1},{3,2},{4,3},{5,4},{6,5},{7,6},{0,7},{9,8},{10,9},{11,1... | collective-permute-start | bytes 884744 | tf_op jit(solution)/shard_map/ppermute | solution.py:301
  7.4 0.0 collective-permute-start
  7.5 0.5 pad_bitcast_fusion.cos_ref
  8.0 0.3 reduce-window.9
  8.3 0.1 slice.48
  8.5 0.1 slice_reduce_fusion
  8.6 0.1 add_bitcast_fusion
  8.7 0.1 dynamic-slice_convert_fusion
  8.8 0.1 slice_bitcast_fusion.3
  8.8 0.1 dynamic-slice_bitcast_fusion.3
  8.9 0.1 copy.22
  9.1 0.1 fusion.14
  9.1 0.1 dynamic_slice.23
  9.2 0.1 multiply_add_fusion
  9.3 0.6 pad.20.scale_in
  9.9 0.1 fusion.11
  10.0 0.6 broadcast_in_dim.32.prev_in.early_in
  10.7 6.2 %legendre_table.3 = (bf16[96,128,128]{2,1,0:T(8,128)(2,1)}, f32[96,128]{1,0:T(8,128)}, f32[96,128]{1,0:T(8,128)}, f32[96,128]{1,0:T(8,128)}) custom-call(s32[1]{0:T(128)} %bitcast.first_ref, f32[1,128]{1,0:T(1,128)} %pad_bitcast_fusion.cos_ref, f32[96,128]{1,0:T(8,128)} %broadcast_in_dim.32.prev_in.early_in, f32[96,128]{1,0:T(8,128)} %broadcast_in_dim.32.prev_in.early_in, ...), custom_call_target="tpu_custom_call" | custom-call | flops 7864320000 | bytes 3145728 | tf_op jit(solution)/shard_map/legendre_table/pallas_call | solution.py:121
  16.9 0.1 copy.26
  17.0 0.1 slice_bitcast_fusion
  17.1 0.7 pad_maximum_fusion.5
  17.8 4.0 %collective-permute-start.2 = (bf16[1,48,768]{2,1,0:T(8,128)(2,1)}, bf16[1,48,768]{2,1,0:T(8,128)(2,1)}, u32[]{:S(2)}, u32[]{:S(2)}) collective-permute-start(bf16[1,48,768]{2,1,0:T(8,128)(2,1)} %get-tuple-element.51), channel_id=1, source_target_pairs={{0,8},{8,16},{16,24},{1,9},{9,17},{17,25},{2,10},{10,18},{18,26},{... | collective-permute-start | bytes 221192 | tf_op jit(solution)/shard_map/ppermute | solution.py:300
  21.8 1.3 collective-permute-start.3
  23.1 0.2 copy.25
  23.4 0.2 copy.21
  23.6 0.3 broadcast_in_dim.38
  23.9 0.9 reshape.203.shift_back_ref
  24.8 0.3 broadcast_in_dim.36
  25.0 0.9 reshape.202.shift_own_ref
  25.9 0.7 broadcast_in_dim.35
  26.7 1.3 reshape_reshape.6.tap_own_ref
  27.9 0.7 broadcast_in_dim.37
  28.7 1.3 reshape_reshape.7.tap_back_ref
  29.9 2.1 %pad_maximum_fusion = bf16[26,48,768]{2,1,0:T(8,128)(2,1)} fusion(bf16[1,48,768]{2,1,0:T(8,128)(2,1)} %collective-permute-done.3, bf16[24,8,768]{2,1,0:T(8,128)(2,1)S(1)} %broadcast_in_dim.33, bf16[24,8,768]{2,1,0:T(8,128)(2,1)S(1)} %collective-permute-done.1, bf16[24,24,768]{2,1,0:T(8,128)(2,1)S(1)} %constant_dynamic-update-slice_fusion, ...), kind=kLoop, calls=%fused_computation.1 | loop fusion | flops 11501568 | bytes 3833856 | tf_op jit(solution)/shard_map/concatenate | solution.py:358
  32.1 9.4 %grid_part.1 = (bf16[576,1152]{1,0:T(8,128)(2,1)}, bf16[576,384]{1,0:T(8,128)(2,1)}, bf16[8,24,1152]{2,1,0:T(8,128)(2,1)}) custom-call(bf16[1248,768]{1,0:T(8,128)(2,1)} %bitcast.54, bf16[576,384]{1,0:T(8,128)(2,1)} %bitcast.55, bf16[3,384,384]{2,1,0:T(8,128)(2,1)} %weight_ref.1, f32[24,24,144]{2,1,0:T(8,128)} %reshape_reshape.6.tap_own_ref, ...), custom_call_target="tpu_custom_call" | custom-call | tf_op jit(solution)/shard_map/grid_part/pallas_call | solution.py:277
  41.5 2.4 %fusion.19 = (bf16[1152,384]{1,0:T(8,128)(2,1)S(1)}, f32[1152,384]{1,0:T(8,128)S(1)}) fusion(bf16[576,1152]{1,0:T(8,128)(2,1)} %get-tuple-element.34, bf16[576,384]{1,0:T(8,128)(2,1)S(1)} %bitcast.56), kind=kOutput, calls=%fused_computation.59 | convolution fusion | flops 510492672 | bytes 4423680 | tf_op jit(solution)/shard_map/dot_general | solution.py:377
  43.9 0.1 dynamic-slice_bitcast_fusion.2
  44.0 2.7 %collective-permute-start.7 = (bf16[288,384]{1,0:T(8,128)(2,1)S(1)}, bf16[288,384]{1,0:T(8,128)(2,1)S(1)}, u32[]{:S(2)}, u32[]{:S(2)}) collective-permute-start(bf16[288,384]{1,0:T(8,128)(2,1)S(1)} %get-tuple-element.53), channel_id=1, source_target_pairs={{0,8},{8,0},{16,24},{24,16},{1,9},{9,1},{17,25},{25,17},{2,10},{10... | collective-permute-start | bytes 663560 | tf_op jit(solution)/shard_map/ppermute | solution.py:318
  46.7 1.8 %collective-permute-start.9 = (bf16[288,384]{1,0:T(8,128)(2,1)S(1)}, bf16[288,384]{1,0:T(8,128)(2,1)S(1)}, u32[]{:S(2)}, u32[]{:S(2)}) collective-permute-start(bf16[288,384]{1,0:T(8,128)(2,1)S(1)} %get-tuple-element.54), channel_id=1, source_target_pairs={{0,24},{8,16},{16,8},{24,0},{1,25},{9,17},{17,9},{25,1},{2,26},{10... | collective-permute-start | bytes 663560 | tf_op jit(solution)/shard_map/ppermute | solution.py:318
  48.5 0.0 collective-permute-start.8
  48.5 4.4 %collective-permute-done.7 = bf16[288,384]{1,0:T(8,128)(2,1)S(1)} collective-permute-done((bf16[288,384]{1,0:T(8,128)(2,1)S(1)}, bf16[288,384]{1,0:T(8,128)(2,1)S(1)}, u32[]{:S(2)}, u32[]{:S(2)}) %collective-permute-start.7) | collective-permute-done | bytes 221216 | tf_op jit(solution)/shard_map/ppermute | solution.py:318
  52.8 3.9 %collective-permute-done.9 = bf16[288,384]{1,0:T(8,128)(2,1)S(1)} collective-permute-done((bf16[288,384]{1,0:T(8,128)(2,1)S(1)}, bf16[288,384]{1,0:T(8,128)(2,1)S(1)}, u32[]{:S(2)}, u32[]{:S(2)}) %collective-permute-start.9) | collective-permute-done | bytes 221216 | tf_op jit(solution)/shard_map/ppermute | solution.py:318
  56.8 1.4 collective-permute-done.8
  58.1 0.1 fusion.2
  58.2 0.7 reshape.208
  59.0 5.2 %all-to-all-start.1 = ((bf16[8,36,384]{2,1,0:T(8,128)(2,1)}), bf16[8,36,384]{2,1,0:T(8,128)(2,1)S(1)}, u32[]{:S(2)}, u32[]{:S(2)}) async-start(bf16[8,36,384]{2,1,0:T(8,128)(2,1)} %reshape.208), calls=%async_computation.1 | async-start | bytes 491520 | tf_op jit(solution)/shard_map/all_to_all | solution.py:411
  64.1 0.6 pad_add_fusion.1.refs_0_
  64.8 0.5 cosine_convert_fusion
  65.3 0.7 pad_maximum_fusion.1
  65.9 7.6 %all-to-all-done.1 = bf16[8,36,384]{2,1,0:T(8,128)(2,1)S(1)} async-done(((bf16[8,36,384]{2,1,0:T(8,128)(2,1)}), bf16[8,36,384]{2,1,0:T(8,128)(2,1)S(1)}, u32[]{:S(2)}, u32[]{:S(2)}) %all-to-all-start.1) | async-done | bytes 221216 | tf_op jit(solution)/shard_map/all_to_all | solution.py:411
  73.5 3.5 %all-to-all-start = ((bf16[8,24,1152]{2,1,0:T(8,128)(2,1)}), bf16[8,24,1152]{2,1,0:T(8,128)(2,1)S(1)}, u32[]{:S(2)}, u32[]{:S(2)}) async-start(bf16[8,24,1152]{2,1,0:T(8,128)(2,1)} %get-tuple-element.35), calls=%async_computation | async-start | bytes 884736 | tf_op jit(solution)/shard_map/all_to_all | solution.py:393
  77.0 6.2 %legendre_table.4 = (bf16[96,128,128]{2,1,0:T(8,128)(2,1)}, f32[96,128]{1,0:T(8,128)}, f32[96,128]{1,0:T(8,128)}, f32[96,128]{1,0:T(8,128)}) custom-call(s32[1]{0:T(128)} %bitcast.first_ref, f32[1,128]{1,0:T(1,128)} %pad_bitcast_fusion.cos_ref, f32[96,128]{1,0:T(8,128)} %get-tuple-element.36.prev_in, f32[96,128]{1,0:T(8,128)} %get-tuple-element.37.early_in, ...), custom_call_target="tpu_custom_call" | custom-call | flops 7864320000 | bytes 3145728 | tf_op jit(solution)/shard_map/legendre_table/pallas_call | solution.py:121
  83.2 45.5 %all-gather.1 = bf16[32,36,384]{2,1,0:T(8,128)(2,1)S(1)} all-gather(bf16[1,36,384]{2,1,0:T(8,128)(2,1)S(1)} %bitcast.63), channel_id=2, replica_groups=mesh['lat'=4,'lon'=8] {'lat','lon'}, dimensions={0}, use_global_device_ids=true | all-gather | bytes 912384 | tf_op jit(solution)/shard_map/all_gather | solution.py:413
  128.7 1.4 reshape.212
  130.1 1.5 collective-permute-start.5
  131.5 2.0 %collective-permute-start.4 = (bf16[192,1152]{1,0:T(8,128)(2,1)S(1)}, bf16[192,1152]{1,0:T(8,128)(2,1)S(1)}, u32[]{:S(2)}, u32[]{:S(2)}) collective-permute-start(bf16[192,1152]{1,0:T(8,128)(2,1)S(1)} %bitcast.61), channel_id=1, source_target_pairs={{0,8},{8,0},{16,24},{24,16},{1,9},{9,1},{17,25},{25,17},{2,10},{10... | collective-permute-start | bytes 1327112 | tf_op jit(solution)/shard_map/ppermute | solution.py:318
  133.6 6.2 %legendre_table.5 = (bf16[96,128,128]{2,1,0:T(8,128)(2,1)}, f32[96,128]{1,0:T(8,128)}, f32[96,128]{1,0:T(8,128)}, f32[96,128]{1,0:T(8,128)}) custom-call(s32[1]{0:T(128)} %bitcast.first_ref, f32[1,128]{1,0:T(1,128)} %pad_bitcast_fusion.cos_ref, f32[96,128]{1,0:T(8,128)} %get-tuple-element.45.prev_in, f32[96,128]{1,0:T(8,128)} %get-tuple-element.46.early_in, ...), custom_call_target="tpu_custom_call" | custom-call | flops 7864320000 | bytes 3145728 | tf_op jit(solution)/shard_map/legendre_table/pallas_call | solution.py:121
  139.8 4.2 %collective-permute-done.6.refs_5_ = bf16[192,1152]{1,0:T(8,128)(2,1)S(1)} collective-permute-done((bf16[192,1152]{1,0:T(8,128)(2,1)S(1)}, bf16[192,1152]{1,0:T(8,128)(2,1)S(1)}, u32[]{:S(2)}, u32[]{:S(2)}) %collective-permute-start.6) | collective-permute-done | bytes 442400 | tf_op jit(solution)/shard_map/ppermute | solution.py:318
  144.0 8.0 %collective-permute-done.5.refs_4_ = bf16[192,1152]{1,0:T(8,128)(2,1)S(1)} collective-permute-done((bf16[192,1152]{1,0:T(8,128)(2,1)S(1)}, bf16[192,1152]{1,0:T(8,128)(2,1)S(1)}, u32[]{:S(2)}, u32[]{:S(2)}) %collective-permute-start.5) | collective-permute-done | bytes 442400 | tf_op jit(solution)/shard_map/ppermute | solution.py:318
  152.0 0.8 collective-permute-done.4.refs_3_
  152.9 0.8 copy-done.7
  153.6 17.1 %dft_synthesis.1 = f32[2,96,48,384]{3,2,1,0:T(8,128)} custom-call(s32[4]{0:T(128)} %pad_add_fusion.1.refs_0_, bf16[192,192]{1,0:T(8,128)(2,1)} %bitcast.64, bf16[192,1152]{1,0:T(8,128)(2,1)} %bitcast.62, bf16[192,1152]{1,0:T(8,128)(2,1)} %copy-done.7, bf16[192,1152]{1,0:T(8,128)(2,1)} %copy-done.6, bf16[192,1152]{1,0:T(8,128)(2,1)} %copy-done.5, ...), custom_call_target="tpu_custom_call" | custom-call | flops 20000000000 | bytes 14155776 | tf_op jit(solution)/shard_map/dft_synthesis/pallas_call | solution.py:190
  (33 shorter events, 0.3 us)
Async XLA Ops:
  0.6 8.0 %copy-start.4 = (s32[96]{0:T(128)S(1)}, s32[96]{0:T(128)}, u32[]{:S(2)}) copy-start(s32[96]{0:T(128)} %param.11) | copy-start | bytes 1156
  0.6 8.0 %copy-start.3 = (f32[96,3,3,8]{0,3,2,1:T(8,128)S(1)}, f32[96,3,3,8]{0,3,2,1:T(8,128)}, u32[]{:S(2)}) copy-start(f32[96,3,3,8]{0,3,2,1:T(8,128)} %param.9) | copy-start | bytes 82948
  0.7 8.2 %copy-start.2 = (s32[96,3,8]{0,2,1:T(8,128)S(1)}, s32[96,3,8]{0,2,1:T(8,128)}, u32[]{:S(2)}) copy-start(s32[96,3,8]{0,2,1:T(8,128)} %param.10) | copy-start | bytes 27652
  2.9 14.2 %collective-permute-start.1 = (bf16[24,8,768]{2,1,0:T(8,128)(2,1)S(1)}, bf16[24,8,768]{2,1,0:T(8,128)(2,1)S(1)}, u32[]{:S(2)}, u32[]{:S(2)}) collective-permute-start(bf16[24,8,768]{2,1,0:T(8,128)(2,1)S(1)} %get-tuple-element.56), channel_id=1, source_target_pairs={{1,0},{2,1},{3,2},{4,3},{5,4},{6,5},{7,6},{0,7},{9,8},{10,9},{11,1... | collective-permute-start | bytes 884744 | tf_op jit(solution)/shard_map/ppermute | solution.py:301
  7.4 9.7 %collective-permute-start = (bf16[24,8,768]{2,1,0:T(8,128)(2,1)S(1)}, bf16[24,8,768]{2,1,0:T(8,128)(2,1)S(1)}, u32[]{:S(2)}, u32[]{:S(2)}) collective-permute-start(bf16[24,8,768]{2,1,0:T(8,128)(2,1)S(1)} %get-tuple-element.57), channel_id=1, source_target_pairs={{0,1},{1,2},{2,3},{3,4},{4,5},{5,6},{6,7},{7,0},{8,9},{9,10},{10,1... | collective-permute-start | bytes 884744 | tf_op jit(solution)/shard_map/ppermute | solution.py:300
  17.8 12.1 %collective-permute-start.2 = (bf16[1,48,768]{2,1,0:T(8,128)(2,1)}, bf16[1,48,768]{2,1,0:T(8,128)(2,1)}, u32[]{:S(2)}, u32[]{:S(2)}) collective-permute-start(bf16[1,48,768]{2,1,0:T(8,128)(2,1)} %get-tuple-element.51), channel_id=1, source_target_pairs={{0,8},{8,16},{16,24},{1,9},{9,17},{17,25},{2,10},{10,18},{18,26},{... | collective-permute-start | bytes 221192 | tf_op jit(solution)/shard_map/ppermute | solution.py:300
  21.8 8.1 %collective-permute-start.3 = (bf16[1,48,768]{2,1,0:T(8,128)(2,1)}, bf16[1,48,768]{2,1,0:T(8,128)(2,1)}, u32[]{:S(2)}, u32[]{:S(2)}) collective-permute-start(bf16[1,48,768]{2,1,0:T(8,128)(2,1)} %get-tuple-element.52), channel_id=1, source_target_pairs={{8,0},{16,8},{24,16},{9,1},{17,9},{25,17},{10,2},{18,10},{26,18},{... | collective-permute-start | bytes 221192 | tf_op jit(solution)/shard_map/ppermute | solution.py:301
  32.1 9.4 %copy-start = (bf16[24,24,384]{2,1,0:T(8,128)(2,1)S(1)}, bf16[24,24,384]{2,1,0:T(8,128)(2,1)}, u32[]{:S(2)}) copy-start(bf16[24,24,384]{2,1,0:T(8,128)(2,1)} %param.7) | copy-start | bytes 1327108
  44.0 8.9 %collective-permute-start.7 = (bf16[288,384]{1,0:T(8,128)(2,1)S(1)}, bf16[288,384]{1,0:T(8,128)(2,1)S(1)}, u32[]{:S(2)}, u32[]{:S(2)}) collective-permute-start(bf16[288,384]{1,0:T(8,128)(2,1)S(1)} %get-tuple-element.53), channel_id=1, source_target_pairs={{0,8},{8,0},{16,24},{24,16},{1,9},{9,1},{17,25},{25,17},{2,10},{10... | collective-permute-start | bytes 663560 | tf_op jit(solution)/shard_map/ppermute | solution.py:318
  46.7 10.1 %collective-permute-start.9 = (bf16[288,384]{1,0:T(8,128)(2,1)S(1)}, bf16[288,384]{1,0:T(8,128)(2,1)S(1)}, u32[]{:S(2)}, u32[]{:S(2)}) collective-permute-start(bf16[288,384]{1,0:T(8,128)(2,1)S(1)} %get-tuple-element.54), channel_id=1, source_target_pairs={{0,24},{8,16},{16,8},{24,0},{1,25},{9,17},{17,9},{25,1},{2,26},{10... | collective-permute-start | bytes 663560 | tf_op jit(solution)/shard_map/ppermute | solution.py:318
  48.5 9.7 %collective-permute-start.8 = (bf16[288,384]{1,0:T(8,128)(2,1)S(1)}, bf16[288,384]{1,0:T(8,128)(2,1)S(1)}, u32[]{:S(2)}, u32[]{:S(2)}) collective-permute-start(bf16[288,384]{1,0:T(8,128)(2,1)S(1)} %get-tuple-element.55), channel_id=1, source_target_pairs={{0,16},{8,24},{16,0},{24,8},{1,17},{9,25},{17,1},{25,9},{2,18},{10... | collective-permute-start | bytes 663560 | tf_op jit(solution)/shard_map/ppermute | solution.py:318
  59.0 14.5 %all-to-all-start.1 = ((bf16[8,36,384]{2,1,0:T(8,128)(2,1)}), bf16[8,36,384]{2,1,0:T(8,128)(2,1)S(1)}, u32[]{:S(2)}, u32[]{:S(2)}) async-start(bf16[8,36,384]{2,1,0:T(8,128)(2,1)} %reshape.208), calls=%async_computation.1 | async-start | bytes 491520 | tf_op jit(solution)/shard_map/all_to_all | solution.py:411
  73.5 56.5 %all-to-all-start = ((bf16[8,24,1152]{2,1,0:T(8,128)(2,1)}), bf16[8,24,1152]{2,1,0:T(8,128)(2,1)S(1)}, u32[]{:S(2)}, u32[]{:S(2)}) async-start(bf16[8,24,1152]{2,1,0:T(8,128)(2,1)} %get-tuple-element.35), calls=%async_computation | async-start | bytes 884736 | tf_op jit(solution)/shard_map/all_to_all | solution.py:393
  130.1 9.7 %copy-start.1 = (bf16[8,24,1152]{2,1,0:T(8,128)(2,1)}, bf16[8,24,1152]{2,1,0:T(8,128)(2,1)S(1)}, u32[]{:S(2)}) copy-start(bf16[8,24,1152]{2,1,0:T(8,128)(2,1)S(1)} %all-to-all-done) | copy-start | bytes 1327108
  130.1 13.9 %collective-permute-start.6 = (bf16[192,1152]{1,0:T(8,128)(2,1)S(1)}, bf16[192,1152]{1,0:T(8,128)(2,1)S(1)}, u32[]{:S(2)}, u32[]{:S(2)}) collective-permute-start(bf16[192,1152]{1,0:T(8,128)(2,1)S(1)} %bitcast.59), channel_id=1, source_target_pairs={{0,24},{8,16},{16,8},{24,0},{1,25},{9,17},{17,9},{25,1},{2,26},{10... | collective-permute-start | bytes 1327112 | tf_op jit(solution)/shard_map/ppermute | solution.py:318
  130.1 22.0 %collective-permute-start.5 = (bf16[192,1152]{1,0:T(8,128)(2,1)S(1)}, bf16[192,1152]{1,0:T(8,128)(2,1)S(1)}, u32[]{:S(2)}, u32[]{:S(2)}) collective-permute-start(bf16[192,1152]{1,0:T(8,128)(2,1)S(1)} %bitcast.60), channel_id=1, source_target_pairs={{0,16},{8,24},{16,0},{24,8},{1,17},{9,25},{17,1},{25,9},{2,18},{10... | collective-permute-start | bytes 1327112 | tf_op jit(solution)/shard_map/ppermute | solution.py:318
  131.5 21.3 %collective-permute-start.4 = (bf16[192,1152]{1,0:T(8,128)(2,1)S(1)}, bf16[192,1152]{1,0:T(8,128)(2,1)S(1)}, u32[]{:S(2)}, u32[]{:S(2)}) collective-permute-start(bf16[192,1152]{1,0:T(8,128)(2,1)S(1)} %bitcast.61), channel_id=1, source_target_pairs={{0,8},{8,0},{16,24},{24,16},{1,9},{9,1},{17,25},{25,17},{2,10},{10... | collective-permute-start | bytes 1327112 | tf_op jit(solution)/shard_map/ppermute | solution.py:318
  144.0 8.9 %copy-start.5 = (bf16[192,1152]{1,0:T(8,128)(2,1)}, bf16[192,1152]{1,0:T(8,128)(2,1)S(1)}, u32[]{:S(2)}) copy-start(bf16[192,1152]{1,0:T(8,128)(2,1)S(1)} %collective-permute-done.6.refs_5_) | copy-start | bytes 1327108
  152.0 0.8 copy-start.6
  152.9 0.8 copy-start.7

commit v3 on v2

--- a/solution.py
+++ b/solution.py
@@ -348,15 +348,6 @@
         tables.append(table)
         return later
 
-    before, after = swap_edges(both, "lon", 1, R, True)
-    state = next_table(state)
-    before, after, state = lax.optimization_barrier((before, after, state))
-    spare = jnp.zeros((lat_dev, ext_width - lon_dev - 2 * R, 2 * channels), jnp.bfloat16)
-    wide = jnp.concatenate([before, both, after, spare], axis=1)
-    above, below = swap_edges(wide, "lat", 0, 1, False)
-    state = next_table(state)
-    ext = jnp.concatenate([above, wide, below], axis=0).reshape((lat_dev + 2) * ext_width, 2 * channels)
-
     live = live_taps(taps, counts).astype(jnp.float32)
     live_ext = lax.dynamic_slice_in_dim(jnp.pad(live, ((1, 1), (0, 0), (0, 0), (0, 0))), first_row, lat_dev + 2, 0)
     shift_ext = lax.dynamic_slice_in_dim(jnp.pad(offsets, ((1, 1), (0, 0), (0, 0))), first_row, lat_dev + 2, 0)
@@ -367,10 +358,20 @@
     tap_back = spread(live_back, ext_width).reshape(lat_dev, K * S, 3 * ext_width)
     shift_back = spread(shift_back, ext_width)
 
+    before, after = swap_edges(both, "lon", 1, R, True)
+    rows_of_taps = (tap_own, shift_own, tap_back, shift_back)
+    before, after, rows_of_taps = lax.optimization_barrier((before, after, rows_of_taps))
+    spare = jnp.zeros((lat_dev, ext_width - lon_dev - 2 * R, 2 * channels), jnp.bfloat16)
+    wide = jnp.concatenate([before, both, after, spare], axis=1)
+    above, below = swap_edges(wide, "lat", 0, 1, False)
+    ext = jnp.concatenate([above, wide, below], axis=0).reshape((lat_dev + 2) * ext_width, 2 * channels)
+
     cot_flat = cotangent.reshape(lat_dev * lon_dev, channels)
     response, grad_field, packed = grid_part(
-        ext, cot_flat, mix_weight, tap_own, shift_own, tap_back, shift_back, lon_count
+        ext, cot_flat, mix_weight, *rows_of_taps, lon_count
     )
+    packed, state = lax.optimization_barrier((packed, state))
+    state = next_table(state)
 
     dft_rows = dft_table(total_lon, orders).reshape(2 * block_rows, total_lon)
 
@@ -381,7 +382,6 @@
     split_sum = mix_rows % (lat_count * lon_count) == 0
     if split_sum:
         mix_sent = mix_local.astype(jnp.bfloat16).reshape(lat_count, mix_rows // lat_count, channels)
-        packed, mix_sent, mix_local = lax.optimization_barrier((packed, mix_sent, mix_local))
         lat_share = lax.dynamic_index_in_dim(
             mix_local.reshape(lat_count, mix_rows // lat_count, channels), lat_pos, 0, keepdims=False
         )
@@ -392,25 +392,39 @@
 
     columns = lax.all_to_all(packed, "lon", split_axis=0, concat_axis=0, tiled=True)
     columns, state = lax.optimization_barrier((columns, state))
-    while len(tables) * DEGREES < L:
-        state = next_table(state)
+    state = next_table(state)
     columns = columns.reshape(total_lon, lat_dev * chans)
     gathered, bands = [columns], [lat_pos]
     for turn in range(1, lat_count):
         gathered.append(swap_with(columns, turn, lat_count))
         bands.append(source_of(lat_pos, turn, lat_count))
-    grad_spectra = synthesis(
-        jnp.stack(bands).astype(jnp.int32), dft_rows, gathered, tables, chans, total_lat, total_lon
-    )
-
     if split_sum:
         for piece in arrived:
             lat_share = lat_share + piece.astype(jnp.float32)
         lon_rows = mix_rows // (lat_count * lon_count)
         lon_sent = lat_share.astype(jnp.bfloat16).reshape(lon_count, lon_rows, channels)
         lon_got = lax.all_to_all(lon_sent, "lon", split_axis=0, concat_axis=0, tiled=True)
+        lon_got, state = lax.optimization_barrier((lon_got, state))
         mix_share = jnp.sum(lon_got.astype(jnp.float32), axis=0).astype(jnp.bfloat16)
-        grad_mix = lax.all_gather(mix_share, ("lat", "lon"), axis=0, tiled=False).astype(jnp.float32)
+        copies = jnp.broadcast_to(mix_share[None], lon_got.shape)
+        mix_band = lax.all_to_all(copies, "lon", split_axis=0, concat_axis=0, tiled=True)
+    while len(tables) * DEGREES < L:
+        state = next_table(state)
+    if split_sum:
+        gathered, tables, mix_band = lax.optimization_barrier((gathered, tables, mix_band))
+        mix_bands = [mix_band] + [swap_with(mix_band, turn, lat_count) for turn in range(1, lat_count)]
+    grad_spectra = synthesis(
+        jnp.stack(bands).astype(jnp.int32), dft_rows, gathered, tables, chans, total_lat, total_lon
+    )
+
+    if split_sum:
+        ordered = []
+        for band in range(lat_count):
+            chosen = mix_bands[0]
+            for turn in range(1, lat_count):
+                chosen = jnp.where(source_of(lat_pos, turn, lat_count) == band, mix_bands[turn], chosen)
+            ordered.append(chosen.astype(jnp.float32))
+        grad_mix = jnp.stack(ordered)
     else:
         grad_mix = lax.psum(mix_local, ("lat", "lon"))
     grad_mix = grad_mix.reshape(K, channels, channels)

time: 172 us -> 117 us (0.68)
  blocking collectives: 45.5 us -> 0 us
  waiting for transfers between devices: 30.4 us -> 8.18 us
  starting transfers between devices: 26.4 us -> 37 us
    all_gather x1 -> x0, blocking collectives: 45.5 us -> none  [on_device(): lax.all_gather(mix_share, ('lat', 'lon'), axis=0, tiled=False)]
    ppermute x6 -> x9, waiting for transfers between devices: 22.7 us -> 3.68 us  [swap_with(): lax.ppermute(value, 'lat', [(i, partner(i, turn, count)) for i in range(c...]
    all_to_all x1, waiting for transfers between devices: 7.6 us -> 0.01 us  [on_device(): lax.all_to_all(lon_sent, 'lon', split_axis=0, concat_axis=0, tiled=True)]
    ppermute x6 -> x9, starting transfers between devices: 7.97 us -> 13.2 us  [swap_with(): lax.ppermute(value, 'lat', [(i, partner(i, turn, count)) for i in range(c...]
    all_to_all x0 -> x1, starting transfers between devices: none -> 5.1 us  [on_device(): lax.all_to_all(copies, 'lon', split_axis=0, concat_axis=0, tiled=True)]
    all_to_all x0 -> x1, waiting for transfers between devices: none -> 3.15 us  [on_device(): lax.all_to_all(copies, 'lon', split_axis=0, concat_axis=0, tiled=True)]
  transfers between devices with their start and end apart: 12 -> 16, of which waited for: 7 -> 4; matrix products, arithmetic and copies ran while one was open for 8% -> 17% of each run, Pallas kernels for 11% -> 31%
where the time goes in v3:
time: 117 us; the launch traced here: 116 us
  Pallas kernels  45.2 us (39%)
  starting transfers between devices  37 us (32%)
  local copies, waits for them, and re-layouts  15.9 us (14%)
  waiting for transfers between devices  8.18 us (7%)
  other arithmetic  6.83 us (6%)
  matrix products  2.38 us (2%)
    pallas_call x3, Pallas kernels, legendre_table(): pl.pallas_call(functools.partial(legendre_kernel, start_block), grid=(DEG...  18.7 us
    pallas_call x1, Pallas kernels, synthesis(): pl.pallas_call(functools.partial(synthesis_kernel, lon_total, lat_total,...  17.1 us
    ppermute x9, starting transfers between devices, swap_with(): lax.ppermute(value, 'lat', [(i, partner(i, turn, count)) for i in range(c...  13.2 us
    pallas_call x1, Pallas kernels, grid_part(): pl.pallas_call(functools.partial(grid_kernel, lon_count), in_specs=[pl.Bl...  9.4 us
    ppermute x2, starting transfers between devices, swap_edges(): lax.ppermute(lax.slice_in_dim(shard, 0, width, axis=dim), axis, down)  5.39 us
    all_to_all x1, starting transfers between devices, on_device(): lax.all_to_all(copies, 'lon', split_axis=0, concat_axis=0, tiled=True)  5.1 us
    ppermute x2, starting transfers between devices, swap_edges(): lax.ppermute(lax.slice_in_dim(shard, length - width, length, axis=dim), a...  5.05 us
    all_to_all x1, starting transfers between devices, on_device(): lax.all_to_all(lon_sent, 'lon', split_axis=0, concat_axis=0, tiled=True)  4.74 us
  transfers between devices with their start and end apart: 16, of which 4 were waited for; matrix products, arithmetic and copies ran while one was open for 17% of the time, Pallas kernels for 31%

profile of v3, /device:TPU:0, one launch (start us, length us, event | category | flops | bytes accessed | tf_op | source)
XLA Modules:
  0.0 116.4 jit_solution(14104517724497494671)
XLA Ops:
  0.7 1.1 constant_dynamic-update-slice_fusion.1
  1.7 1.1 constant_dynamic-update-slice_fusion
  2.9 0.5 collective-permute-start
  3.4 4.1 %collective-permute-start.1 = (bf16[24,8,768]{2,1,0:T(8,128)(2,1)S(1)}, bf16[24,8,768]{2,1,0:T(8,128)(2,1)S(1)}, u32[]{:S(2)}, u32[]{:S(2)}) collective-permute-start(bf16[24,8,768]{2,1,0:T(8,128)(2,1)S(1)} %get-tuple-element.88), channel_id=1, source_target_pairs={{1,0},{2,1},{3,2},{4,3},{5,4},{6,5},{7,6},{0,7},{9,8},{10,9},{11,1... | collective-permute-start | bytes 884744 | tf_op jit(solution)/shard_map/ppermute | solution.py:301
  7.5 0.1 dynamic-slice_convert_fusion
  7.7 0.7 slice_bitcast_fusion.3
  8.3 0.5 sine_log_fusion
  8.9 0.6 iota_add_fusion
  9.5 0.6 fusion.16
  10.0 0.2 copy.15
  10.3 0.8 broadcast_in_dim.38
  11.1 1.3 %reshape_reshape.6.tap_own_ref = f32[24,24,144]{2,1,0:T(8,128)} reshape(f32[24,3,8,3,48]{4,3,2,1,0:T(4,128)S(1)} %broadcast_in_dim.38) | data formatting | bytes 663552 | tf_op jit(solution)/shard_map/reshape;reshape | solution.py:354
  12.3 0.8 dynamic-slice_bitcast_fusion.3
  13.1 0.1 copy.16
  13.2 0.3 broadcast_in_dim.39
  13.5 0.9 reshape.199.shift_own_ref
  14.4 0.2 copy.19
  14.7 0.8 broadcast_in_dim.40
  15.4 1.3 %reshape_reshape.7.tap_back_ref = f32[24,24,144]{2,1,0:T(8,128)} reshape(f32[24,3,8,3,48]{4,3,2,1,0:T(4,128)S(1)} %broadcast_in_dim.40) | data formatting | bytes 663552 | tf_op jit(solution)/shard_map/reshape;reshape | solution.py:358
  16.7 0.8 fusion.11
  17.5 0.1 copy.20
  17.7 0.3 broadcast_in_dim.41
  17.9 0.9 reshape.200.shift_back_ref
  18.8 0.3 reduce-window.9
  19.2 0.1 slice_reduce_fusion
  19.4 0.5 pad_bitcast_fusion.cos_ref
  20.1 0.1 multiply_add_fusion
  20.2 0.6 pad.22.scale_in
  20.8 0.5 cosine_convert_fusion
  21.3 0.6 pad_maximum_fusion.1
  22.0 1.3 %collective-permute-start.3 = (bf16[1,48,768]{2,1,0:T(8,128)(2,1)S(1)}, bf16[1,48,768]{2,1,0:T(8,128)(2,1)S(1)}, u32[]{:S(2)}, u32[]{:S(2)}) collective-permute-start(bf16[1,48,768]{2,1,0:T(8,128)(2,1)S(1)} %get-tuple-element.80), channel_id=1, source_target_pairs={{8,0},{16,8},{24,16},{9,1},{17,9},{25,17},{10,2},{18,10},{26,18},{... | collective-permute-start | bytes 221192 | tf_op jit(solution)/shard_map/ppermute | solution.py:301
  23.3 4.5 %collective-permute-start.2 = (bf16[1,48,768]{2,1,0:T(8,128)(2,1)S(1)}, bf16[1,48,768]{2,1,0:T(8,128)(2,1)S(1)}, u32[]{:S(2)}, u32[]{:S(2)}) collective-permute-start(bf16[1,48,768]{2,1,0:T(8,128)(2,1)S(1)} %get-tuple-element.79), channel_id=1, source_target_pairs={{0,8},{8,16},{16,24},{1,9},{9,17},{17,25},{2,10},{10,18},{18,26},{... | collective-permute-start | bytes 221192 | tf_op jit(solution)/shard_map/ppermute | solution.py:300
  27.9 0.6 pad_add_fusion.1.refs_0_
  28.5 1.3 %collective-permute-done.2 = bf16[1,48,768]{2,1,0:T(8,128)(2,1)S(1)} collective-permute-done((bf16[1,48,768]{2,1,0:T(8,128)(2,1)S(1)}, bf16[1,48,768]{2,1,0:T(8,128)(2,1)S(1)}, u32[]{:S(2)}, u32[]{:S(2)}) %collective-permute-start.2) | collective-permute-done | bytes 73760 | tf_op jit(solution)/shard_map/ppermute | solution.py:300
  29.8 1.4 %pad_maximum_fusion = bf16[26,48,768]{2,1,0:T(8,128)(2,1)} fusion(bf16[1,48,768]{2,1,0:T(8,128)(2,1)S(1)} %collective-permute-done.3, bf16[24,8,768]{2,1,0:T(8,128)(2,1)S(1)} %broadcast_in_dim.42, bf16[24,8,768]{2,1,0:T(8,128)(2,1)S(1)} %collective-permute-done.1, bf16[24,24,768]{2,1,0:T(8,128)(2,1)S(1)} %constant_dynamic-update-slice_fusion, ...), kind=kLoop, calls=%fused_computation.1 | loop fusion | flops 11501568 | bytes 3833856 | tf_op jit(solution)/shard_map/concatenate | solution.py:367
  31.2 9.4 %grid_part.1 = (bf16[576,1152]{1,0:T(8,128)(2,1)}, bf16[576,384]{1,0:T(8,128)(2,1)}, bf16[8,24,1152]{2,1,0:T(8,128)(2,1)}) custom-call(bf16[1248,768]{1,0:T(8,128)(2,1)} %bitcast.61, bf16[576,384]{1,0:T(8,128)(2,1)} %bitcast.62, bf16[3,384,384]{2,1,0:T(8,128)(2,1)} %weight_ref.1, f32[24,24,144]{2,1,0:T(8,128)} %reshape_reshape.6.tap_own_ref, ...), custom_call_target="tpu_custom_call" | custom-call | tf_op jit(solution)/shard_map/grid_part/pallas_call | solution.py:277
  40.6 3.5 %all-to-all-start = ((bf16[8,24,1152]{2,1,0:T(8,128)(2,1)}), bf16[8,24,1152]{2,1,0:T(8,128)(2,1)S(1)}, u32[]{:S(2)}, u32[]{:S(2)}) async-start(bf16[8,24,1152]{2,1,0:T(8,128)(2,1)} %get-tuple-element.49), calls=%async_computation | async-start | bytes 884736 | tf_op jit(solution)/shard_map/all_to_all | solution.py:393
  44.1 2.4 %fusion.19 = (bf16[1152,384]{1,0:T(8,128)(2,1)S(1)}, f32[1152,384]{1,0:T(8,128)S(1)}) fusion(bf16[576,1152]{1,0:T(8,128)(2,1)} %get-tuple-element.62, bf16[576,384]{1,0:T(8,128)(2,1)S(1)} %bitcast.63), kind=kOutput, calls=%fused_computation.64 | convolution fusion | flops 510492672 | bytes 4423680 | tf_op jit(solution)/shard_map/dot_general | solution.py:378
  46.5 0.1 dynamic-slice_bitcast_fusion.2
  46.6 3.8 %collective-permute-start.9 = (bf16[288,384]{1,0:T(8,128)(2,1)S(1)}, bf16[288,384]{1,0:T(8,128)(2,1)S(1)}, u32[]{:S(2)}, u32[]{:S(2)}) collective-permute-start(bf16[288,384]{1,0:T(8,128)(2,1)S(1)} %get-tuple-element.86), channel_id=1, source_target_pairs={{0,24},{8,16},{16,8},{24,0},{1,25},{9,17},{17,9},{25,1},{2,26},{10... | collective-permute-start | bytes 663560 | tf_op jit(solution)/shard_map/ppermute | solution.py:318
  50.4 0.9 collective-permute-start.8
  51.3 1.4 %collective-permute-start.7 = (bf16[288,384]{1,0:T(8,128)(2,1)S(1)}, bf16[288,384]{1,0:T(8,128)(2,1)S(1)}, u32[]{:S(2)}, u32[]{:S(2)}) collective-permute-start(bf16[288,384]{1,0:T(8,128)(2,1)S(1)} %get-tuple-element.85), channel_id=1, source_target_pairs={{0,8},{8,0},{16,24},{24,16},{1,9},{9,1},{17,25},{25,17},{2,10},{10... | collective-permute-start | bytes 663560 | tf_op jit(solution)/shard_map/ppermute | solution.py:318
  52.7 0.6 broadcast_in_dim.43.prev_in.early_in
  53.4 6.2 %legendre_table.3 = (bf16[96,128,128]{2,1,0:T(8,128)(2,1)}, f32[96,128]{1,0:T(8,128)}, f32[96,128]{1,0:T(8,128)}, f32[96,128]{1,0:T(8,128)}) custom-call(s32[1]{0:T(128)} %bitcast.17.first_ref, f32[1,128]{1,0:T(1,128)} %pad_bitcast_fusion.cos_ref, f32[96,128]{1,0:T(8,128)} %broadcast_in_dim.43.prev_in.early_in, f32[96,128]{1,0:T(8,128)} %broadcast_in_dim.43.prev_in.early_in, ...), custom_call_target="tpu_custom_call" | custom-call | flops 7864320000 | bytes 3145728 | tf_op jit(solution)/shard_map/legendre_table/pallas_call | solution.py:121
  59.6 1.8 %collective-permute-done.8 = bf16[288,384]{1,0:T(8,128)(2,1)S(1)} collective-permute-done((bf16[288,384]{1,0:T(8,128)(2,1)S(1)}, bf16[288,384]{1,0:T(8,128)(2,1)S(1)}, u32[]{:S(2)}, u32[]{:S(2)}) %collective-permute-start.8) | collective-permute-done | bytes 221216 | tf_op jit(solution)/shard_map/ppermute | solution.py:318
  61.4 1.9 %collective-permute-done.7 = bf16[288,384]{1,0:T(8,128)(2,1)S(1)} collective-permute-done((bf16[288,384]{1,0:T(8,128)(2,1)S(1)}, bf16[288,384]{1,0:T(8,128)(2,1)S(1)}, u32[]{:S(2)}, u32[]{:S(2)}) %collective-permute-start.7) | collective-permute-done | bytes 221216 | tf_op jit(solution)/shard_map/ppermute | solution.py:318
  63.3 0.1 fusion.2
  63.4 0.7 reshape.209
  64.1 4.7 %all-to-all-start.1 = ((bf16[8,36,384]{2,1,0:T(8,128)(2,1)}), bf16[8,36,384]{2,1,0:T(8,128)(2,1)S(1)}, u32[]{:S(2)}, u32[]{:S(2)}) async-start(bf16[8,36,384]{2,1,0:T(8,128)(2,1)} %reshape.209), calls=%async_computation.1 | async-start | bytes 491520 | tf_op jit(solution)/shard_map/all_to_all | solution.py:406
  68.8 0.2 collective-permute-start.4
  69.1 0.9 collective-permute-start.5
  70.0 2.4 %collective-permute-start.6 = (bf16[192,1152]{1,0:T(8,128)(2,1)S(1)}, bf16[192,1152]{1,0:T(8,128)(2,1)S(1)}, u32[]{:S(2)}, u32[]{:S(2)}) collective-permute-start(bf16[192,1152]{1,0:T(8,128)(2,1)S(1)} %bitcast.68), channel_id=1, source_target_pairs={{0,24},{8,16},{16,8},{24,0},{1,25},{9,17},{17,9},{25,1},{2,26},{10... | collective-permute-start | bytes 1327112 | tf_op jit(solution)/shard_map/ppermute | solution.py:318
  72.3 6.2 %legendre_table.4 = (bf16[96,128,128]{2,1,0:T(8,128)(2,1)}, f32[96,128]{1,0:T(8,128)}, f32[96,128]{1,0:T(8,128)}, f32[96,128]{1,0:T(8,128)}) custom-call(s32[1]{0:T(128)} %bitcast.17.first_ref, f32[1,128]{1,0:T(1,128)} %pad_bitcast_fusion.cos_ref, f32[96,128]{1,0:T(8,128)} %get-tuple-element.58.prev_in, f32[96,128]{1,0:T(8,128)} %get-tuple-element.59.early_in, ...), custom_call_target="tpu_custom_call" | custom-call | flops 7864320000 | bytes 3145728 | tf_op jit(solution)/shard_map/legendre_table/pallas_call | solution.py:121
  78.6 0.7 broadcast_in_dim.45
  79.3 5.1 %all-to-all-start.2 = ((bf16[8,36,384]{2,1,0:T(8,128)(2,1)}), bf16[8,36,384]{2,1,0:T(8,128)(2,1)S(1)}, u32[]{:S(2)}, u32[]{:S(2)}) async-start(bf16[8,36,384]{2,1,0:T(8,128)(2,1)} %broadcast_in_dim.45), calls=%async_computation.2 | async-start | bytes 491520 | tf_op jit(solution)/shard_map/all_to_all | solution.py:410
  84.4 6.2 %legendre_table.5 = (bf16[96,128,128]{2,1,0:T(8,128)(2,1)}, f32[96,128]{1,0:T(8,128)}, f32[96,128]{1,0:T(8,128)}, f32[96,128]{1,0:T(8,128)}) custom-call(s32[1]{0:T(128)} %bitcast.17.first_ref, f32[1,128]{1,0:T(1,128)} %pad_bitcast_fusion.cos_ref, f32[96,128]{1,0:T(8,128)} %get-tuple-element.66.prev_in, f32[96,128]{1,0:T(8,128)} %get-tuple-element.67.early_in, ...), custom_call_target="tpu_custom_call" | custom-call | flops 7864320000 | bytes 3145728 | tf_op jit(solution)/shard_map/legendre_table/pallas_call | solution.py:121
  90.7 3.1 %all-to-all-done.2 = bf16[8,36,384]{2,1,0:T(8,128)(2,1)S(1)} async-done(((bf16[8,36,384]{2,1,0:T(8,128)(2,1)}), bf16[8,36,384]{2,1,0:T(8,128)(2,1)S(1)}, u32[]{:S(2)}, u32[]{:S(2)}) %all-to-all-start.2) | async-done | bytes 221216 | tf_op jit(solution)/shard_map/all_to_all | solution.py:410
  93.9 0.6 collective-permute-start.10
  94.5 1.2 collective-permute-start.11
  95.6 1.8 %collective-permute-start.12 = (bf16[8,36,384]{2,1,0:T(8,128)(2,1)S(1)}, bf16[8,36,384]{2,1,0:T(8,128)(2,1)S(1)}, u32[]{:S(2)}, u32[]{:S(2)}) collective-permute-start(bf16[8,36,384]{2,1,0:T(8,128)(2,1)S(1)} %all-to-all-done.2), channel_id=1, source_target_pairs={{0,8},{8,0},{16,24},{24,16},{1,9},{9,1},{17,25},{25,17},{2,10},{10... | collective-permute-start | bytes 663560 | tf_op jit(solution)/shard_map/ppermute | solution.py:318
  97.4 17.1 %dft_synthesis.1 = f32[2,96,48,384]{3,2,1,0:T(8,128)} custom-call(s32[4]{0:T(128)} %pad_add_fusion.1.refs_0_, bf16[192,192]{1,0:T(8,128)(2,1)} %bitcast.70, bf16[192,1152]{1,0:T(8,128)(2,1)} %bitcast.69, bf16[192,1152]{1,0:T(8,128)(2,1)} %copy-done.9, bf16[192,1152]{1,0:T(8,128)(2,1)} %copy-done.10, bf16[192,1152]{1,0:T(8,128)(2,1)} %copy-done.11, ...), custom_call_target="tpu_custom_call" | custom-call | flops 20000000000 | bytes 14155776 | tf_op jit(solution)/shard_map/dft_synthesis/pallas_call | solution.py:190
  114.6 0.2 select_bitcast_fusion.3
  114.8 0.2 maximum_convert_fusion
  115.0 1.4 %reshape.213 = f32[3,384,384]{2,1,0:T(8,128)} reshape(f32[4,8,36,384]{3,2,1,0:T(8,128)S(1)} %maximum_convert_fusion) | data formatting | bytes 3538944 | tf_op jit(solution)/shard_map/reshape | solution.py:430
  (52 shorter events, 0.7 us)
Async XLA Ops:
  0.6 6.8 %copy-start.4 = (f32[96,3,3,8]{0,3,2,1:T(8,128)S(1)}, f32[96,3,3,8]{0,3,2,1:T(8,128)}, u32[]{:S(2)}) copy-start(f32[96,3,3,8]{0,3,2,1:T(8,128)} %param.9) | copy-start | bytes 82948
  0.6 6.8 %copy-start.5 = (s32[96]{0:T(128)S(1)}, s32[96]{0:T(128)}, u32[]{:S(2)}) copy-start(s32[96]{0:T(128)} %param.11) | copy-start | bytes 1156
  2.9 19.1 %collective-permute-start = (bf16[24,8,768]{2,1,0:T(8,128)(2,1)S(1)}, bf16[24,8,768]{2,1,0:T(8,128)(2,1)S(1)}, u32[]{:S(2)}, u32[]{:S(2)}) collective-permute-start(bf16[24,8,768]{2,1,0:T(8,128)(2,1)S(1)} %get-tuple-element.89), channel_id=1, source_target_pairs={{0,1},{1,2},{2,3},{3,4},{4,5},{5,6},{6,7},{7,0},{8,9},{9,10},{10,1... | collective-permute-start | bytes 884744 | tf_op jit(solution)/shard_map/ppermute | solution.py:300
  3.4 18.6 %collective-permute-start.1 = (bf16[24,8,768]{2,1,0:T(8,128)(2,1)S(1)}, bf16[24,8,768]{2,1,0:T(8,128)(2,1)S(1)}, u32[]{:S(2)}, u32[]{:S(2)}) collective-permute-start(bf16[24,8,768]{2,1,0:T(8,128)(2,1)S(1)} %get-tuple-element.88), channel_id=1, source_target_pairs={{1,0},{2,1},{3,2},{4,3},{5,4},{6,5},{7,6},{0,7},{9,8},{10,9},{11,1... | collective-permute-start | bytes 884744 | tf_op jit(solution)/shard_map/ppermute | solution.py:301
  11.0 3.3 %copy-start.2 = (f32[24,3,8,1]{0,2,1,3:T(8,128)S(1)}, f32[24,3,8,1]{0,2,1,3:T(8,128)}, u32[]{:S(2)}) copy-start(f32[24,3,8,1]{0,2,1,3:T(8,128)} %get-tuple-element.91) | copy-start | bytes 6916
  11.1 3.3 %copy-start.3 = (f32[24,3,8,1]{0,2,1,3:T(8,128)S(1)}, f32[24,3,8,1]{0,2,1,3:T(8,128)}, u32[]{:S(2)}) copy-start(f32[24,3,8,1]{0,2,1,3:T(8,128)} %get-tuple-element.92) | copy-start | bytes 6916
  14.6 5.5 %copy-start.7 = (f32[96]{0:T(128)S(1)}, f32[96]{0:T(128)}, u32[]{:S(2)}) copy-start(f32[96]{0:T(128)} %sine_log_fusion) | copy-start | bytes 1156
  14.6 5.5 %copy-start.8 = (f32[96]{0:T(128)S(1)}, f32[96]{0:T(128)}, u32[]{:S(2)}) copy-start(f32[96]{0:T(128)} %get-tuple-element.101) | copy-start | bytes 1156
  15.4 4.0 %copy-start.12 = (f32[96]{0:T(128)S(1)}, f32[96]{0:T(128)}, u32[]{:S(2)}) copy-start(f32[96]{0:T(128)} %fusion.16) | copy-start | bytes 1156
  15.4 5.4 %copy-start.6 = (s32[96]{0:T(128)S(1)}, s32[96]{0:T(128)}, u32[]{:S(2)}) copy-start(s32[96]{0:T(128)} %get-tuple-element.100) | copy-start | bytes 1156
  22.0 6.5 %collective-permute-start.3 = (bf16[1,48,768]{2,1,0:T(8,128)(2,1)S(1)}, bf16[1,48,768]{2,1,0:T(8,128)(2,1)S(1)}, u32[]{:S(2)}, u32[]{:S(2)}) collective-permute-start(bf16[1,48,768]{2,1,0:T(8,128)(2,1)S(1)} %get-tuple-element.80), channel_id=1, source_target_pairs={{8,0},{16,8},{24,16},{9,1},{17,9},{25,17},{10,2},{18,10},{26,18},{... | collective-permute-start | bytes 221192 | tf_op jit(solution)/shard_map/ppermute | solution.py:301
  23.3 6.5 %collective-permute-start.2 = (bf16[1,48,768]{2,1,0:T(8,128)(2,1)S(1)}, bf16[1,48,768]{2,1,0:T(8,128)(2,1)S(1)}, u32[]{:S(2)}, u32[]{:S(2)}) collective-permute-start(bf16[1,48,768]{2,1,0:T(8,128)(2,1)S(1)} %get-tuple-element.79), channel_id=1, source_target_pairs={{0,8},{8,16},{16,24},{1,9},{9,17},{17,25},{2,10},{10,18},{18,26},{... | collective-permute-start | bytes 221192 | tf_op jit(solution)/shard_map/ppermute | solution.py:300
  31.2 12.9 %copy-start = (bf16[24,24,384]{2,1,0:T(8,128)(2,1)S(1)}, bf16[24,24,384]{2,1,0:T(8,128)(2,1)}, u32[]{:S(2)}) copy-start(bf16[24,24,384]{2,1,0:T(8,128)(2,1)} %param.7) | copy-start | bytes 1327108
  40.6 23.5 %all-to-all-start = ((bf16[8,24,1152]{2,1,0:T(8,128)(2,1)}), bf16[8,24,1152]{2,1,0:T(8,128)(2,1)S(1)}, u32[]{:S(2)}, u32[]{:S(2)}) async-start(bf16[8,24,1152]{2,1,0:T(8,128)(2,1)} %get-tuple-element.49), calls=%async_computation | async-start | bytes 884736 | tf_op jit(solution)/shard_map/all_to_all | solution.py:393
  46.6 13.0 %collective-permute-start.9 = (bf16[288,384]{1,0:T(8,128)(2,1)S(1)}, bf16[288,384]{1,0:T(8,128)(2,1)S(1)}, u32[]{:S(2)}, u32[]{:S(2)}) collective-permute-start(bf16[288,384]{1,0:T(8,128)(2,1)S(1)} %get-tuple-element.86), channel_id=1, source_target_pairs={{0,24},{8,16},{16,8},{24,0},{1,25},{9,17},{17,9},{25,1},{2,26},{10... | collective-permute-start | bytes 663560 | tf_op jit(solution)/shard_map/ppermute | solution.py:318
  50.4 11.0 %collective-permute-start.8 = (bf16[288,384]{1,0:T(8,128)(2,1)S(1)}, bf16[288,384]{1,0:T(8,128)(2,1)S(1)}, u32[]{:S(2)}, u32[]{:S(2)}) collective-permute-start(bf16[288,384]{1,0:T(8,128)(2,1)S(1)} %get-tuple-element.87), channel_id=1, source_target_pairs={{0,16},{8,24},{16,0},{24,8},{1,17},{9,25},{17,1},{25,9},{2,18},{10... | collective-permute-start | bytes 663560 | tf_op jit(solution)/shard_map/ppermute | solution.py:318
  51.3 11.9 %collective-permute-start.7 = (bf16[288,384]{1,0:T(8,128)(2,1)S(1)}, bf16[288,384]{1,0:T(8,128)(2,1)S(1)}, u32[]{:S(2)}, u32[]{:S(2)}) collective-permute-start(bf16[288,384]{1,0:T(8,128)(2,1)S(1)} %get-tuple-element.85), channel_id=1, source_target_pairs={{0,8},{8,0},{16,24},{24,16},{1,9},{9,1},{17,25},{25,17},{2,10},{10... | collective-permute-start | bytes 663560 | tf_op jit(solution)/shard_map/ppermute | solution.py:318
  64.1 14.5 %copy-start.1 = (bf16[8,24,1152]{2,1,0:T(8,128)(2,1)}, bf16[8,24,1152]{2,1,0:T(8,128)(2,1)S(1)}, u32[]{:S(2)}) copy-start(bf16[8,24,1152]{2,1,0:T(8,128)(2,1)S(1)} %all-to-all-done) | copy-start | bytes 1327108
  64.1 14.5 %all-to-all-start.1 = ((bf16[8,36,384]{2,1,0:T(8,128)(2,1)}), bf16[8,36,384]{2,1,0:T(8,128)(2,1)S(1)}, u32[]{:S(2)}, u32[]{:S(2)}) async-start(bf16[8,36,384]{2,1,0:T(8,128)(2,1)} %reshape.209), calls=%async_computation.1 | async-start | bytes 491520 | tf_op jit(solution)/shard_map/all_to_all | solution.py:406
  68.8 25.0 %collective-permute-start.4 = (bf16[192,1152]{1,0:T(8,128)(2,1)S(1)}, bf16[192,1152]{1,0:T(8,128)(2,1)S(1)}, u32[]{:S(2)}, u32[]{:S(2)}) collective-permute-start(bf16[192,1152]{1,0:T(8,128)(2,1)S(1)} %bitcast.66), channel_id=1, source_target_pairs={{0,8},{8,0},{16,24},{24,16},{1,9},{9,1},{17,25},{25,17},{2,10},{10... | collective-permute-start | bytes 1327112 | tf_op jit(solution)/shard_map/ppermute | solution.py:318
  69.1 24.7 %collective-permute-start.5 = (bf16[192,1152]{1,0:T(8,128)(2,1)S(1)}, bf16[192,1152]{1,0:T(8,128)(2,1)S(1)}, u32[]{:S(2)}, u32[]{:S(2)}) collective-permute-start(bf16[192,1152]{1,0:T(8,128)(2,1)S(1)} %bitcast.67), channel_id=1, source_target_pairs={{0,16},{8,24},{16,0},{24,8},{1,17},{9,25},{17,1},{25,9},{2,18},{10... | collective-permute-start | bytes 1327112 | tf_op jit(solution)/shard_map/ppermute | solution.py:318
  70.0 23.9 %collective-permute-start.6 = (bf16[192,1152]{1,0:T(8,128)(2,1)S(1)}, bf16[192,1152]{1,0:T(8,128)(2,1)S(1)}, u32[]{:S(2)}, u32[]{:S(2)}) collective-permute-start(bf16[192,1152]{1,0:T(8,128)(2,1)S(1)} %bitcast.68), channel_id=1, source_target_pairs={{0,24},{8,16},{16,8},{24,0},{1,25},{9,17},{17,9},{25,1},{2,26},{10... | collective-permute-start | bytes 1327112 | tf_op jit(solution)/shard_map/ppermute | solution.py:318
  79.3 14.5 %all-to-all-start.2 = ((bf16[8,36,384]{2,1,0:T(8,128)(2,1)}), bf16[8,36,384]{2,1,0:T(8,128)(2,1)S(1)}, u32[]{:S(2)}, u32[]{:S(2)}) async-start(bf16[8,36,384]{2,1,0:T(8,128)(2,1)} %broadcast_in_dim.45), calls=%async_computation.2 | async-start | bytes 491520 | tf_op jit(solution)/shard_map/all_to_all | solution.py:410
  93.8 3.6 %copy-start.9 = (bf16[192,1152]{1,0:T(8,128)(2,1)}, bf16[192,1152]{1,0:T(8,128)(2,1)S(1)}, u32[]{:S(2)}) copy-start(bf16[192,1152]{1,0:T(8,128)(2,1)S(1)} %collective-permute-done.4.refs_3_) | copy-start | bytes 1327108
  93.8 3.6 %copy-start.10 = (bf16[192,1152]{1,0:T(8,128)(2,1)}, bf16[192,1152]{1,0:T(8,128)(2,1)S(1)}, u32[]{:S(2)}) copy-start(bf16[192,1152]{1,0:T(8,128)(2,1)S(1)} %collective-permute-done.5.refs_4_) | copy-start | bytes 1327108
  93.9 3.6 %copy-start.11 = (bf16[192,1152]{1,0:T(8,128)(2,1)}, bf16[192,1152]{1,0:T(8,128)(2,1)S(1)}, u32[]{:S(2)}) copy-start(bf16[192,1152]{1,0:T(8,128)(2,1)S(1)} %collective-permute-done.6.refs_5_) | copy-start | bytes 1327108
  93.9 20.7 %collective-permute-start.10 = (bf16[8,36,384]{2,1,0:T(8,128)(2,1)S(1)}, bf16[8,36,384]{2,1,0:T(8,128)(2,1)S(1)}, u32[]{:S(2)}, u32[]{:S(2)}) collective-permute-start(bf16[8,36,384]{2,1,0:T(8,128)(2,1)S(1)} %all-to-all-done.2), channel_id=1, source_target_pairs={{0,24},{8,16},{16,8},{24,0},{1,25},{9,17},{17,9},{25,1},{2,26},{10... | collective-permute-start | bytes 663560 | tf_op jit(solution)/shard_map/ppermute | solution.py:318
  94.5 20.1 %collective-permute-start.11 = (bf16[8,36,384]{2,1,0:T(8,128)(2,1)S(1)}, bf16[8,36,384]{2,1,0:T(8,128)(2,1)S(1)}, u32[]{:S(2)}, u32[]{:S(2)}) collective-permute-start(bf16[8,36,384]{2,1,0:T(8,128)(2,1)S(1)} %all-to-all-done.2), channel_id=1, source_target_pairs={{0,16},{8,24},{16,0},{24,8},{1,17},{9,25},{17,1},{25,9},{2,18},{10... | collective-permute-start | bytes 663560 | tf_op jit(solution)/shard_map/ppermute | solution.py:318
  95.6 18.9 %collective-permute-start.12 = (bf16[8,36,384]{2,1,0:T(8,128)(2,1)S(1)}, bf16[8,36,384]{2,1,0:T(8,128)(2,1)S(1)}, u32[]{:S(2)}, u32[]{:S(2)}) collective-permute-start(bf16[8,36,384]{2,1,0:T(8,128)(2,1)S(1)} %all-to-all-done.2), channel_id=1, source_target_pairs={{0,8},{8,0},{16,24},{24,16},{1,9},{9,1},{17,25},{25,17},{2,10},{10... | collective-permute-start | bytes 663560 | tf_op jit(solution)/shard_map/ppermute | solution.py:318

commit v4 on v3

--- a/solution.py
+++ b/solution.py
@@ -205,24 +205,34 @@
 
 
 def grid_kernel(
-    lon_count, ext_ref, cot_ref, weight_ref, tap_own_ref, shift_own_ref, tap_back_ref, shift_back_ref,
+    lon_count, ext_ref, cot_ref, weight_ref, tap_ref, shift_ref,
     response_ref, field_ref, send_ref, moved_ref, total_ref, packed_ref,
 ):
-    lat_dev = tap_own_ref.shape[0]
+    lat_dev = tap_ref.shape[0] - 2
     cells, channels = cot_ref.shape
     lon_dev = cells // lat_dev
-    lanes = tap_own_ref.shape[2]
-    ext_width = lanes // 3
+    ext_width = ext_ref.shape[0] // (lat_dev + 2)
+    lanes = 3 * ext_width
+    place = lax.broadcasted_iota(jnp.int32, (1, lanes), 1)
+    at_first, at_second = place < ext_width, place < 2 * ext_width
     lane = lax.broadcasted_iota(jnp.int32, (lon_dev, lanes), 1)
     lane = jnp.where(lane >= 2 * ext_width, lane - 2 * ext_width, jnp.where(lane >= ext_width, lane - ext_width, lane))
     relative = lane - lax.broadcasted_iota(jnp.int32, (lon_dev, lanes), 0) - R
 
-    def bands(row, tap_ref, shift_ref):
+    def across(three):
+        return jnp.where(at_first, three[0], jnp.where(at_second, three[1], three[2]))
+
+    def bands(row, adjoint):
+        if adjoint:
+            sources = [(row + a, 2 - a) for a in range(3)]
+        else:
+            sources = [(row + 1, a) for a in range(3)]
         summed = [jnp.zeros((lon_dev, lanes), jnp.float32)] * K
         for slot in range(S):
-            hit = relative == shift_ref[row, slot : slot + 1, :]
+            shift = across([shift_ref[source, a * S + slot] for source, a in sources])
+            hit = relative == (-shift if adjoint else shift)
             for k in range(K):
-                tap = tap_ref[row, k * S + slot : k * S + slot + 1, :]
+                tap = across([tap_ref[source, (k * 3 + a) * S + slot] for source, a in sources])
                 summed[k] = summed[k] + jnp.where(hit, tap, 0.0)
         return jnp.concatenate(summed, axis=0).astype(jnp.bfloat16)
 
@@ -234,13 +244,13 @@
             rows = pl.ds(pl.multiple_of(row * ext_width, 16), lanes)
             own.append(
                 jnp.dot(
-                    bands(row, tap_own_ref, shift_own_ref), ext_ref[rows, 0:channels],
+                    bands(row, False), ext_ref[rows, 0:channels],
                     preferred_element_type=jnp.float32,
                 )
             )
             back.append(
                 jnp.dot(
-                    bands(row, tap_back_ref, shift_back_ref), ext_ref[rows, channels : 2 * channels],
+                    bands(row, True), ext_ref[rows, channels : 2 * channels],
                     preferred_element_type=jnp.float32,
                 )
             )
@@ -269,14 +279,14 @@
     send_ref[...] = packed_ref[...].astype(jnp.bfloat16)
 
 
-def grid_part(ext, cot, mix_weight, tap_own, shift_own, tap_back, shift_back, lon_count):
+def grid_part(ext, cot, mix_weight, taps, shifts, lon_count):
     cells, channels = cot.shape
-    lat_dev = tap_own.shape[0]
+    lat_dev = taps.shape[0] - 2
     lon_dev = cells // lat_dev
     packed = (lon_count, lon_dev, lat_dev * (channels // lon_count))
     return pl.pallas_call(
         functools.partial(grid_kernel, lon_count),
-        in_specs=[pl.BlockSpec(memory_space=pltpu.VMEM)] * 7,
+        in_specs=[pl.BlockSpec(memory_space=pltpu.VMEM)] * 3 + [pl.BlockSpec(memory_space=pltpu.SMEM)] * 2,
         out_specs=[pl.BlockSpec(memory_space=pltpu.VMEM)] * 3,
         out_shape=[
             jax.ShapeDtypeStruct((cells, K * channels), jnp.bfloat16),
@@ -290,7 +300,7 @@
         ],
         compiler_params=pltpu.CompilerParams(vmem_limit_bytes=VMEM_BYTES),
         name="grid_part",
-    )(ext, cot, mix_weight, tap_own, shift_own, tap_back, shift_back)
+    )(ext, cot, mix_weight, taps, shifts)
 
 
 def swap_edges(shard, axis, dim, width, wrap):
@@ -316,10 +326,6 @@
 
 def swap_with(value, turn, count):
     return lax.ppermute(value, "lat", [(i, partner(i, turn, count)) for i in range(count)])
-
-
-def spread(values, ext_width):
-    return jnp.repeat(values, ext_width, axis=-1)
 
 
 def on_device(field, cotangent, mix_weight, taps, offsets, counts):
@@ -348,19 +354,16 @@
         tables.append(table)
         return later
 
-    live = live_taps(taps, counts).astype(jnp.float32)
-    live_ext = lax.dynamic_slice_in_dim(jnp.pad(live, ((1, 1), (0, 0), (0, 0), (0, 0))), first_row, lat_dev + 2, 0)
-    shift_ext = lax.dynamic_slice_in_dim(jnp.pad(offsets, ((1, 1), (0, 0), (0, 0))), first_row, lat_dev + 2, 0)
-    tap_own = spread(jnp.transpose(live_ext[1:-1], (0, 1, 3, 2)), ext_width).reshape(lat_dev, K * S, 3 * ext_width)
-    shift_own = spread(jnp.transpose(shift_ext[1:-1], (0, 2, 1)), ext_width)
-    live_back = jnp.stack([live_ext[a : a + lat_dev, :, 2 - a, :] for a in range(3)], axis=-1)
-    shift_back = jnp.stack([-shift_ext[a : a + lat_dev, 2 - a, :] for a in range(3)], axis=-1)
-    tap_back = spread(live_back, ext_width).reshape(lat_dev, K * S, 3 * ext_width)
-    shift_back = spread(shift_back, ext_width)
+    live = live_taps(taps, counts).astype(jnp.float32).reshape(total_lat, K * 3 * S)
+    live_ext = lax.dynamic_slice_in_dim(jnp.pad(live, ((1, 1), (0, 0))), first_row, lat_dev + 2, 0)
+    shift_pad = jnp.pad(offsets.reshape(total_lat, 3 * S), ((1, 1), (0, 0)))
+    shift_ext = lax.dynamic_slice_in_dim(shift_pad, first_row, lat_dev + 2, 0)
 
     before, after = swap_edges(both, "lon", 1, R, True)
-    rows_of_taps = (tap_own, shift_own, tap_back, shift_back)
-    before, after, rows_of_taps = lax.optimization_barrier((before, after, rows_of_taps))
+    state = next_table(state)
+    before, after, live_ext, shift_ext, state = lax.optimization_barrier(
+        (before, after, live_ext, shift_ext, state)
+    )
     spare = jnp.zeros((lat_dev, ext_width - lon_dev - 2 * R, 2 * channels), jnp.bfloat16)
     wide = jnp.concatenate([before, both, after, spare], axis=1)
     above, below = swap_edges(wide, "lat", 0, 1, False)
@@ -368,7 +371,7 @@
 
     cot_flat = cotangent.reshape(lat_dev * lon_dev, channels)
     response, grad_field, packed = grid_part(
-        ext, cot_flat, mix_weight, *rows_of_taps, lon_count
+        ext, cot_flat, mix_weight, live_ext, shift_ext, lon_count
     )
     packed, state = lax.optimization_barrier((packed, state))
     state = next_table(state)

time: 117 us -> 134 us (1.15)
  waiting for transfers between devices: 8.18 us -> 35.7 us
  local copies, waits for them, and re-layouts: 15.9 us -> 8.12 us
  starting transfers between devices: 37 us -> 34.5 us
  other arithmetic: 6.83 us -> 5.05 us
    ppermute x9, waiting for transfers between devices: 3.68 us -> 18.9 us  [swap_with(): lax.ppermute(value, 'lat', [(i, partner(i, turn, count)) for i in range(c...]
    all_to_all x1, waiting for transfers between devices: 0.01 us -> 8.21 us  [on_device(): lax.all_to_all(lon_sent, 'lon', split_axis=0, concat_axis=0, tiled=True)]
    all_to_all x1, waiting for transfers between devices: 0.01 us -> 6.62 us  [on_device(): lax.all_to_all(packed, 'lon', split_axis=0, concat_axis=0, tiled=True)]
    another operation x6 -> x1, local copies, waits for them, and re-layouts: 3.73 us -> 0.12 us  [the longest x1 1.29 us: on_device(): spread(live_back, ext_width).reshape(lat_dev, K * S, 3 * ext_width)]
    all_to_all x1, waiting for transfers between devices: 3.15 us -> 0.01 us  [on_device(): lax.all_to_all(copies, 'lon', split_axis=0, concat_axis=0, tiled=True)]
    broadcast_in_dim x4 -> x0, local copies, waits for them, and re-layouts: 2.05 us -> none  [spread(): return jnp.repeat(values, ext_width, axis=-1)]
    reshape x2, local copies, waits for them, and re-layouts: 1.73 us -> 0.19 us  [the longest x1 0.1 us: on_device(): live_taps(taps, counts).astype(jnp.float32).reshape(total_lat, K * 3 * S)]
    all_to_all x1, starting transfers between devices: 5.1 us -> 3.59 us  [on_device(): lax.all_to_all(copies, 'lon', split_axis=0, concat_axis=0, tiled=True)]
  transfers between devices with their start and end apart: 16 -> 16, of which waited for: 4 -> 9; matrix products, arithmetic and copies ran while one was open for 17% -> 5% of each run, Pallas kernels for 31% -> 27%
where the time goes in v4:
time: 134 us; the launch traced here: 133 us
  Pallas kernels  46 us (34%)
  waiting for transfers between devices  35.7 us (27%)
  starting transfers between devices  34.5 us (26%)
  local copies, waits for them, and re-layouts  8.12 us (6%)
  other arithmetic  5.05 us (4%)
  matrix products  2.38 us (2%)
    ppermute x9, waiting for transfers between devices, swap_with(): lax.ppermute(value, 'lat', [(i, partner(i, turn, count)) for i in range(c...  18.9 us
    pallas_call x3, Pallas kernels, legendre_table(): pl.pallas_call(functools.partial(legendre_kernel, start_block), grid=(DEG...  18.7 us
    pallas_call x1, Pallas kernels, synthesis(): pl.pallas_call(functools.partial(synthesis_kernel, lon_total, lat_total,...  17.1 us
    ppermute x9, starting transfers between devices, swap_with(): lax.ppermute(value, 'lat', [(i, partner(i, turn, count)) for i in range(c...  13.2 us
    pallas_call x1, Pallas kernels, grid_part(): pl.pallas_call(functools.partial(grid_kernel, lon_count), in_specs=[pl.Bl...  10.2 us
    all_to_all x1, waiting for transfers between devices, on_device(): lax.all_to_all(lon_sent, 'lon', split_axis=0, concat_axis=0, tiled=True)  8.21 us
    all_to_all x1, waiting for transfers between devices, on_device(): lax.all_to_all(packed, 'lon', split_axis=0, concat_axis=0, tiled=True)  6.62 us
    ppermute x2, starting transfers between devices, swap_edges(): lax.ppermute(lax.slice_in_dim(shard, 0, width, axis=dim), axis, down)  5.39 us
  transfers between devices with their start and end apart: 16, of which 9 were waited for; matrix products, arithmetic and copies ran while one was open for 5% of the time, Pallas kernels for 27%

profile of v4, /device:TPU:0, one launch (start us, length us, event | category | flops | bytes accessed | tf_op | source)
XLA Modules:
  0.0 132.6 jit_solution(6246677272688392451)
XLA Ops:
  0.6 1.1 constant_dynamic-update-slice_fusion.1
  1.7 1.1 constant_dynamic-update-slice_fusion
  2.8 0.5 collective-permute-start
  3.3 4.1 %collective-permute-start.1 = (bf16[24,8,768]{2,1,0:T(8,128)(2,1)S(1)}, bf16[24,8,768]{2,1,0:T(8,128)(2,1)S(1)}, u32[]{:S(2)}, u32[]{:S(2)}) collective-permute-start(bf16[24,8,768]{2,1,0:T(8,128)(2,1)S(1)} %get-tuple-element.82), channel_id=1, source_target_pairs={{1,0},{2,1},{3,2},{4,3},{5,4},{6,5},{7,6},{0,7},{9,8},{10,9},{11,1... | collective-permute-start | bytes 884744 | tf_op jit(solution)/shard_map/ppermute | solution.py:311
  7.6 0.6 pad_bitcast_fusion.cos_ref
  8.1 0.3 reduce-window.9
  8.4 0.1 slice.24
  8.6 0.1 slice_reduce_fusion
  8.7 0.1 add_bitcast_fusion
  8.8 0.1 fusion.9
  8.8 0.1 dynamic_slice.25
  8.9 0.1 multiply_add_fusion
  9.0 0.6 pad.23.scale_in
  9.6 0.6 broadcast_in_dim.14.prev_in.early_in
  10.3 6.2 %legendre_table.3 = (bf16[96,128,128]{2,1,0:T(8,128)(2,1)}, f32[96,128]{1,0:T(8,128)}, f32[96,128]{1,0:T(8,128)}, f32[96,128]{1,0:T(8,128)}) custom-call(s32[1]{0:T(128)} %bitcast.2.first_ref, f32[1,128]{1,0:T(1,128)} %pad_bitcast_fusion.cos_ref, f32[96,128]{1,0:T(8,128)} %broadcast_in_dim.14.prev_in.early_in, f32[96,128]{1,0:T(8,128)} %broadcast_in_dim.14.prev_in.early_in, ...), custom_call_target="tpu_custom_call" | custom-call | flops 7864320000 | bytes 3145728 | tf_op jit(solution)/shard_map/legendre_table/pallas_call | solution.py:121
  16.5 0.1 copy.11
  16.7 0.1 copy.12
  16.7 0.6 fusion.8.tap_ref
  17.4 0.6 pad_dynamic-slice_fusion.shift_ref
  18.0 0.0 collective-permute-done
  18.0 0.0 collective-permute-done.1
  18.0 1.3 collective-permute-start.3
  19.3 4.5 %collective-permute-start.2 = (bf16[1,48,768]{2,1,0:T(8,128)(2,1)S(1)}, bf16[1,48,768]{2,1,0:T(8,128)(2,1)S(1)}, u32[]{:S(2)}, u32[]{:S(2)}) collective-permute-start(bf16[1,48,768]{2,1,0:T(8,128)(2,1)S(1)} %get-tuple-element.73), channel_id=1, source_target_pairs={{0,8},{8,16},{16,24},{1,9},{9,17},{17,25},{2,10},{10,18},{18,26},{... | collective-permute-start | bytes 221192 | tf_op jit(solution)/shard_map/ppermute | solution.py:310
  23.9 0.4 collective-permute-done.3
  24.3 1.6 %collective-permute-done.2 = bf16[1,48,768]{2,1,0:T(8,128)(2,1)S(1)} collective-permute-done((bf16[1,48,768]{2,1,0:T(8,128)(2,1)S(1)}, bf16[1,48,768]{2,1,0:T(8,128)(2,1)S(1)}, u32[]{:S(2)}, u32[]{:S(2)}) %collective-permute-start.2) | collective-permute-done | bytes 73760 | tf_op jit(solution)/shard_map/ppermute | solution.py:310
  25.9 1.4 %pad_maximum_fusion = bf16[26,48,768]{2,1,0:T(8,128)(2,1)} fusion(bf16[1,48,768]{2,1,0:T(8,128)(2,1)S(1)} %collective-permute-done.3, bf16[24,8,768]{2,1,0:T(8,128)(2,1)S(1)} %broadcast_in_dim.28, bf16[24,8,768]{2,1,0:T(8,128)(2,1)S(1)} %collective-permute-done.1, bf16[24,24,768]{2,1,0:T(8,128)(2,1)S(1)} %constant_dynamic-update-slice_fusion, ...), kind=kLoop, calls=%fused_computation.1 | loop fusion | flops 11501568 | bytes 3833856 | tf_op jit(solution)/shard_map/concatenate | solution.py:370
  27.2 10.2 %grid_part.1 = (bf16[576,1152]{1,0:T(8,128)(2,1)}, bf16[576,384]{1,0:T(8,128)(2,1)}, bf16[8,24,1152]{2,1,0:T(8,128)(2,1)}) custom-call(bf16[1248,768]{1,0:T(8,128)(2,1)} %bitcast.43, bf16[576,384]{1,0:T(8,128)(2,1)} %bitcast.44, bf16[3,384,384]{2,1,0:T(8,128)(2,1)} %weight_ref.1, f32[26,72]{1,0:T(8,128)} %fusion.8.tap_ref, ...), custom_call_target="tpu_custom_call" | custom-call | tf_op jit(solution)/shard_map/grid_part/pallas_call | solution.py:287
  37.4 2.4 %fusion.14 = (bf16[1152,384]{1,0:T(8,128)(2,1)S(1)}, f32[1152,384]{1,0:T(8,128)S(1)}) fusion(bf16[576,1152]{1,0:T(8,128)(2,1)} %get-tuple-element.64, bf16[576,384]{1,0:T(8,128)(2,1)S(1)} %bitcast.45), kind=kOutput, calls=%fused_computation.50 | convolution fusion | flops 510492672 | bytes 4423680 | tf_op jit(solution)/shard_map/dot_general | solution.py:381
  39.8 0.1 dynamic-slice_bitcast_fusion.2
  39.9 3.8 %collective-permute-start.9 = (bf16[288,384]{1,0:T(8,128)(2,1)S(1)}, bf16[288,384]{1,0:T(8,128)(2,1)S(1)}, u32[]{:S(2)}, u32[]{:S(2)}) collective-permute-start(bf16[288,384]{1,0:T(8,128)(2,1)S(1)} %get-tuple-element.80), channel_id=1, source_target_pairs={{0,24},{8,16},{16,8},{24,0},{1,25},{9,17},{17,9},{25,1},{2,26},{10... | collective-permute-start | bytes 663560 | tf_op jit(solution)/shard_map/ppermute | solution.py:328
  43.8 0.9 collective-permute-start.8
  44.7 1.4 %collective-permute-start.7 = (bf16[288,384]{1,0:T(8,128)(2,1)S(1)}, bf16[288,384]{1,0:T(8,128)(2,1)S(1)}, u32[]{:S(2)}, u32[]{:S(2)}) collective-permute-start(bf16[288,384]{1,0:T(8,128)(2,1)S(1)} %get-tuple-element.79), channel_id=1, source_target_pairs={{0,8},{8,0},{16,24},{24,16},{1,9},{9,1},{17,25},{25,17},{2,10},{10... | collective-permute-start | bytes 663560 | tf_op jit(solution)/shard_map/ppermute | solution.py:328
  46.1 3.3 %collective-permute-done.9 = bf16[288,384]{1,0:T(8,128)(2,1)S(1)} collective-permute-done((bf16[288,384]{1,0:T(8,128)(2,1)S(1)}, bf16[288,384]{1,0:T(8,128)(2,1)S(1)}, u32[]{:S(2)}, u32[]{:S(2)}) %collective-permute-start.9) | collective-permute-done | bytes 221216 | tf_op jit(solution)/shard_map/ppermute | solution.py:328
  49.4 1.7 %collective-permute-done.8 = bf16[288,384]{1,0:T(8,128)(2,1)S(1)} collective-permute-done((bf16[288,384]{1,0:T(8,128)(2,1)S(1)}, bf16[288,384]{1,0:T(8,128)(2,1)S(1)}, u32[]{:S(2)}, u32[]{:S(2)}) %collective-permute-start.8) | collective-permute-done | bytes 221216 | tf_op jit(solution)/shard_map/ppermute | solution.py:328
  51.1 1.9 %collective-permute-done.7 = bf16[288,384]{1,0:T(8,128)(2,1)S(1)} collective-permute-done((bf16[288,384]{1,0:T(8,128)(2,1)S(1)}, bf16[288,384]{1,0:T(8,128)(2,1)S(1)}, u32[]{:S(2)}, u32[]{:S(2)}) %collective-permute-start.7) | collective-permute-done | bytes 221216 | tf_op jit(solution)/shard_map/ppermute | solution.py:328
  52.9 0.1 fusion.2
  53.1 0.7 reshape.177
  53.8 3.8 %all-to-all-start.1 = ((bf16[8,36,384]{2,1,0:T(8,128)(2,1)}), bf16[8,36,384]{2,1,0:T(8,128)(2,1)S(1)}, u32[]{:S(2)}, u32[]{:S(2)}) async-start(bf16[8,36,384]{2,1,0:T(8,128)(2,1)} %reshape.177), calls=%async_computation.1 | async-start | bytes 491520 | tf_op jit(solution)/shard_map/all_to_all | solution.py:409
  57.6 0.5 cosine_convert_fusion
  58.1 0.7 pad_maximum_fusion.1
  58.8 8.2 %all-to-all-done.1 = bf16[8,36,384]{2,1,0:T(8,128)(2,1)S(1)} async-done(((bf16[8,36,384]{2,1,0:T(8,128)(2,1)}), bf16[8,36,384]{2,1,0:T(8,128)(2,1)S(1)}, u32[]{:S(2)}, u32[]{:S(2)}) %all-to-all-start.1) | async-done | bytes 221216 | tf_op jit(solution)/shard_map/all_to_all | solution.py:409
  67.0 3.5 %all-to-all-start = ((bf16[8,24,1152]{2,1,0:T(8,128)(2,1)}), bf16[8,24,1152]{2,1,0:T(8,128)(2,1)S(1)}, u32[]{:S(2)}, u32[]{:S(2)}) async-start(bf16[8,24,1152]{2,1,0:T(8,128)(2,1)} %get-tuple-element.50), calls=%async_computation | async-start | bytes 884736 | tf_op jit(solution)/shard_map/all_to_all | solution.py:396
  70.5 0.7 pad_add_fusion.refs_0_
  71.1 6.2 %legendre_table.4 = (bf16[96,128,128]{2,1,0:T(8,128)(2,1)}, f32[96,128]{1,0:T(8,128)}, f32[96,128]{1,0:T(8,128)}, f32[96,128]{1,0:T(8,128)}) custom-call(s32[1]{0:T(128)} %bitcast.2.first_ref, f32[1,128]{1,0:T(1,128)} %pad_bitcast_fusion.cos_ref, f32[96,128]{1,0:T(8,128)} %get-tuple-element.51.prev_in, f32[96,128]{1,0:T(8,128)} %get-tuple-element.52.early_in, ...), custom_call_target="tpu_custom_call" | custom-call | flops 7864320000 | bytes 3145728 | tf_op jit(solution)/shard_map/legendre_table/pallas_call | solution.py:121
  77.4 6.6 %all-to-all-done = bf16[8,24,1152]{2,1,0:T(8,128)(2,1)S(1)} async-done(((bf16[8,24,1152]{2,1,0:T(8,128)(2,1)}), bf16[8,24,1152]{2,1,0:T(8,128)(2,1)S(1)}, u32[]{:S(2)}, u32[]{:S(2)}) %all-to-all-start) | async-done | bytes 442400 | tf_op jit(solution)/shard_map/all_to_all | solution.py:396
  84.0 0.8 broadcast_in_dim.29
  84.8 3.6 %all-to-all-start.2 = ((bf16[8,36,384]{2,1,0:T(8,128)(2,1)}), bf16[8,36,384]{2,1,0:T(8,128)(2,1)S(1)}, u32[]{:S(2)}, u32[]{:S(2)}) async-start(bf16[8,36,384]{2,1,0:T(8,128)(2,1)} %broadcast_in_dim.29), calls=%async_computation.2 | async-start | bytes 491520 | tf_op jit(solution)/shard_map/all_to_all | solution.py:413
  88.4 0.3 collective-permute-start.4
  88.7 1.4 %collective-permute-start.5 = (bf16[192,1152]{1,0:T(8,128)(2,1)S(1)}, bf16[192,1152]{1,0:T(8,128)(2,1)S(1)}, u32[]{:S(2)}, u32[]{:S(2)}) collective-permute-start(bf16[192,1152]{1,0:T(8,128)(2,1)S(1)} %bitcast.49), channel_id=1, source_target_pairs={{0,16},{8,24},{16,0},{24,8},{1,17},{9,25},{17,1},{25,9},{2,18},{10... | collective-permute-start | bytes 1327112 | tf_op jit(solution)/shard_map/ppermute | solution.py:328
  90.2 1.8 %collective-permute-start.6 = (bf16[192,1152]{1,0:T(8,128)(2,1)S(1)}, bf16[192,1152]{1,0:T(8,128)(2,1)S(1)}, u32[]{:S(2)}, u32[]{:S(2)}) collective-permute-start(bf16[192,1152]{1,0:T(8,128)(2,1)S(1)} %bitcast.50), channel_id=1, source_target_pairs={{0,24},{8,16},{16,8},{24,0},{1,25},{9,17},{17,9},{25,1},{2,26},{10... | collective-permute-start | bytes 1327112 | tf_op jit(solution)/shard_map/ppermute | solution.py:328
  91.9 6.2 %legendre_table.5 = (bf16[96,128,128]{2,1,0:T(8,128)(2,1)}, f32[96,128]{1,0:T(8,128)}, f32[96,128]{1,0:T(8,128)}, f32[96,128]{1,0:T(8,128)}) custom-call(s32[1]{0:T(128)} %bitcast.2.first_ref, f32[1,128]{1,0:T(1,128)} %pad_bitcast_fusion.cos_ref, f32[96,128]{1,0:T(8,128)} %get-tuple-element.60.prev_in, f32[96,128]{1,0:T(8,128)} %get-tuple-element.61.early_in, ...), custom_call_target="tpu_custom_call" | custom-call | flops 7864320000 | bytes 3145728 | tf_op jit(solution)/shard_map/legendre_table/pallas_call | solution.py:121
  98.2 0.0 all-to-all-done.2
  98.2 3.3 %collective-permute-done.4.refs_3_ = bf16[192,1152]{1,0:T(8,128)(2,1)S(1)} collective-permute-done((bf16[192,1152]{1,0:T(8,128)(2,1)S(1)}, bf16[192,1152]{1,0:T(8,128)(2,1)S(1)}, u32[]{:S(2)}, u32[]{:S(2)}) %collective-permute-start.4) | collective-permute-done | bytes 442400 | tf_op jit(solution)/shard_map/ppermute | solution.py:328
  101.5 0.0 collective-permute-done.5.refs_4_
  101.5 8.7 %collective-permute-done.6.refs_5_ = bf16[192,1152]{1,0:T(8,128)(2,1)S(1)} collective-permute-done((bf16[192,1152]{1,0:T(8,128)(2,1)S(1)}, bf16[192,1152]{1,0:T(8,128)(2,1)S(1)}, u32[]{:S(2)}, u32[]{:S(2)}) %collective-permute-start.6) | collective-permute-done | bytes 442400 | tf_op jit(solution)/shard_map/ppermute | solution.py:328
  110.2 1.8 %collective-permute-start.10 = (bf16[8,36,384]{2,1,0:T(8,128)(2,1)S(1)}, bf16[8,36,384]{2,1,0:T(8,128)(2,1)S(1)}, u32[]{:S(2)}, u32[]{:S(2)}) collective-permute-start(bf16[8,36,384]{2,1,0:T(8,128)(2,1)S(1)} %all-to-all-done.2), channel_id=1, source_target_pairs={{0,24},{8,16},{16,8},{24,0},{1,25},{9,17},{17,9},{25,1},{2,26},{10... | collective-permute-start | bytes 663560 | tf_op jit(solution)/shard_map/ppermute | solution.py:328
  112.0 1.4 %collective-permute-start.11 = (bf16[8,36,384]{2,1,0:T(8,128)(2,1)S(1)}, bf16[8,36,384]{2,1,0:T(8,128)(2,1)S(1)}, u32[]{:S(2)}, u32[]{:S(2)}) collective-permute-start(bf16[8,36,384]{2,1,0:T(8,128)(2,1)S(1)} %all-to-all-done.2), channel_id=1, source_target_pairs={{0,16},{8,24},{16,0},{24,8},{1,17},{9,25},{17,1},{25,9},{2,18},{10... | collective-permute-start | bytes 663560 | tf_op jit(solution)/shard_map/ppermute | solution.py:328
  113.4 0.3 collective-permute-start.12
  113.7 17.1 %dft_synthesis.1 = f32[2,96,48,384]{3,2,1,0:T(8,128)} custom-call(s32[4]{0:T(128)} %pad_add_fusion.refs_0_, bf16[192,192]{1,0:T(8,128)(2,1)} %bitcast.52, bf16[192,1152]{1,0:T(8,128)(2,1)} %bitcast.51, bf16[192,1152]{1,0:T(8,128)(2,1)} %copy-done.5, bf16[192,1152]{1,0:T(8,128)(2,1)} %copy-done.6, bf16[192,1152]{1,0:T(8,128)(2,1)} %copy-done.7, ...), custom_call_target="tpu_custom_call" | custom-call | flops 20000000000 | bytes 14155776 | tf_op jit(solution)/shard_map/dft_synthesis/pallas_call | solution.py:190
  130.8 0.0 collective-permute-done.10
  130.8 0.0 collective-permute-done.11
  130.8 0.2 select_bitcast_fusion.3
  131.0 0.2 maximum_convert_fusion
  131.2 1.4 %reshape.181 = f32[3,384,384]{2,1,0:T(8,128)} reshape(f32[4,8,36,384]{3,2,1,0:T(8,128)S(1)} %maximum_convert_fusion) | data formatting | bytes 3538944 | tf_op jit(solution)/shard_map/reshape | solution.py:433
  (28 shorter events, 0.3 us)
Async XLA Ops:
  2.8 15.2 %collective-permute-start = (bf16[24,8,768]{2,1,0:T(8,128)(2,1)S(1)}, bf16[24,8,768]{2,1,0:T(8,128)(2,1)S(1)}, u32[]{:S(2)}, u32[]{:S(2)}) collective-permute-start(bf16[24,8,768]{2,1,0:T(8,128)(2,1)S(1)} %get-tuple-element.83), channel_id=1, source_target_pairs={{0,1},{1,2},{2,3},{3,4},{4,5},{5,6},{6,7},{7,0},{8,9},{9,10},{10,1... | collective-permute-start | bytes 884744 | tf_op jit(solution)/shard_map/ppermute | solution.py:310
  3.3 14.7 %collective-permute-start.1 = (bf16[24,8,768]{2,1,0:T(8,128)(2,1)S(1)}, bf16[24,8,768]{2,1,0:T(8,128)(2,1)S(1)}, u32[]{:S(2)}, u32[]{:S(2)}) collective-permute-start(bf16[24,8,768]{2,1,0:T(8,128)(2,1)S(1)} %get-tuple-element.82), channel_id=1, source_target_pairs={{1,0},{2,1},{3,2},{4,3},{5,4},{6,5},{7,6},{0,7},{9,8},{10,9},{11,1... | collective-permute-start | bytes 884744 | tf_op jit(solution)/shard_map/ppermute | solution.py:311
  10.3 6.3 %copy-start.2 = (f32[96,3,3,8]{0,3,2,1:T(8,128)S(1)}, f32[96,3,3,8]{0,3,2,1:T(8,128)}, u32[]{:S(2)}) copy-start(f32[96,3,3,8]{0,3,2,1:T(8,128)} %param.9) | copy-start | bytes 82948
  10.3 6.3 %copy-start.4 = (s32[96]{0:T(128)S(1)}, s32[96]{0:T(128)}, u32[]{:S(2)}) copy-start(s32[96]{0:T(128)} %param.11) | copy-start | bytes 1156
  10.3 6.4 %copy-start.3 = (s32[96,3,8]{0,2,1:T(8,128)S(1)}, s32[96,3,8]{0,2,1:T(8,128)}, u32[]{:S(2)}) copy-start(s32[96,3,8]{0,2,1:T(8,128)} %param.10) | copy-start | bytes 27652
  18.0 6.2 %collective-permute-start.3 = (bf16[1,48,768]{2,1,0:T(8,128)(2,1)S(1)}, bf16[1,48,768]{2,1,0:T(8,128)(2,1)S(1)}, u32[]{:S(2)}, u32[]{:S(2)}) collective-permute-start(bf16[1,48,768]{2,1,0:T(8,128)(2,1)S(1)} %get-tuple-element.74), channel_id=1, source_target_pairs={{8,0},{16,8},{24,16},{9,1},{17,9},{25,17},{10,2},{18,10},{26,18},{... | collective-permute-start | bytes 221192 | tf_op jit(solution)/shard_map/ppermute | solution.py:311
  19.3 6.5 %collective-permute-start.2 = (bf16[1,48,768]{2,1,0:T(8,128)(2,1)S(1)}, bf16[1,48,768]{2,1,0:T(8,128)(2,1)S(1)}, u32[]{:S(2)}, u32[]{:S(2)}) collective-permute-start(bf16[1,48,768]{2,1,0:T(8,128)(2,1)S(1)} %get-tuple-element.73), channel_id=1, source_target_pairs={{0,8},{8,16},{16,24},{1,9},{9,17},{17,25},{2,10},{10,18},{18,26},{... | collective-permute-start | bytes 221192 | tf_op jit(solution)/shard_map/ppermute | solution.py:310
  27.2 10.2 %copy-start = (bf16[24,24,384]{2,1,0:T(8,128)(2,1)S(1)}, bf16[24,24,384]{2,1,0:T(8,128)(2,1)}, u32[]{:S(2)}) copy-start(bf16[24,24,384]{2,1,0:T(8,128)(2,1)} %param.7) | copy-start | bytes 1327108
  39.9 9.4 %collective-permute-start.9 = (bf16[288,384]{1,0:T(8,128)(2,1)S(1)}, bf16[288,384]{1,0:T(8,128)(2,1)S(1)}, u32[]{:S(2)}, u32[]{:S(2)}) collective-permute-start(bf16[288,384]{1,0:T(8,128)(2,1)S(1)} %get-tuple-element.80), channel_id=1, source_target_pairs={{0,24},{8,16},{16,8},{24,0},{1,25},{9,17},{17,9},{25,1},{2,26},{10... | collective-permute-start | bytes 663560 | tf_op jit(solution)/shard_map/ppermute | solution.py:328
  43.8 7.3 %collective-permute-start.8 = (bf16[288,384]{1,0:T(8,128)(2,1)S(1)}, bf16[288,384]{1,0:T(8,128)(2,1)S(1)}, u32[]{:S(2)}, u32[]{:S(2)}) collective-permute-start(bf16[288,384]{1,0:T(8,128)(2,1)S(1)} %get-tuple-element.81), channel_id=1, source_target_pairs={{0,16},{8,24},{16,0},{24,8},{1,17},{9,25},{17,1},{25,9},{2,18},{10... | collective-permute-start | bytes 663560 | tf_op jit(solution)/shard_map/ppermute | solution.py:328
  44.7 8.2 %collective-permute-start.7 = (bf16[288,384]{1,0:T(8,128)(2,1)S(1)}, bf16[288,384]{1,0:T(8,128)(2,1)S(1)}, u32[]{:S(2)}, u32[]{:S(2)}) collective-permute-start(bf16[288,384]{1,0:T(8,128)(2,1)S(1)} %get-tuple-element.79), channel_id=1, source_target_pairs={{0,8},{8,0},{16,24},{24,16},{1,9},{9,1},{17,25},{25,17},{2,10},{10... | collective-permute-start | bytes 663560 | tf_op jit(solution)/shard_map/ppermute | solution.py:328
  53.8 13.2 %all-to-all-start.1 = ((bf16[8,36,384]{2,1,0:T(8,128)(2,1)}), bf16[8,36,384]{2,1,0:T(8,128)(2,1)S(1)}, u32[]{:S(2)}, u32[]{:S(2)}) async-start(bf16[8,36,384]{2,1,0:T(8,128)(2,1)} %reshape.177), calls=%async_computation.1 | async-start | bytes 491520 | tf_op jit(solution)/shard_map/all_to_all | solution.py:409
  67.0 17.0 %all-to-all-start = ((bf16[8,24,1152]{2,1,0:T(8,128)(2,1)}), bf16[8,24,1152]{2,1,0:T(8,128)(2,1)S(1)}, u32[]{:S(2)}, u32[]{:S(2)}) async-start(bf16[8,24,1152]{2,1,0:T(8,128)(2,1)} %get-tuple-element.50), calls=%async_computation | async-start | bytes 884736 | tf_op jit(solution)/shard_map/all_to_all | solution.py:396
  84.0 14.1 %copy-start.1 = (bf16[8,24,1152]{2,1,0:T(8,128)(2,1)}, bf16[8,24,1152]{2,1,0:T(8,128)(2,1)S(1)}, u32[]{:S(2)}) copy-start(bf16[8,24,1152]{2,1,0:T(8,128)(2,1)S(1)} %all-to-all-done) | copy-start | bytes 1327108
  84.8 13.4 %all-to-all-start.2 = ((bf16[8,36,384]{2,1,0:T(8,128)(2,1)}), bf16[8,36,384]{2,1,0:T(8,128)(2,1)S(1)}, u32[]{:S(2)}, u32[]{:S(2)}) async-start(bf16[8,36,384]{2,1,0:T(8,128)(2,1)} %broadcast_in_dim.29), calls=%async_computation.2 | async-start | bytes 491520 | tf_op jit(solution)/shard_map/all_to_all | solution.py:413
  88.4 13.1 %collective-permute-start.4 = (bf16[192,1152]{1,0:T(8,128)(2,1)S(1)}, bf16[192,1152]{1,0:T(8,128)(2,1)S(1)}, u32[]{:S(2)}, u32[]{:S(2)}) collective-permute-start(bf16[192,1152]{1,0:T(8,128)(2,1)S(1)} %bitcast.48), channel_id=1, source_target_pairs={{0,8},{8,0},{16,24},{24,16},{1,9},{9,1},{17,25},{25,17},{2,10},{10... | collective-permute-start | bytes 1327112 | tf_op jit(solution)/shard_map/ppermute | solution.py:328
  88.7 12.7 %collective-permute-start.5 = (bf16[192,1152]{1,0:T(8,128)(2,1)S(1)}, bf16[192,1152]{1,0:T(8,128)(2,1)S(1)}, u32[]{:S(2)}, u32[]{:S(2)}) collective-permute-start(bf16[192,1152]{1,0:T(8,128)(2,1)S(1)} %bitcast.49), channel_id=1, source_target_pairs={{0,16},{8,24},{16,0},{24,8},{1,17},{9,25},{17,1},{25,9},{2,18},{10... | collective-permute-start | bytes 1327112 | tf_op jit(solution)/shard_map/ppermute | solution.py:328
  90.2 20.0 %collective-permute-start.6 = (bf16[192,1152]{1,0:T(8,128)(2,1)S(1)}, bf16[192,1152]{1,0:T(8,128)(2,1)S(1)}, u32[]{:S(2)}, u32[]{:S(2)}) collective-permute-start(bf16[192,1152]{1,0:T(8,128)(2,1)S(1)} %bitcast.50), channel_id=1, source_target_pairs={{0,24},{8,16},{16,8},{24,0},{1,25},{9,17},{17,9},{25,1},{2,26},{10... | collective-permute-start | bytes 1327112 | tf_op jit(solution)/shard_map/ppermute | solution.py:328
  101.5 12.2 %copy-start.5 = (bf16[192,1152]{1,0:T(8,128)(2,1)}, bf16[192,1152]{1,0:T(8,128)(2,1)S(1)}, u32[]{:S(2)}) copy-start(bf16[192,1152]{1,0:T(8,128)(2,1)S(1)} %collective-permute-done.4.refs_3_) | copy-start | bytes 1327108
  101.5 12.2 %copy-start.6 = (bf16[192,1152]{1,0:T(8,128)(2,1)}, bf16[192,1152]{1,0:T(8,128)(2,1)S(1)}, u32[]{:S(2)}) copy-start(bf16[192,1152]{1,0:T(8,128)(2,1)S(1)} %collective-permute-done.5.refs_4_) | copy-start | bytes 1327108
  110.2 3.5 %copy-start.7 = (bf16[192,1152]{1,0:T(8,128)(2,1)}, bf16[192,1152]{1,0:T(8,128)(2,1)S(1)}, u32[]{:S(2)}) copy-start(bf16[192,1152]{1,0:T(8,128)(2,1)S(1)} %collective-permute-done.6.refs_5_) | copy-start | bytes 1327108
  110.2 20.6 %collective-permute-start.10 = (bf16[8,36,384]{2,1,0:T(8,128)(2,1)S(1)}, bf16[8,36,384]{2,1,0:T(8,128)(2,1)S(1)}, u32[]{:S(2)}, u32[]{:S(2)}) collective-permute-start(bf16[8,36,384]{2,1,0:T(8,128)(2,1)S(1)} %all-to-all-done.2), channel_id=1, source_target_pairs={{0,24},{8,16},{16,8},{24,0},{1,25},{9,17},{17,9},{25,1},{2,26},{10... | collective-permute-start | bytes 663560 | tf_op jit(solution)/shard_map/ppermute | solution.py:328
  112.0 18.8 %collective-permute-start.11 = (bf16[8,36,384]{2,1,0:T(8,128)(2,1)S(1)}, bf16[8,36,384]{2,1,0:T(8,128)(2,1)S(1)}, u32[]{:S(2)}, u32[]{:S(2)}) collective-permute-start(bf16[8,36,384]{2,1,0:T(8,128)(2,1)S(1)} %all-to-all-done.2), channel_id=1, source_target_pairs={{0,16},{8,24},{16,0},{24,8},{1,17},{9,25},{17,1},{25,9},{2,18},{10... | collective-permute-start | bytes 663560 | tf_op jit(solution)/shard_map/ppermute | solution.py:328
  113.4 17.4 %collective-permute-start.12 = (bf16[8,36,384]{2,1,0:T(8,128)(2,1)S(1)}, bf16[8,36,384]{2,1,0:T(8,128)(2,1)S(1)}, u32[]{:S(2)}, u32[]{:S(2)}) collective-permute-start(bf16[8,36,384]{2,1,0:T(8,128)(2,1)S(1)} %all-to-all-done.2), channel_id=1, source_target_pairs={{0,8},{8,0},{16,24},{24,16},{1,9},{9,1},{17,25},{25,17},{2,10},{10... | collective-permute-start | bytes 663560 | tf_op jit(solution)/shard_map/ppermute | solution.py:328

commit v5 on v4

--- a/solution.py
+++ b/solution.py
@@ -382,19 +382,19 @@
         response, cot_flat, (((0,), (0,)), ((), ())), preferred_element_type=jnp.float32
     ) * (1.0 / math.sqrt(total_lat * total_lon))
     mix_rows = K * channels
+    arrived = []
     split_sum = mix_rows % (lat_count * lon_count) == 0
     if split_sum:
         mix_sent = mix_local.astype(jnp.bfloat16).reshape(lat_count, mix_rows // lat_count, channels)
         lat_share = lax.dynamic_index_in_dim(
             mix_local.reshape(lat_count, mix_rows // lat_count, channels), lat_pos, 0, keepdims=False
         )
-        arrived = []
         for turn in range(1, lat_count):
             piece = lax.dynamic_index_in_dim(mix_sent, partner(lat_pos, turn, lat_count), 0, keepdims=False)
             arrived.append(swap_with(piece, turn, lat_count))
 
     columns = lax.all_to_all(packed, "lon", split_axis=0, concat_axis=0, tiled=True)
-    columns, state = lax.optimization_barrier((columns, state))
+    columns, state, arrived = lax.optimization_barrier((columns, state, arrived))
     state = next_table(state)
     columns = columns.reshape(total_lon, lat_dev * chans)
     gathered, bands = [columns], [lat_pos]

time: 134 us -> 113 us (0.84)
  waiting for transfers between devices: 35.7 us -> 14.4 us
    ppermute x9, waiting for transfers between devices: 18.9 us -> 8.37 us  [swap_with(): lax.ppermute(value, 'lat', [(i, partner(i, turn, count)) for i in range(c...]
    all_to_all x1, waiting for transfers between devices: 6.62 us -> 0.01 us  [on_device(): lax.all_to_all(packed, 'lon', split_axis=0, concat_axis=0, tiled=True)]
    all_to_all x1, waiting for transfers between devices: 8.21 us -> 4.07 us  [on_device(): lax.all_to_all(lon_sent, 'lon', split_axis=0, concat_axis=0, tiled=True)]
  transfers between devices with their start and end apart: 16 -> 16, of which waited for: 9 -> 6; matrix products, arithmetic and copies ran while one was open for 5% -> 8% of each run, Pallas kernels for 27% -> 32%
where the time goes in v5:
time: 113 us; the launch traced here: 112 us
  Pallas kernels  46.1 us (41%)
  starting transfers between devices  35.5 us (31%)
  waiting for transfers between devices  14.4 us (13%)
  local copies, waits for them, and re-layouts  8.11 us (7%)
  other arithmetic  5.04 us (4%)
  matrix products  2.38 us (2%)
    pallas_call x3, Pallas kernels, legendre_table(): pl.pallas_call(functools.partial(legendre_kernel, start_block), grid=(DEG...  18.7 us
    pallas_call x1, Pallas kernels, synthesis(): pl.pallas_call(functools.partial(synthesis_kernel, lon_total, lat_total,...  17.1 us
    ppermute x9, starting transfers between devices, swap_with(): lax.ppermute(value, 'lat', [(i, partner(i, turn, count)) for i in range(c...  13.2 us
    pallas_call x1, Pallas kernels, grid_part(): pl.pallas_call(functools.partial(grid_kernel, lon_count), in_specs=[pl.Bl...  10.2 us
    ppermute x9, waiting for transfers between devices, swap_with(): lax.ppermute(value, 'lat', [(i, partner(i, turn, count)) for i in range(c...  8.37 us
    ppermute x2, starting transfers between devices, swap_edges(): lax.ppermute(lax.slice_in_dim(shard, 0, width, axis=dim), axis, down)  5.39 us
    ppermute x2, starting transfers between devices, swap_edges(): lax.ppermute(lax.slice_in_dim(shard, length - width, length, axis=dim), a...  5.05 us
    all_to_all x1, starting transfers between devices, on_device(): lax.all_to_all(lon_sent, 'lon', split_axis=0, concat_axis=0, tiled=True)  4.78 us
  transfers between devices with their start and end apart: 16, of which 6 were waited for; matrix products, arithmetic and copies ran while one was open for 8% of the time, Pallas kernels for 32%

profile of v5, /device:TPU:0, one launch (start us, length us, event | category | flops | bytes accessed | tf_op | source)
XLA Modules:
  0.0 112.4 jit_solution(996206093087396156)
XLA Ops:
  0.6 1.1 constant_dynamic-update-slice_fusion.1
  1.7 1.1 constant_dynamic-update-slice_fusion
  2.8 0.5 collective-permute-start
  3.3 4.1 %collective-permute-start.1 = (bf16[24,8,768]{2,1,0:T(8,128)(2,1)S(1)}, bf16[24,8,768]{2,1,0:T(8,128)(2,1)S(1)}, u32[]{:S(2)}, u32[]{:S(2)}) collective-permute-start(bf16[24,8,768]{2,1,0:T(8,128)(2,1)S(1)} %get-tuple-element.88), channel_id=1, source_target_pairs={{1,0},{2,1},{3,2},{4,3},{5,4},{6,5},{7,6},{0,7},{9,8},{10,9},{11,1... | collective-permute-start | bytes 884744 | tf_op jit(solution)/shard_map/ppermute | solution.py:311
  7.6 0.6 pad_bitcast_fusion.cos_ref
  8.1 0.3 reduce-window.9
  8.4 0.1 slice.24
  8.6 0.1 slice_reduce_fusion
  8.7 0.1 add_bitcast_fusion
  8.8 0.1 fusion.9
  8.8 0.1 dynamic_slice.25
  8.9 0.1 multiply_add_fusion
  9.0 0.6 pad.23.scale_in
  9.6 0.6 broadcast_in_dim.14.prev_in.early_in
  10.3 6.2 %legendre_table.3 = (bf16[96,128,128]{2,1,0:T(8,128)(2,1)}, f32[96,128]{1,0:T(8,128)}, f32[96,128]{1,0:T(8,128)}, f32[96,128]{1,0:T(8,128)}) custom-call(s32[1]{0:T(128)} %bitcast.2.first_ref, f32[1,128]{1,0:T(1,128)} %pad_bitcast_fusion.cos_ref, f32[96,128]{1,0:T(8,128)} %broadcast_in_dim.14.prev_in.early_in, f32[96,128]{1,0:T(8,128)} %broadcast_in_dim.14.prev_in.early_in, ...), custom_call_target="tpu_custom_call" | custom-call | flops 7864320000 | bytes 3145728 | tf_op jit(solution)/shard_map/legendre_table/pallas_call | solution.py:121
  16.6 0.1 copy.11
  16.7 0.1 copy.12
  16.8 0.6 fusion.8.tap_ref
  17.4 0.6 pad_dynamic-slice_fusion.shift_ref
  18.0 0.0 collective-permute-done
  18.0 0.0 collective-permute-done.1
  18.1 1.3 %collective-permute-start.3 = (bf16[1,48,768]{2,1,0:T(8,128)(2,1)S(1)}, bf16[1,48,768]{2,1,0:T(8,128)(2,1)S(1)}, u32[]{:S(2)}, u32[]{:S(2)}) collective-permute-start(bf16[1,48,768]{2,1,0:T(8,128)(2,1)S(1)} %get-tuple-element.80), channel_id=1, source_target_pairs={{8,0},{16,8},{24,16},{9,1},{17,9},{25,17},{10,2},{18,10},{26,18},{... | collective-permute-start | bytes 221192 | tf_op jit(solution)/shard_map/ppermute | solution.py:311
  19.4 4.5 %collective-permute-start.2 = (bf16[1,48,768]{2,1,0:T(8,128)(2,1)S(1)}, bf16[1,48,768]{2,1,0:T(8,128)(2,1)S(1)}, u32[]{:S(2)}, u32[]{:S(2)}) collective-permute-start(bf16[1,48,768]{2,1,0:T(8,128)(2,1)S(1)} %get-tuple-element.79), channel_id=1, source_target_pairs={{0,8},{8,16},{16,24},{1,9},{9,17},{17,25},{2,10},{10,18},{18,26},{... | collective-permute-start | bytes 221192 | tf_op jit(solution)/shard_map/ppermute | solution.py:310
  23.9 0.4 collective-permute-done.3
  24.3 1.6 %collective-permute-done.2 = bf16[1,48,768]{2,1,0:T(8,128)(2,1)S(1)} collective-permute-done((bf16[1,48,768]{2,1,0:T(8,128)(2,1)S(1)}, bf16[1,48,768]{2,1,0:T(8,128)(2,1)S(1)}, u32[]{:S(2)}, u32[]{:S(2)}) %collective-permute-start.2) | collective-permute-done | bytes 73760 | tf_op jit(solution)/shard_map/ppermute | solution.py:310
  25.9 1.4 %pad_maximum_fusion = bf16[26,48,768]{2,1,0:T(8,128)(2,1)} fusion(bf16[1,48,768]{2,1,0:T(8,128)(2,1)S(1)} %collective-permute-done.3, bf16[24,8,768]{2,1,0:T(8,128)(2,1)S(1)} %broadcast_in_dim.28, bf16[24,8,768]{2,1,0:T(8,128)(2,1)S(1)} %collective-permute-done.1, bf16[24,24,768]{2,1,0:T(8,128)(2,1)S(1)} %constant_dynamic-update-slice_fusion, ...), kind=kLoop, calls=%fused_computation.1 | loop fusion | flops 11501568 | bytes 3833856 | tf_op jit(solution)/shard_map/concatenate | solution.py:370
  27.2 10.2 %grid_part.1 = (bf16[576,1152]{1,0:T(8,128)(2,1)}, bf16[576,384]{1,0:T(8,128)(2,1)}, bf16[8,24,1152]{2,1,0:T(8,128)(2,1)}) custom-call(bf16[1248,768]{1,0:T(8,128)(2,1)} %bitcast.43, bf16[576,384]{1,0:T(8,128)(2,1)} %bitcast.44, bf16[3,384,384]{2,1,0:T(8,128)(2,1)} %weight_ref.1, f32[26,72]{1,0:T(8,128)} %fusion.8.tap_ref, ...), custom_call_target="tpu_custom_call" | custom-call | tf_op jit(solution)/shard_map/grid_part/pallas_call | solution.py:287
  37.5 3.5 %all-to-all-start = ((bf16[8,24,1152]{2,1,0:T(8,128)(2,1)}), bf16[8,24,1152]{2,1,0:T(8,128)(2,1)S(1)}, u32[]{:S(2)}, u32[]{:S(2)}) async-start(bf16[8,24,1152]{2,1,0:T(8,128)(2,1)} %get-tuple-element.53), calls=%async_computation | async-start | bytes 884736 | tf_op jit(solution)/shard_map/all_to_all | solution.py:396
  41.0 2.4 %fusion.14 = (bf16[1152,384]{1,0:T(8,128)(2,1)S(1)}, f32[1152,384]{1,0:T(8,128)S(1)}) fusion(bf16[576,1152]{1,0:T(8,128)(2,1)} %get-tuple-element.60, bf16[576,384]{1,0:T(8,128)(2,1)S(1)} %bitcast.45), kind=kOutput, calls=%fused_computation.50 | convolution fusion | flops 510492672 | bytes 4423680 | tf_op jit(solution)/shard_map/dot_general | solution.py:381
  43.4 0.1 dynamic-slice_bitcast_fusion
  43.5 2.9 %collective-permute-start.4 = (bf16[288,384]{1,0:T(8,128)(2,1)S(1)}, bf16[288,384]{1,0:T(8,128)(2,1)S(1)}, u32[]{:S(2)}, u32[]{:S(2)}) collective-permute-start(bf16[288,384]{1,0:T(8,128)(2,1)S(1)} %get-tuple-element.87), channel_id=1, source_target_pairs={{0,8},{8,0},{16,24},{24,16},{1,9},{9,1},{17,25},{25,17},{2,10},{10... | collective-permute-start | bytes 663560 | tf_op jit(solution)/shard_map/ppermute | solution.py:328
  46.3 1.9 %collective-permute-start.5 = (bf16[288,384]{1,0:T(8,128)(2,1)S(1)}, bf16[288,384]{1,0:T(8,128)(2,1)S(1)}, u32[]{:S(2)}, u32[]{:S(2)}) collective-permute-start(bf16[288,384]{1,0:T(8,128)(2,1)S(1)} %get-tuple-element.86), channel_id=1, source_target_pairs={{0,16},{8,24},{16,0},{24,8},{1,17},{9,25},{17,1},{25,9},{2,18},{10... | collective-permute-start | bytes 663560 | tf_op jit(solution)/shard_map/ppermute | solution.py:328
  48.3 1.4 %collective-permute-start.6 = (bf16[288,384]{1,0:T(8,128)(2,1)S(1)}, bf16[288,384]{1,0:T(8,128)(2,1)S(1)}, u32[]{:S(2)}, u32[]{:S(2)}) collective-permute-start(bf16[288,384]{1,0:T(8,128)(2,1)S(1)} %get-tuple-element.85), channel_id=1, source_target_pairs={{0,24},{8,16},{16,8},{24,0},{1,25},{9,17},{17,9},{25,1},{2,26},{10... | collective-permute-start | bytes 663560 | tf_op jit(solution)/shard_map/ppermute | solution.py:328
  49.6 6.2 %legendre_table.4 = (bf16[96,128,128]{2,1,0:T(8,128)(2,1)}, f32[96,128]{1,0:T(8,128)}, f32[96,128]{1,0:T(8,128)}, f32[96,128]{1,0:T(8,128)}) custom-call(s32[1]{0:T(128)} %bitcast.2.first_ref, f32[1,128]{1,0:T(1,128)} %pad_bitcast_fusion.cos_ref, f32[96,128]{1,0:T(8,128)} %get-tuple-element.54.prev_in, f32[96,128]{1,0:T(8,128)} %get-tuple-element.55.early_in, ...), custom_call_target="tpu_custom_call" | custom-call | flops 7864320000 | bytes 3145728 | tf_op jit(solution)/shard_map/legendre_table/pallas_call | solution.py:121
  55.8 0.0 collective-permute-done.4
  55.9 2.4 %collective-permute-done.5 = bf16[288,384]{1,0:T(8,128)(2,1)S(1)} collective-permute-done((bf16[288,384]{1,0:T(8,128)(2,1)S(1)}, bf16[288,384]{1,0:T(8,128)(2,1)S(1)}, u32[]{:S(2)}, u32[]{:S(2)}) %collective-permute-start.5) | collective-permute-done | bytes 221216 | tf_op jit(solution)/shard_map/ppermute | solution.py:328
  58.2 1.8 %collective-permute-done.6 = bf16[288,384]{1,0:T(8,128)(2,1)S(1)} collective-permute-done((bf16[288,384]{1,0:T(8,128)(2,1)S(1)}, bf16[288,384]{1,0:T(8,128)(2,1)S(1)}, u32[]{:S(2)}, u32[]{:S(2)}) %collective-permute-start.6) | collective-permute-done | bytes 221216 | tf_op jit(solution)/shard_map/ppermute | solution.py:328
  60.1 0.0 all-to-all-done
  60.1 0.1 fusion.2
  60.2 0.8 reshape.177
  61.0 4.8 %all-to-all-start.1 = ((bf16[8,36,384]{2,1,0:T(8,128)(2,1)}), bf16[8,36,384]{2,1,0:T(8,128)(2,1)S(1)}, u32[]{:S(2)}, u32[]{:S(2)}) async-start(bf16[8,36,384]{2,1,0:T(8,128)(2,1)} %reshape.177), calls=%async_computation.1 | async-start | bytes 491520 | tf_op jit(solution)/shard_map/all_to_all | solution.py:409
  65.7 0.7 pad_add_fusion.refs_0_
  66.4 0.5 cosine_convert_fusion
  66.9 0.7 pad_maximum_fusion.1
  67.6 0.6 collective-permute-start.7
  68.1 1.7 %collective-permute-start.8 = (bf16[192,1152]{1,0:T(8,128)(2,1)S(1)}, bf16[192,1152]{1,0:T(8,128)(2,1)S(1)}, u32[]{:S(2)}, u32[]{:S(2)}) collective-permute-start(bf16[192,1152]{1,0:T(8,128)(2,1)S(1)} %bitcast.49), channel_id=1, source_target_pairs={{0,16},{8,24},{16,0},{24,8},{1,17},{9,25},{17,1},{25,9},{2,18},{10... | collective-permute-start | bytes 1327112 | tf_op jit(solution)/shard_map/ppermute | solution.py:328
  69.9 1.2 %collective-permute-start.9 = (bf16[192,1152]{1,0:T(8,128)(2,1)S(1)}, bf16[192,1152]{1,0:T(8,128)(2,1)S(1)}, u32[]{:S(2)}, u32[]{:S(2)}) collective-permute-start(bf16[192,1152]{1,0:T(8,128)(2,1)S(1)} %bitcast.50), channel_id=1, source_target_pairs={{0,24},{8,16},{16,8},{24,0},{1,25},{9,17},{17,9},{25,1},{2,26},{10... | collective-permute-start | bytes 1327112 | tf_op jit(solution)/shard_map/ppermute | solution.py:328
  71.0 4.1 %all-to-all-done.1 = bf16[8,36,384]{2,1,0:T(8,128)(2,1)S(1)} async-done(((bf16[8,36,384]{2,1,0:T(8,128)(2,1)}), bf16[8,36,384]{2,1,0:T(8,128)(2,1)S(1)}, u32[]{:S(2)}, u32[]{:S(2)}) %all-to-all-start.1) | async-done | bytes 221216 | tf_op jit(solution)/shard_map/all_to_all | solution.py:409
  75.2 0.7 broadcast_in_dim.29
  75.9 3.6 %all-to-all-start.2 = ((bf16[8,36,384]{2,1,0:T(8,128)(2,1)}), bf16[8,36,384]{2,1,0:T(8,128)(2,1)S(1)}, u32[]{:S(2)}, u32[]{:S(2)}) async-start(bf16[8,36,384]{2,1,0:T(8,128)(2,1)} %broadcast_in_dim.29), calls=%async_computation.2 | async-start | bytes 491520 | tf_op jit(solution)/shard_map/all_to_all | solution.py:413
  79.5 6.3 %legendre_table.5 = (bf16[96,128,128]{2,1,0:T(8,128)(2,1)}, f32[96,128]{1,0:T(8,128)}, f32[96,128]{1,0:T(8,128)}, f32[96,128]{1,0:T(8,128)}) custom-call(s32[1]{0:T(128)} %bitcast.2.first_ref, f32[1,128]{1,0:T(1,128)} %pad_bitcast_fusion.cos_ref, f32[96,128]{1,0:T(8,128)} %get-tuple-element.64.prev_in, f32[96,128]{1,0:T(8,128)} %get-tuple-element.65.early_in, ...), custom_call_target="tpu_custom_call" | custom-call | flops 7864320000 | bytes 3145728 | tf_op jit(solution)/shard_map/legendre_table/pallas_call | solution.py:121
  85.7 0.0 collective-permute-done.7.refs_3_
  85.8 4.2 %collective-permute-done.8.refs_4_ = bf16[192,1152]{1,0:T(8,128)(2,1)S(1)} collective-permute-done((bf16[192,1152]{1,0:T(8,128)(2,1)S(1)}, bf16[192,1152]{1,0:T(8,128)(2,1)S(1)}, u32[]{:S(2)}, u32[]{:S(2)}) %collective-permute-start.8) | collective-permute-done | bytes 442400 | tf_op jit(solution)/shard_map/ppermute | solution.py:328
  89.9 0.0 collective-permute-done.9.refs_5_
  89.9 0.0 all-to-all-done.2
  89.9 1.6 %collective-permute-start.10 = (bf16[8,36,384]{2,1,0:T(8,128)(2,1)S(1)}, bf16[8,36,384]{2,1,0:T(8,128)(2,1)S(1)}, u32[]{:S(2)}, u32[]{:S(2)}) collective-permute-start(bf16[8,36,384]{2,1,0:T(8,128)(2,1)S(1)} %all-to-all-done.2), channel_id=1, source_target_pairs={{0,24},{8,16},{16,8},{24,0},{1,25},{9,17},{17,9},{25,1},{2,26},{10... | collective-permute-start | bytes 663560 | tf_op jit(solution)/shard_map/ppermute | solution.py:328
  91.5 1.3 %collective-permute-start.11 = (bf16[8,36,384]{2,1,0:T(8,128)(2,1)S(1)}, bf16[8,36,384]{2,1,0:T(8,128)(2,1)S(1)}, u32[]{:S(2)}, u32[]{:S(2)}) collective-permute-start(bf16[8,36,384]{2,1,0:T(8,128)(2,1)S(1)} %all-to-all-done.2), channel_id=1, source_target_pairs={{0,16},{8,24},{16,0},{24,8},{1,17},{9,25},{17,1},{25,9},{2,18},{10... | collective-permute-start | bytes 663560 | tf_op jit(solution)/shard_map/ppermute | solution.py:328
  92.8 0.6 collective-permute-start.12
  93.5 17.1 %dft_synthesis.1 = f32[2,96,48,384]{3,2,1,0:T(8,128)} custom-call(s32[4]{0:T(128)} %pad_add_fusion.refs_0_, bf16[192,192]{1,0:T(8,128)(2,1)} %bitcast.52, bf16[192,1152]{1,0:T(8,128)(2,1)} %bitcast.51, bf16[192,1152]{1,0:T(8,128)(2,1)} %copy-done.5, bf16[192,1152]{1,0:T(8,128)(2,1)} %copy-done.6, bf16[192,1152]{1,0:T(8,128)(2,1)} %copy-done.7, ...), custom_call_target="tpu_custom_call" | custom-call | flops 20000000000 | bytes 14155776 | tf_op jit(solution)/shard_map/dft_synthesis/pallas_call | solution.py:190
  110.6 0.0 collective-permute-done.10
  110.6 0.0 collective-permute-done.11
  110.6 0.2 select_bitcast_fusion.3
  110.8 0.2 maximum_convert_fusion
  111.0 1.4 %reshape.181 = f32[3,384,384]{2,1,0:T(8,128)} reshape(f32[4,8,36,384]{3,2,1,0:T(8,128)S(1)} %maximum_convert_fusion) | data formatting | bytes 3538944 | tf_op jit(solution)/shard_map/reshape | solution.py:433
  (28 shorter events, 0.3 us)
Async XLA Ops:
  2.8 15.2 %collective-permute-start = (bf16[24,8,768]{2,1,0:T(8,128)(2,1)S(1)}, bf16[24,8,768]{2,1,0:T(8,128)(2,1)S(1)}, u32[]{:S(2)}, u32[]{:S(2)}) collective-permute-start(bf16[24,8,768]{2,1,0:T(8,128)(2,1)S(1)} %get-tuple-element.89), channel_id=1, source_target_pairs={{0,1},{1,2},{2,3},{3,4},{4,5},{5,6},{6,7},{7,0},{8,9},{9,10},{10,1... | collective-permute-start | bytes 884744 | tf_op jit(solution)/shard_map/ppermute | solution.py:310
  3.3 14.7 %collective-permute-start.1 = (bf16[24,8,768]{2,1,0:T(8,128)(2,1)S(1)}, bf16[24,8,768]{2,1,0:T(8,128)(2,1)S(1)}, u32[]{:S(2)}, u32[]{:S(2)}) collective-permute-start(bf16[24,8,768]{2,1,0:T(8,128)(2,1)S(1)} %get-tuple-element.88), channel_id=1, source_target_pairs={{1,0},{2,1},{3,2},{4,3},{5,4},{6,5},{7,6},{0,7},{9,8},{10,9},{11,1... | collective-permute-start | bytes 884744 | tf_op jit(solution)/shard_map/ppermute | solution.py:311
  10.3 6.3 %copy-start.2 = (f32[96,3,3,8]{0,3,2,1:T(8,128)S(1)}, f32[96,3,3,8]{0,3,2,1:T(8,128)}, u32[]{:S(2)}) copy-start(f32[96,3,3,8]{0,3,2,1:T(8,128)} %param.9) | copy-start | bytes 82948
  10.3 6.3 %copy-start.4 = (s32[96]{0:T(128)S(1)}, s32[96]{0:T(128)}, u32[]{:S(2)}) copy-start(s32[96]{0:T(128)} %param.11) | copy-start | bytes 1156
  10.3 6.4 %copy-start.3 = (s32[96,3,8]{0,2,1:T(8,128)S(1)}, s32[96,3,8]{0,2,1:T(8,128)}, u32[]{:S(2)}) copy-start(s32[96,3,8]{0,2,1:T(8,128)} %param.10) | copy-start | bytes 27652
  18.1 6.2 %collective-permute-start.3 = (bf16[1,48,768]{2,1,0:T(8,128)(2,1)S(1)}, bf16[1,48,768]{2,1,0:T(8,128)(2,1)S(1)}, u32[]{:S(2)}, u32[]{:S(2)}) collective-permute-start(bf16[1,48,768]{2,1,0:T(8,128)(2,1)S(1)} %get-tuple-element.80), channel_id=1, source_target_pairs={{8,0},{16,8},{24,16},{9,1},{17,9},{25,17},{10,2},{18,10},{26,18},{... | collective-permute-start | bytes 221192 | tf_op jit(solution)/shard_map/ppermute | solution.py:311
  19.4 6.5 %collective-permute-start.2 = (bf16[1,48,768]{2,1,0:T(8,128)(2,1)S(1)}, bf16[1,48,768]{2,1,0:T(8,128)(2,1)S(1)}, u32[]{:S(2)}, u32[]{:S(2)}) collective-permute-start(bf16[1,48,768]{2,1,0:T(8,128)(2,1)S(1)} %get-tuple-element.79), channel_id=1, source_target_pairs={{0,8},{8,16},{16,24},{1,9},{9,17},{17,25},{2,10},{10,18},{18,26},{... | collective-permute-start | bytes 221192 | tf_op jit(solution)/shard_map/ppermute | solution.py:310
  27.2 13.8 %copy-start = (bf16[24,24,384]{2,1,0:T(8,128)(2,1)S(1)}, bf16[24,24,384]{2,1,0:T(8,128)(2,1)}, u32[]{:S(2)}) copy-start(bf16[24,24,384]{2,1,0:T(8,128)(2,1)} %param.7) | copy-start | bytes 1327108
  37.5 22.6 %all-to-all-start = ((bf16[8,24,1152]{2,1,0:T(8,128)(2,1)}), bf16[8,24,1152]{2,1,0:T(8,128)(2,1)S(1)}, u32[]{:S(2)}, u32[]{:S(2)}) async-start(bf16[8,24,1152]{2,1,0:T(8,128)(2,1)} %get-tuple-element.53), calls=%async_computation | async-start | bytes 884736 | tf_op jit(solution)/shard_map/all_to_all | solution.py:396
  43.5 12.4 %collective-permute-start.4 = (bf16[288,384]{1,0:T(8,128)(2,1)S(1)}, bf16[288,384]{1,0:T(8,128)(2,1)S(1)}, u32[]{:S(2)}, u32[]{:S(2)}) collective-permute-start(bf16[288,384]{1,0:T(8,128)(2,1)S(1)} %get-tuple-element.87), channel_id=1, source_target_pairs={{0,8},{8,0},{16,24},{24,16},{1,9},{9,1},{17,25},{25,17},{2,10},{10... | collective-permute-start | bytes 663560 | tf_op jit(solution)/shard_map/ppermute | solution.py:328
  46.3 11.9 %collective-permute-start.5 = (bf16[288,384]{1,0:T(8,128)(2,1)S(1)}, bf16[288,384]{1,0:T(8,128)(2,1)S(1)}, u32[]{:S(2)}, u32[]{:S(2)}) collective-permute-start(bf16[288,384]{1,0:T(8,128)(2,1)S(1)} %get-tuple-element.86), channel_id=1, source_target_pairs={{0,16},{8,24},{16,0},{24,8},{1,17},{9,25},{17,1},{25,9},{2,18},{10... | collective-permute-start | bytes 663560 | tf_op jit(solution)/shard_map/ppermute | solution.py:328
  48.3 11.8 %collective-permute-start.6 = (bf16[288,384]{1,0:T(8,128)(2,1)S(1)}, bf16[288,384]{1,0:T(8,128)(2,1)S(1)}, u32[]{:S(2)}, u32[]{:S(2)}) collective-permute-start(bf16[288,384]{1,0:T(8,128)(2,1)S(1)} %get-tuple-element.85), channel_id=1, source_target_pairs={{0,24},{8,16},{16,8},{24,0},{1,25},{9,17},{17,9},{25,1},{2,26},{10... | collective-permute-start | bytes 663560 | tf_op jit(solution)/shard_map/ppermute | solution.py:328
  60.1 25.7 %copy-start.1 = (bf16[8,24,1152]{2,1,0:T(8,128)(2,1)}, bf16[8,24,1152]{2,1,0:T(8,128)(2,1)S(1)}, u32[]{:S(2)}) copy-start(bf16[8,24,1152]{2,1,0:T(8,128)(2,1)S(1)} %all-to-all-done) | copy-start | bytes 1327108
  61.0 14.2 %all-to-all-start.1 = ((bf16[8,36,384]{2,1,0:T(8,128)(2,1)}), bf16[8,36,384]{2,1,0:T(8,128)(2,1)S(1)}, u32[]{:S(2)}, u32[]{:S(2)}) async-start(bf16[8,36,384]{2,1,0:T(8,128)(2,1)} %reshape.177), calls=%async_computation.1 | async-start | bytes 491520 | tf_op jit(solution)/shard_map/all_to_all | solution.py:409
  67.6 18.2 %collective-permute-start.7 = (bf16[192,1152]{1,0:T(8,128)(2,1)S(1)}, bf16[192,1152]{1,0:T(8,128)(2,1)S(1)}, u32[]{:S(2)}, u32[]{:S(2)}) collective-permute-start(bf16[192,1152]{1,0:T(8,128)(2,1)S(1)} %bitcast.48), channel_id=1, source_target_pairs={{0,8},{8,0},{16,24},{24,16},{1,9},{9,1},{17,25},{25,17},{2,10},{10... | collective-permute-start | bytes 1327112 | tf_op jit(solution)/shard_map/ppermute | solution.py:328
  68.1 21.8 %collective-permute-start.8 = (bf16[192,1152]{1,0:T(8,128)(2,1)S(1)}, bf16[192,1152]{1,0:T(8,128)(2,1)S(1)}, u32[]{:S(2)}, u32[]{:S(2)}) collective-permute-start(bf16[192,1152]{1,0:T(8,128)(2,1)S(1)} %bitcast.49), channel_id=1, source_target_pairs={{0,16},{8,24},{16,0},{24,8},{1,17},{9,25},{17,1},{25,9},{2,18},{10... | collective-permute-start | bytes 1327112 | tf_op jit(solution)/shard_map/ppermute | solution.py:328
  69.9 20.0 %collective-permute-start.9 = (bf16[192,1152]{1,0:T(8,128)(2,1)S(1)}, bf16[192,1152]{1,0:T(8,128)(2,1)S(1)}, u32[]{:S(2)}, u32[]{:S(2)}) collective-permute-start(bf16[192,1152]{1,0:T(8,128)(2,1)S(1)} %bitcast.50), channel_id=1, source_target_pairs={{0,24},{8,16},{16,8},{24,0},{1,25},{9,17},{17,9},{25,1},{2,26},{10... | collective-permute-start | bytes 1327112 | tf_op jit(solution)/shard_map/ppermute | solution.py:328
  75.9 14.0 %all-to-all-start.2 = ((bf16[8,36,384]{2,1,0:T(8,128)(2,1)}), bf16[8,36,384]{2,1,0:T(8,128)(2,1)S(1)}, u32[]{:S(2)}, u32[]{:S(2)}) async-start(bf16[8,36,384]{2,1,0:T(8,128)(2,1)} %broadcast_in_dim.29), calls=%async_computation.2 | async-start | bytes 491520 | tf_op jit(solution)/shard_map/all_to_all | solution.py:413
  85.7 7.7 %copy-start.5 = (bf16[192,1152]{1,0:T(8,128)(2,1)}, bf16[192,1152]{1,0:T(8,128)(2,1)S(1)}, u32[]{:S(2)}) copy-start(bf16[192,1152]{1,0:T(8,128)(2,1)S(1)} %collective-permute-done.7.refs_3_) | copy-start | bytes 1327108
  89.9 3.6 %copy-start.6 = (bf16[192,1152]{1,0:T(8,128)(2,1)}, bf16[192,1152]{1,0:T(8,128)(2,1)S(1)}, u32[]{:S(2)}) copy-start(bf16[192,1152]{1,0:T(8,128)(2,1)S(1)} %collective-permute-done.8.refs_4_) | copy-start | bytes 1327108
  89.9 3.6 %copy-start.7 = (bf16[192,1152]{1,0:T(8,128)(2,1)}, bf16[192,1152]{1,0:T(8,128)(2,1)S(1)}, u32[]{:S(2)}) copy-start(bf16[192,1152]{1,0:T(8,128)(2,1)S(1)} %collective-permute-done.9.refs_5_) | copy-start | bytes 1327108
  89.9 20.7 %collective-permute-start.10 = (bf16[8,36,384]{2,1,0:T(8,128)(2,1)S(1)}, bf16[8,36,384]{2,1,0:T(8,128)(2,1)S(1)}, u32[]{:S(2)}, u32[]{:S(2)}) collective-permute-start(bf16[8,36,384]{2,1,0:T(8,128)(2,1)S(1)} %all-to-all-done.2), channel_id=1, source_target_pairs={{0,24},{8,16},{16,8},{24,0},{1,25},{9,17},{17,9},{25,1},{2,26},{10... | collective-permute-start | bytes 663560 | tf_op jit(solution)/shard_map/ppermute | solution.py:328
  91.5 19.1 %collective-permute-start.11 = (bf16[8,36,384]{2,1,0:T(8,128)(2,1)S(1)}, bf16[8,36,384]{2,1,0:T(8,128)(2,1)S(1)}, u32[]{:S(2)}, u32[]{:S(2)}) collective-permute-start(bf16[8,36,384]{2,1,0:T(8,128)(2,1)S(1)} %all-to-all-done.2), channel_id=1, source_target_pairs={{0,16},{8,24},{16,0},{24,8},{1,17},{9,25},{17,1},{25,9},{2,18},{10... | collective-permute-start | bytes 663560 | tf_op jit(solution)/shard_map/ppermute | solution.py:328
  92.8 17.8 %collective-permute-start.12 = (bf16[8,36,384]{2,1,0:T(8,128)(2,1)S(1)}, bf16[8,36,384]{2,1,0:T(8,128)(2,1)S(1)}, u32[]{:S(2)}, u32[]{:S(2)}) collective-permute-start(bf16[8,36,384]{2,1,0:T(8,128)(2,1)S(1)} %all-to-all-done.2), channel_id=1, source_target_pairs={{0,8},{8,0},{16,24},{24,16},{1,9},{9,1},{17,25},{25,17},{2,10},{10... | collective-permute-start | bytes 663560 | tf_op jit(solution)/shard_map/ppermute | solution.py:328
